TPU v7x, 512 devices: a whole 4x8x8 slice. The times are simulated.
512 devices in a mesh: frames: 128 (over x, y, z_lo), tensor: 4 (over z_hi, core).
Axes of the slice: x: 4, y: 8, z: 8 (z_hi: 2, z_lo: 4; z = z_hi * 4 + z_lo), core: 2. Of those that a mesh axis runs over, the one named last changes fastest.
Arguments:
- tokens: bfloat16 [49152, 1280], P('frames', 'tensor'), may hold values from -24 to 24
- reference_image: bfloat16 [384, 1280], P('frames'), may hold values from -6 to 6
- query_weight: bfloat16 [1280, 1280], P(None, 'tensor'), may hold values from -0.15625 to 0.15625
- key_weight: bfloat16 [1280, 1280], P(None, 'tensor'), may hold values from -0.15625 to 0.15625
- value_weight: bfloat16 [1280, 1280], P(None, 'tensor'), may hold values from -0.15625 to 0.15625
- ref_weight: bfloat16 [1280, 1280], P(None, 'tensor'), may hold values from -0.15625 to 0.15625
- cotangent: bfloat16 [49152, 1280], P('frames', 'tensor'), may hold values from -6 to 6
Outputs:
- attended: bfloat16 [49152, 1280], P('frames', 'tensor')
- token_grads: bfloat16 [49152, 1280], P('frames', 'tensor')
- query_weight_grad: float32 [1280, 1280], P('frames', 'tensor')
- ref_key_grads: bfloat16 [384, 1280], P('frames', 'tensor')
- ref_value_grads: bfloat16 [384, 1280], P('frames', 'tensor')
All inputs are finite; a program needn't handle non-finite values.
Results may differ from a plain program's by a relative error of at most 0.019.
Values may be sent and summed in bfloat16 or wider, within the bound.
No kernel may reach another device: no remote copies, remote signals or barrier semaphores. Data moves between devices by JAX's collectives and lax.ppermute only.
A program may use at most 64 MiB of HBM per device.

v0:
```python
import math

import jax
import jax.numpy as jnp
from jax import lax
from jax.sharding import PartitionSpec as P

E = 64
P_SIZE = 384


def per_device(
    tokens, reference_image, query_weight, key_weight, value_weight, ref_weight, cotangent
):
    width_here = tokens.shape[1]
    row_total = tokens.shape[0]
    frames_here = row_total // P_SIZE
    heads_here = width_here // E
    score_scale = 1.0 / math.sqrt(E)
    start_col = lax.axis_index("tensor") * width_here
    ref_source = lax.all_gather(reference_image, "frames", axis=0, tiled=True)
    source_cols = lax.dynamic_slice_in_dim(ref_source, start_col, width_here, 1)
    ref_cols = (
        source_cols.astype(jnp.float32)
        + jnp.dot(ref_source, ref_weight, preferred_element_type=jnp.float32)
    ).astype(jnp.bfloat16)
    whole_tokens, ref_hidden = (
        lax.all_gather(tokens, "tensor", axis=1, tiled=True),
        lax.all_gather(ref_cols, "tensor", axis=1, tiled=True),
    )
    queries = jnp.dot(whole_tokens, query_weight, preferred_element_type=jnp.float32).astype(
        jnp.bfloat16
    )
    own_keys = jnp.dot(whole_tokens, key_weight, preferred_element_type=jnp.float32).astype(
        jnp.bfloat16
    )
    own_values = jnp.dot(whole_tokens, value_weight, preferred_element_type=jnp.float32).astype(
        jnp.bfloat16
    )
    ref_keys = jnp.dot(ref_hidden, key_weight, preferred_element_type=jnp.float32).astype(
        jnp.bfloat16
    )
    ref_values = jnp.dot(ref_hidden, value_weight, preferred_element_type=jnp.float32).astype(
        jnp.bfloat16
    )
    frame_shape = (frames_here, P_SIZE, heads_here, E)
    query_split = queries.reshape(frame_shape)
    key_split = own_keys.reshape(frame_shape)
    value_split = own_values.reshape(frame_shape)
    grad_split = cotangent.reshape(frame_shape)
    ref_key_split = ref_keys.reshape(P_SIZE, heads_here, E)
    ref_value_split = ref_values.reshape(P_SIZE, heads_here, E)
    own_scores = jnp.einsum(
        "fphe,fkhe->fhpk", query_split, key_split, preferred_element_type=jnp.float32
    )
    ref_scores = jnp.einsum(
        "fphe,khe->fhpk", query_split, ref_key_split, preferred_element_type=jnp.float32
    )
    scores = jnp.concatenate([own_scores, ref_scores], -1) * score_scale
    probs = jax.nn.softmax(scores, axis=-1)
    probs_low = probs.astype(jnp.bfloat16)
    attended = jnp.einsum(
        "fhpk,fkhe->fphe", probs_low[..., :P_SIZE], value_split, preferred_element_type=jnp.float32
    )
    attended = attended + jnp.einsum(
        "fhpk,khe->fphe",
        probs_low[..., P_SIZE:],
        ref_value_split,
        preferred_element_type=jnp.float32,
    )
    attended = attended.reshape(row_total, width_here).astype(jnp.bfloat16)
    own_grads = jnp.einsum(
        "fphe,fkhe->fhpk", grad_split, value_split, preferred_element_type=jnp.float32
    )
    ref_grads = jnp.einsum(
        "fphe,khe->fhpk", grad_split, ref_value_split, preferred_element_type=jnp.float32
    )
    prob_grads = jnp.concatenate([own_grads, ref_grads], -1)
    score_grads = (
        probs * (prob_grads - jnp.sum(probs * prob_grads, axis=-1, keepdims=True)) * score_scale
    ).astype(jnp.bfloat16)
    query_grads = jnp.einsum(
        "fhpk,fkhe->fphe", score_grads[..., :P_SIZE], key_split, preferred_element_type=jnp.float32
    )
    query_grads = query_grads + jnp.einsum(
        "fhpk,khe->fphe",
        score_grads[..., P_SIZE:],
        ref_key_split,
        preferred_element_type=jnp.float32,
    )
    query_grads = query_grads.reshape(row_total, width_here).astype(jnp.bfloat16)
    key_grads = (
        jnp.einsum(
            "fhpk,fphe->fkhe",
            score_grads[..., :P_SIZE],
            query_split,
            preferred_element_type=jnp.float32,
        )
        .reshape(row_total, width_here)
        .astype(jnp.bfloat16)
    )
    value_grads = (
        jnp.einsum(
            "fhpk,fphe->fkhe",
            probs_low[..., :P_SIZE],
            grad_split,
            preferred_element_type=jnp.float32,
        )
        .reshape(row_total, width_here)
        .astype(jnp.bfloat16)
    )
    ref_key_part = jnp.einsum(
        "fhpk,fphe->khe", score_grads[..., P_SIZE:], query_split, preferred_element_type=jnp.float32
    ).reshape(P_SIZE, width_here)
    ref_value_part = jnp.einsum(
        "fhpk,fphe->khe", probs_low[..., P_SIZE:], grad_split, preferred_element_type=jnp.float32
    ).reshape(P_SIZE, width_here)
    ref_key_grads, ref_value_grads = (
        lax.psum_scatter(ref_key_part, "frames", scatter_dimension=0, tiled=True),
        lax.psum_scatter(ref_value_part, "frames", scatter_dimension=0, tiled=True),
    )
    back_dims = (((1,), (1,)), ((), ()))
    token_part = lax.dot_general(
        query_grads, query_weight, back_dims, preferred_element_type=jnp.float32
    )
    token_part = token_part + lax.dot_general(
        key_grads, key_weight, back_dims, preferred_element_type=jnp.float32
    )
    token_part = token_part + lax.dot_general(
        value_grads, value_weight, back_dims, preferred_element_type=jnp.float32
    )
    token_grads = lax.psum_scatter(
        token_part.astype(jnp.bfloat16), "tensor", scatter_dimension=1, tiled=True
    )
    query_weight_grad = lax.psum_scatter(
        lax.dot_general(
            whole_tokens, query_grads, (((0,), (0,)), ((), ())), preferred_element_type=jnp.float32
        ),
        "frames",
        scatter_dimension=0,
        tiled=True,
    )
    return (
        attended,
        token_grads,
        query_weight_grad,
        ref_key_grads.astype(jnp.bfloat16),
        ref_value_grads.astype(jnp.bfloat16),
    )


def solution(mesh):
    return jax.shard_map(
        per_device,
        mesh=mesh,
        in_specs=(
            P("frames", "tensor"),
            P("frames", None),
            P(None, "tensor"),
            P(None, "tensor"),
            P(None, "tensor"),
            P(None, "tensor"),
            P("frames", "tensor"),
        ),
        out_specs=(
            P("frames", "tensor"),
            P("frames", "tensor"),
            P("frames", "tensor"),
            P("frames", "tensor"),
            P("frames", "tensor"),
        ),
        check_vma=False,
    )
```

profile of v0, /device:TPU:64, one launch (start us, length us, event | category | flops | bytes accessed | tf_op | source)
XLA Modules:
  0.0 1807.3 jit_solution(11813602825239939821)
XLA Ops:
  8.0 0.0 copy-start
  8.0 0.0 all-reduce.7.cloned.1.call-start
  8.1 369.7 %all-gather = bf16[128,3,1280]{2,1,0:T(4,128)(2,1)S(1)} all-gather(bf16[1,3,1280]{2,1,0:T(4,128)(2,1)} %bitcast.165), channel_id=1, replica_groups=mesh['frames'=128,'tensor'=4] {'frames'}, dimensions={0}, use_global_device_ids=true | all-gather | bytes 990720 | tf_op jit(solution)/shard_map/all_gather | solution.py:21
  377.7 0.8 reshape.294
  378.6 0.0 copy-start.6
  378.6 0.2 constant_dynamic-slice_fusion.1
  378.8 0.2 copy.58
  379.0 1.8 fusion.20
  380.7 12.9 all_gather.11
  393.6 0.0 copy-done.6
  393.6 0.0 copy-start.4
  393.6 13.8 all_gather.9
  407.4 0.0 copy-done
  407.5 0.6 convolution_convert_fusion.1
  408.0 0.0 copy-start.3
  408.1 0.6 convolution_convert_fusion.2
  408.7 0.0 copy-done.4
  408.7 0.6 convolution_convert_fusion
  409.3 0.6 convolution_convert_fusion.4
  409.9 0.0 copy-done.3
  409.9 0.6 convolution_convert_fusion.3
  410.5 0.6 convolution_bitcast_fusion.3
  411.1 0.6 convolution_bitcast_fusion.4
  411.7 0.4 fusion.2
  412.1 0.0 copy-start.2
  412.1 1.0 fusion.1
  413.1 0.0 copy-done.2
  413.1 0.6 convolution_bitcast_fusion.1
  413.7 0.6 convolution_bitcast_fusion.2
  414.3 1.5 multiply_reduce_fusion
  415.8 3.4 multiply_convert_fusion
  419.3 0.0 copy-start.1
  419.3 0.4 fusion.12
  419.7 1.2 copy-done.1
  420.9 0.4 fusion.18
  421.3 1.9 convolution_bitcast_fusion
  423.2 0.0 all-reduce.7.cloned.1.call-update
  423.2 0.2 reduce-scatter.3.cloned.1.call-start
  423.4 2.0 fusion.21
  425.5 2.0 fusion.22
  427.5 0.8 fusion.24
  428.3 0.0 copy-start.5
  428.3 0.8 convolution_add_fusion.1
  429.1 0.3 copy-done.5
  429.4 1.8 fusion.3
  431.2 0.0 reduce-scatter.3.cloned.1.call-update
  431.3 2.0 fusion.10
  433.3 0.2 copy.44
  433.5 2.0 fusion.6
  435.5 0.2 copy.46
  435.8 1.3 dynamic-slice
  438.3 736.2 %all-reduce.8 = (bf16[384,320]{1,0:T(8,128)(2,1)S(1)}, bf16[384,320]{1,0:T(8,128)(2,1)S(1)}) all-reduce(f32[384,320]{1,0:T(8,128)S(1)} %copy.44, f32[384,320]{1,0:T(8,128)S(1)} %copy.46), channel_id=4, replica_groups=mesh['frames'=128,'tensor'=4] {'frames'}, use_global_device_ids=true, to_apply=%region_5.0.clone | all-reduce | flops 245760 | bytes 1474560
  1174.6 0.6 dynamic-slice_convert_fusion
  1175.2 1.8 fusion.14
  1176.9 2.4 fusion.19
  1179.4 618.7 %all-reduce.7.cloned.1.call-done = f32[1280,320]{0,1:T(8,128)} async-done(((f32[1280,320]{0,1:T(8,128)}), f32[1280,320]{0,1:T(8,128)}) %all-reduce.7.cloned.1.call-update) | async-done | bytes 1638416
  1798.0 1.1 constant_dynamic-slice_fusion
  1799.1 0.7 copy.47
  1799.8 0.0 reduce-scatter.3.cloned.1.call-done
Async XLA Ops:
  8.0 399.5 %copy-start = (bf16[1280,320]{0,1:T(8,128)(2,1)S(1)}, bf16[1280,320]{0,1:T(8,128)(2,1)}, u32[]{:S(2)}) copy-start(bf16[1280,320]{0,1:T(8,128)(2,1)} %param.10) | copy-start | bytes 2457604
  8.0 1790.0 %all-reduce.7.cloned.1.call-start = ((), (), s32[]{:S(2)}) async-start(), calls=%async_computation.2 | async-start | bytes 3276800
  378.6 15.0 copy-start.6
  393.6 15.0 copy-start.4
  408.0 1.8 copy-start.3
  412.1 1.0 copy-start.2
  419.3 1.6 copy-start.1
  423.2 1376.6 %reduce-scatter.3.cloned.1.call-start = ((), (), s32[]{:S(2)}) async-start(), calls=%async_computation.1 | async-start | bytes 1228800 | tf_op jit(solution)/shard_map/reduce_scatter | solution.py:132
  428.3 1.1 copy-start.5
Sparse Core Ops, SparseCore 0:
  423.3 1374.6 all-reduce.6
Sparse Core Ops, SparseCore 1:
  431.3 48.8 reduce-scatter.2
where the time goes:
time: 1810 us
  blocking collectives  1130 us (62%)
  waiting for transfers between devices  619 us (34%)
  matrix products  25.5 us (1%)
    unnamed x1, blocking collectives  736 us
    unnamed x3, waiting for transfers between devices  619 us
    all_gather x1, blocking collectives, per_device(): ref_source = lax.all_gather(reference_image, 'frames', axis=0, tiled=True)  370 us
  transfers between devices with their start and end apart: 2, of which 1 were waited for; matrix products, arithmetic and copies ran while one was open for 1% of the time, Pallas kernels for 0%

commit v1 on v0

--- a/solution.py
+++ b/solution.py
@@ -3,10 +3,13 @@
 import jax
 import jax.numpy as jnp
 from jax import lax
+from jax.sharding import Mesh
 from jax.sharding import PartitionSpec as P
 
 E = 64
 P_SIZE = 384
+FRAMES = ("x", "y", "z")
+TENSOR = ("h", "c")
 
 
 def per_device(
@@ -17,17 +20,26 @@
     frames_here = row_total // P_SIZE
     heads_here = width_here // E
     score_scale = 1.0 / math.sqrt(E)
-    start_col = lax.axis_index("tensor") * width_here
-    ref_source = lax.all_gather(reference_image, "frames", axis=0, tiled=True)
-    source_cols = lax.dynamic_slice_in_dim(ref_source, start_col, width_here, 1)
+    start_col = lax.axis_index(TENSOR) * width_here
+    source_cols = lax.dynamic_slice_in_dim(reference_image, start_col, width_here, 1)
     ref_cols = (
         source_cols.astype(jnp.float32)
-        + jnp.dot(ref_source, ref_weight, preferred_element_type=jnp.float32)
+        + jnp.dot(reference_image, ref_weight, preferred_element_type=jnp.float32)
     ).astype(jnp.bfloat16)
-    whole_tokens, ref_hidden = (
-        lax.all_gather(tokens, "tensor", axis=1, tiled=True),
-        lax.all_gather(ref_cols, "tensor", axis=1, tiled=True),
-    )
+    rows_here = reference_image.shape[0]
+    ref_hidden = lax.all_gather(ref_cols, TENSOR, axis=1, tiled=True)
+    ref_pair = jnp.concatenate(
+        [
+            jnp.dot(ref_hidden, key_weight, preferred_element_type=jnp.float32),
+            jnp.dot(ref_hidden, value_weight, preferred_element_type=jnp.float32),
+        ],
+        axis=1,
+    ).astype(jnp.bfloat16)
+    n_frames = P_SIZE // rows_here
+    ref_pair = jnp.broadcast_to(ref_pair.reshape(1, -1, 128), (n_frames, rows_here * 5, 128))
+    ref_all = lax.all_to_all(ref_pair, FRAMES, 0, 0, tiled=True).reshape(P_SIZE, 2 * width_here)
+    ref_keys, ref_values = ref_all[:, :width_here], ref_all[:, width_here:]
+    whole_tokens = lax.all_gather(tokens, TENSOR, axis=1, tiled=True)
     queries = jnp.dot(whole_tokens, query_weight, preferred_element_type=jnp.float32).astype(
         jnp.bfloat16
     )
@@ -35,12 +47,6 @@
         jnp.bfloat16
     )
     own_values = jnp.dot(whole_tokens, value_weight, preferred_element_type=jnp.float32).astype(
-        jnp.bfloat16
-    )
-    ref_keys = jnp.dot(ref_hidden, key_weight, preferred_element_type=jnp.float32).astype(
-        jnp.bfloat16
-    )
-    ref_values = jnp.dot(ref_hidden, value_weight, preferred_element_type=jnp.float32).astype(
         jnp.bfloat16
     )
     frame_shape = (frames_here, P_SIZE, heads_here, E)
@@ -115,10 +121,6 @@
     ref_value_part = jnp.einsum(
         "fhpk,fphe->khe", probs_low[..., P_SIZE:], grad_split, preferred_element_type=jnp.float32
     ).reshape(P_SIZE, width_here)
-    ref_key_grads, ref_value_grads = (
-        lax.psum_scatter(ref_key_part, "frames", scatter_dimension=0, tiled=True),
-        lax.psum_scatter(ref_value_part, "frames", scatter_dimension=0, tiled=True),
-    )
     back_dims = (((1,), (1,)), ((), ()))
     token_part = lax.dot_general(
         query_grads, query_weight, back_dims, preferred_element_type=jnp.float32
@@ -129,45 +131,54 @@
     token_part = token_part + lax.dot_general(
         value_grads, value_weight, back_dims, preferred_element_type=jnp.float32
     )
-    token_grads = lax.psum_scatter(
-        token_part.astype(jnp.bfloat16), "tensor", scatter_dimension=1, tiled=True
+    weight_part = lax.dot_general(
+        whole_tokens, query_grads, (((0,), (0,)), ((), ())), preferred_element_type=jnp.float32
     )
-    query_weight_grad = lax.psum_scatter(
-        lax.dot_general(
-            whole_tokens, query_grads, (((0,), (0,)), ((), ())), preferred_element_type=jnp.float32
-        ),
-        "frames",
-        scatter_dimension=0,
-        tiled=True,
-    )
+    sums = jnp.concatenate(
+        [
+            ref_key_part.reshape(n_frames, -1),
+            ref_value_part.reshape(n_frames, -1),
+            weight_part.reshape(n_frames, -1),
+        ],
+        axis=1,
+    ).astype(jnp.bfloat16)
+    sums = lax.all_to_all(sums.reshape(n_frames, -1, 128), FRAMES, 0, 0, tiled=True)
+    sums = jnp.sum(sums.astype(jnp.float32), axis=0).reshape(-1)
+    ref_size = rows_here * width_here
+    token_blocks = token_part.astype(jnp.bfloat16).reshape(row_total, 2, 2, width_here)
+    core = lax.axis_index("c")
+    kept = lax.dynamic_index_in_dim(token_blocks, core, 2, False)
+    sent = lax.dynamic_index_in_dim(token_blocks, 1 - core, 2, False)
+    got = lax.ppermute(sent, "c", [(0, 1), (1, 0)])
+    paired = (kept.astype(jnp.float32) + got.astype(jnp.float32)).astype(jnp.bfloat16)
+    half = lax.axis_index("h")
+    kept = lax.dynamic_index_in_dim(paired, half, 1, False)
+    sent = lax.dynamic_index_in_dim(paired, 1 - half, 1, False)
+    got = lax.ppermute(sent, "h", [(0, 1), (1, 0)])
+    token_grads = (kept.astype(jnp.float32) + got.astype(jnp.float32)).astype(jnp.bfloat16)
     return (
         attended,
         token_grads,
-        query_weight_grad,
-        ref_key_grads.astype(jnp.bfloat16),
-        ref_value_grads.astype(jnp.bfloat16),
+        sums[2 * ref_size :].reshape(-1, width_here),
+        sums[:ref_size].reshape(rows_here, width_here).astype(jnp.bfloat16),
+        sums[ref_size : 2 * ref_size].reshape(rows_here, width_here).astype(jnp.bfloat16),
     )
 
 
 def solution(mesh):
+    mesh = Mesh(mesh.devices.reshape(4, 8, 4, 2, 2), ("x", "y", "z", "h", "c"))
     return jax.shard_map(
         per_device,
         mesh=mesh,
         in_specs=(
-            P("frames", "tensor"),
-            P("frames", None),
-            P(None, "tensor"),
-            P(None, "tensor"),
-            P(None, "tensor"),
-            P(None, "tensor"),
-            P("frames", "tensor"),
+            P(FRAMES, TENSOR),
+            P(FRAMES, None),
+            P(None, TENSOR),
+            P(None, TENSOR),
+            P(None, TENSOR),
+            P(None, TENSOR),
+            P(FRAMES, TENSOR),
         ),
-        out_specs=(
-            P("frames", "tensor"),
-            P("frames", "tensor"),
-            P("frames", "tensor"),
-            P("frames", "tensor"),
-            P("frames", "tensor"),
-        ),
+        out_specs=(P(FRAMES, TENSOR),) * 5,
         check_vma=False,
     )

time: 1810 us -> 159 us (0.09)
  the two profiles are of different devices: /device:TPU:64 before, /device:TPU:1 now
where the time goes in v1:
time: 159 us; the launch traced here: 156 us
  blocking collectives  44.6 us (28%)
  starting transfers between devices  29.1 us (18%)
  matrix products  26.8 us (17%)
  waiting for transfers between devices  22.1 us (14%)
  local copies, waits for them, and re-layouts  20.5 us (13%)
  other arithmetic  12.1 us (8%)
    all_gather x1, blocking collectives, per_device(): whole_tokens = lax.all_gather(tokens, TENSOR, axis=1, tiled=True)  28.9 us
    ppermute x1, waiting for transfers between devices, per_device(): got = lax.ppermute(sent, 'h', [(0, 1), (1, 0)])  22.1 us
    all_gather x1, blocking collectives, per_device(): ref_hidden = lax.all_gather(ref_cols, TENSOR, axis=1, tiled=True)  15.8 us
    all_to_all x1, starting transfers between devices, per_device(): lax.all_to_all(sums.reshape(n_frames, -1, 128), FRAMES, 0, 0, tiled=True)  12.8 us
    all_to_all x1, starting transfers between devices, per_device(): lax.all_to_all(ref_pair, FRAMES, 0, 0, tiled=True)  12 us
    unnamed x46, local copies, waits for them, and re-layouts  5.69 us
    reduce_sum x1, other arithmetic, per_device(): jnp.sum(probs * prob_grads, axis=-1, keepdims=True)  5.06 us
    convert_element_type x1, other arithmetic, per_device(): score_grads = (probs * (prob_grads - jnp.sum(probs * prob_grads, axis=-1,...  3.37 us
  transfers between devices with their start and end apart: 4, of which 1 were waited for; matrix products, arithmetic and copies ran while one was open for 13% of the time, Pallas kernels for 0%

profile of v1, /device:TPU:1, one launch (start us, length us, event | category | flops | bytes accessed | tf_op | source)
XLA Modules:
  0.0 156.3 jit_solution(13331647186872431739)
XLA Ops:
  0.6 0.0 copy-start
  0.7 1.6 fusion.28
  2.2 15.8 %all-gather = bf16[4,320,3]{1,2,0:T(4,128)(2,1)S(1)} all-gather(bf16[1,320,3]{1,2,0:T(4,128)(2,1)S(1)} %fusion.28), channel_id=1, replica_groups=mesh['x'=4,'y'=8,'z'=4,'h'=2,'c'=2] {'h','c'}, dimensions={0}, use_global_device_ids=true | all-gather | bytes 9600 | tf_op jit(solution)/shard_map/all_gather | solution.py:30
  18.0 0.1 reshape.329
  18.1 1.4 convolution_convert_fusion.4
  19.5 0.3 convolution_convert_fusion.5
  19.8 0.1 pad_maximum_fusion.1
  20.0 0.9 broadcast_in_dim.2
  20.9 12.0 %all-to-all-start = ((bf16[128,15,128]{2,1,0:T(8,128)(2,1)}), bf16[128,15,128]{2,1,0:T(8,128)(2,1)S(1)}, u32[]{:S(2)}, u32[]{:S(2)}) async-start(bf16[128,15,128]{2,1,0:T(8,128)(2,1)} %broadcast_in_dim.2), calls=%async_computation | async-start | bytes 1048576 | tf_op jit(solution)/shard_map/all_to_all | solution.py:40
  32.9 28.9 %all_gather.6 = bf16[384,1280]{0,1:T(8,128)(2,1)S(1)} all-gather(bf16[384,320]{0,1:T(8,128)(2,1)S(1)} %copy-done.21), channel_id=1, replica_groups=mesh['x'=4,'y'=8,'z'=4,'h'=2,'c'=2] {'h','c'}, dimensions={1}, use_global_device_ids=true | all-gather | bytes 1228800 | tf_op jit(solution)/shard_map/all_gather | solution.py:42
  61.8 0.6 convolution_convert_fusion.1
  62.4 0.0 copy-start.7
  62.4 1.8 %convolution_convert_fusion.2 = bf16[384,320]{0,1:T(8,128)(2,1)S(1)} fusion(bf16[1280,320]{0,1:T(8,128)(2,1)} %param.9, bf16[384,1280]{0,1:T(8,128)(2,1)S(1)} %all_gather.6), kind=kOutput, calls=%fused_computation.43 | convolution fusion | flops 314695680 | bytes 2048000 | tf_op jit(solution)/shard_map/dot_general | solution.py:43
  64.3 2.2 %convolution_bitcast_fusion.3 = f32[1,5,384,384]{2,3,1,0:T(8,128)} fusion(bf16[384,5,64]{0,2,1:T(8,128)(2,1)S(1)} %bitcast.166, bf16[384,5,64]{0,2,1:T(8,128)(2,1)S(1)} %bitcast.179), kind=kOutput, calls=%fused_computation.17 | convolution fusion | flops 94371840 | bytes 3440640 | tf_op jit(solution)/shard_map/fphe,fkhe->fhpk/dot_general | solution.py:59
  66.5 0.6 convolution_convert_fusion.3
  67.1 2.2 %convolution_bitcast_fusion.1 = f32[1,5,384,384]{2,3,1,0:T(8,128)} fusion(bf16[384,5,64]{0,2,1:T(8,128)(2,1)S(1)} %bitcast.177, bf16[384,5,64]{0,2,1:T(8,128)(2,1)S(1)} %bitcast.181), kind=kOutput, calls=%fused_computation.15 | convolution fusion | flops 94371840 | bytes 3440640 | tf_op jit(solution)/shard_map/fphe,fkhe->fhpk/dot_general | solution.py:78
  69.3 0.4 reshape.314
  69.7 0.1 fusion.32
  69.9 0.2 copy.38
  70.1 0.6 convolution_bitcast_fusion.2
  70.7 1.2 copy-done.1
  71.9 0.4 fusion.2
  72.3 1.3 copy-done.3
  73.6 1.0 fusion.1
  74.6 0.2 copy.40
  74.8 0.6 convolution_bitcast_fusion
  75.4 1.2 copy-done.2
  76.6 5.1 %multiply_reduce_fusion = f32[5,384]{1,0:T(8,128)S(1)} fusion(f32[1,5,384,384]{2,3,1,0:T(8,128)S(1)} %convolution_bitcast_fusion, f32[1,5,384,384]{2,3,1,0:T(8,128)} %convolution_bitcast_fusion.1, f32[5,384]{1,0:T(8,128)S(1)} %fusion.1, f32[5,384]{1,0:T(8,128)S(1)} %fusion.2, f32[1,5,384,384]{2,3,1,0:T(8,128)} %copy-done.3, f32[1,5,384,384]{2,3,1,0:T(8,128)S(1)} %copy-done.2), kind=kLoop, calls=%fused_computation.3 | loop fusion | flops 10320000 | bytes 11819520 | tf_op jit(solution)/shard_map/reduce_sum | solution.py:86
  81.7 3.4 %multiply_convert_fusion = (bf16[1,5,384,768]{2,3,1,0:T(8,128)(2,1)S(1)}, bf16[1,5,384,768]{2,3,1,0:T(8,128)(2,1)}) fusion(f32[1,5,384,384]{2,3,1,0:T(8,128)S(1)} %convolution_bitcast_fusion, f32[1,5,384,384]{2,3,1,0:T(8,128)S(1)} %copy-done.5, f32[5,384]{1,0:T(8,128)S(1)} %multiply_reduce_fusion, f32[5,384]{1,0:T(8,128)S(1)} %fusion.1, ...), kind=kLoop, calls=%fused_computation.2 | loop fusion | flops 14745600 | bytes 17717760 | tf_op jit(solution)/shard_map/convert_element_type | solution.py:87
  85.1 0.4 fusion.13
  85.4 1.3 fusion.26
  86.8 1.3 fusion.22
  88.1 0.4 fusion.19
  88.5 0.6 fusion.4
  89.1 0.1 copy-done.9
  89.2 0.6 copy.51
  89.8 1.1 reshape.323
  91.0 1.4 copy.48
  92.4 1.2 reshape_reshape.8
  93.6 2.7 %fusion.25 = bf16[384,5,64]{0,2,1:T(8,128)(2,1)} fusion(bf16[384,5,64]{0,2,1:T(8,128)(2,1)S(1)} %bitcast.183, bf16[1,5,384,768]{2,3,1,0:T(8,128)(2,1)} %get-tuple-element.6), kind=kOutput, calls=%fused_computation.45 | convolution fusion | flops 94494720 | bytes 1966080 | tf_op jit(solution)/shard_map/fhpk,fphe->khe/dot_general | solution.py:121
  96.3 1.4 copy.50
  97.7 1.1 reshape_reshape.9
  98.9 2.2 %concatenate.63 = bf16[128,5120]{1,0:T(8,128)(2,1)S(1)} concatenate(bf16[128,960]{1,0:T(8,128)(2,1)} %reshape_reshape.8, bf16[128,960]{1,0:T(8,128)(2,1)} %reshape_reshape.9, bf16[128,3200]{1,0:T(8,128)(2,1)S(1)} %reshape.323), dimensions={1} | concatenate | bytes 2621440 | tf_op jit(solution)/shard_map/concatenate | solution.py:137
  101.1 1.3 copy.60
  102.4 12.8 %all-to-all-start.1 = ((bf16[128,40,128]{2,1,0:T(8,128)(2,1)}), bf16[128,40,128]{2,1,0:T(8,128)(2,1)S(1)}, u32[]{:S(2)}, u32[]{:S(2)}) async-start(bf16[128,40,128]{2,1,0:T(8,128)(2,1)} %bitcast.61), calls=%async_computation.1 | async-start | bytes 2621440 | tf_op jit(solution)/shard_map/all_to_all | solution.py:145
  115.2 2.1 %fusion.24 = bf16[5,384,64]{1,2,0:T(8,128)(2,1)S(1)} fusion(bf16[384,5,64]{0,2,1:T(8,128)(2,1)S(1)} %bitcast.184, bf16[1,5,384,768]{2,3,1,0:T(8,128)(2,1)} %get-tuple-element.6), kind=kOutput, calls=%fused_computation.41 | convolution fusion | flops 94494720 | bytes 1966080 | tf_op jit(solution)/shard_map/fhpk,fphe->fkhe/dot_general | solution.py:109
  117.3 0.0 copy-done.20
  117.3 0.7 fusion.34
  118.1 0.7 convolution_add_fusion.1
  118.8 0.4 copy-done.8
  119.2 1.6 %fusion.3 = bf16[384,1280]{1,0:T(8,128)(2,1)} fusion(f32[384,1280]{1,0:T(8,128)S(1)} %convolution_add_fusion.1, bf16[384,320]{0,1:T(8,128)(2,1)S(1)} %bitcast.186, bf16[1280,320]{0,1:T(8,128)(2,1)S(1)} %copy-done.8), kind=kOutput, calls=%fused_computation.10 | convolution fusion | flops 315555840 | bytes 4014080 | tf_op jit(solution)/shard_map/dot_general | solution.py:131
  120.8 1.6 %copy.46 = bf16[384,1280]{0,1:T(8,128)(2,1)S(1)} copy(bf16[384,1280]{1,0:T(8,128)(2,1)} %fusion.3) | data formatting | bytes 1966080 | tf_op jit(solution)/shard_map/convert_element_type | solution.py:148
  122.4 0.8 dynamic-slice_bitcast_fusion
  123.3 2.3 %collective-permute-start = (bf16[384,2,320]{0,2,1:T(8,128)(2,1)}, bf16[384,2,320]{0,2,1:T(8,128)(2,1)}, u32[]{:S(2)}, u32[]{:S(2)}) collective-permute-start(bf16[384,2,320]{0,2,1:T(8,128)(2,1)} %dynamic-slice_bitcast_fusion), channel_id=1, source_target_pairs={{0,1},{1,0},{2,3},{3,2},{4,5},{5,4},{6,7},{7,6},{8,9},{9,8},{10,11... | collective-permute-start | bytes 1474568 | tf_op jit(solution)/shard_map/ppermute | solution.py:152
  125.6 1.9 %fusion.15 = f32[1,384,5,64]{1,3,2,0:T(8,128)S(1)} fusion(bf16[384,5,64]{0,2,1:T(8,128)(2,1)S(1)} %bitcast.171, bf16[1,5,384,768]{2,3,1,0:T(8,128)(2,1)} %get-tuple-element.6), kind=kOutput, calls=%fused_computation.32 | convolution fusion | flops 94371840 | bytes 2211840 | tf_op jit(solution)/shard_map/fhpk,khe->fphe/dot_general | solution.py:71
  127.5 1.2 fusion.29
  128.7 1.9 %collective-permute-start.1 = (bf16[384,320]{0,1:T(8,128)(2,1)S(1)}, bf16[384,320]{0,1:T(8,128)(2,1)S(1)}, u32[]{:S(2)}, u32[]{:S(2)}) collective-permute-start(bf16[384,320]{0,1:T(8,128)(2,1)S(1)} %dynamic-slice_bitcast_fusion.1), channel_id=1, source_target_pairs={{0,2},{2,0},{1,3},{3,1},{4,6},{6,4},{5,7},{7,5},{8,10},{10,8},{9,1... | collective-permute-start | bytes 737288 | tf_op jit(solution)/shard_map/ppermute | solution.py:157
  130.7 1.1 fusion.20
  131.8 22.1 %collective-permute-done.1 = bf16[384,320]{0,1:T(8,128)(2,1)S(1)} collective-permute-done((bf16[384,320]{0,1:T(8,128)(2,1)S(1)}, bf16[384,320]{0,1:T(8,128)(2,1)S(1)}, u32[]{:S(2)}, u32[]{:S(2)}) %collective-permute-start.1) | collective-permute-done | bytes 245792 | tf_op jit(solution)/shard_map/ppermute | solution.py:157
  153.9 0.8 fusion.30
  154.6 0.2 convert_reduce_fusion
  154.9 0.7 reshape.324
  155.6 0.1 reshape.327
  155.7 0.6 fusion.33
  (44 shorter events, 0.2 us)
Async XLA Ops:
  0.6 18.9 %copy-start = (bf16[1280,320]{0,1:T(8,128)(2,1)S(1)}, bf16[1280,320]{0,1:T(8,128)(2,1)}, u32[]{:S(2)}) copy-start(bf16[1280,320]{0,1:T(8,128)(2,1)} %param.10) | copy-start | bytes 2457604
  0.6 32.3 %copy-start.21 = (bf16[384,320]{0,1:T(8,128)(2,1)S(1)}, bf16[384,320]{0,1:T(8,128)(2,1)}, u32[]{:S(2)}) copy-start(bf16[384,320]{0,1:T(8,128)(2,1)} %param.7) | copy-start | bytes 737284
  20.9 48.4 %all-to-all-start = ((bf16[128,15,128]{2,1,0:T(8,128)(2,1)}), bf16[128,15,128]{2,1,0:T(8,128)(2,1)S(1)}, u32[]{:S(2)}, u32[]{:S(2)}) async-start(bf16[128,15,128]{2,1,0:T(8,128)(2,1)} %broadcast_in_dim.2), calls=%async_computation | async-start | bytes 1048576 | tf_op jit(solution)/shard_map/all_to_all | solution.py:40
  62.4 1.9 %copy-start.14 = (bf16[384,320]{0,1:T(8,128)(2,1)}, bf16[384,320]{0,1:T(8,128)(2,1)S(1)}, u32[]{:S(2)}) copy-start(bf16[384,320]{0,1:T(8,128)(2,1)S(1)} %convolution_convert_fusion.1) | copy-start | bytes 737284
  62.4 4.1 %copy-start.7 = (bf16[1280,320]{0,1:T(8,128)(2,1)S(1)}, bf16[1280,320]{0,1:T(8,128)(2,1)}, u32[]{:S(2)}) copy-start(bf16[1280,320]{0,1:T(8,128)(2,1)} %param.11) | copy-start | bytes 2457604
  64.3 2.8 %copy-start.16 = (bf16[384,320]{0,1:T(8,128)(2,1)S(1)}, bf16[384,320]{0,1:T(8,128)(2,1)}, u32[]{:S(2)}) copy-start(bf16[384,320]{0,1:T(8,128)(2,1)} %param.13) | copy-start | bytes 737284
  67.1 2.2 %copy-start.12 = (bf16[384,320]{0,1:T(8,128)(2,1)}, bf16[384,320]{0,1:T(8,128)(2,1)S(1)}, u32[]{:S(2)}) copy-start(bf16[384,320]{0,1:T(8,128)(2,1)S(1)} %convolution_convert_fusion.3) | copy-start | bytes 737284
  70.1 1.8 %copy-start.1 = (f32[1,5,384,384]{2,3,1,0:T(8,128)S(1)}, f32[1,5,384,384]{2,3,1,0:T(8,128)}, u32[]{:S(2)}) copy-start(f32[1,5,384,384]{2,3,1,0:T(8,128)} %convolution_bitcast_fusion.3) | copy-start | bytes 8847364
  71.9 1.7 %copy-start.3 = (f32[1,5,384,384]{2,3,1,0:T(8,128)}, f32[1,5,384,384]{2,3,1,0:T(8,128)S(1)}, u32[]{:S(2)}) copy-start(f32[1,5,384,384]{2,3,1,0:T(8,128)S(1)} %convolution_bitcast_fusion.2) | copy-start | bytes 8847364
  73.6 1.2 copy-start.17
  74.8 1.8 %copy-start.2 = (f32[1,5,384,384]{2,3,1,0:T(8,128)S(1)}, f32[1,5,384,384]{2,3,1,0:T(8,128)}, u32[]{:S(2)}) copy-start(f32[1,5,384,384]{2,3,1,0:T(8,128)} %convolution_bitcast_fusion.3) | copy-start | bytes 8847364
  76.6 5.1 %copy-start.4 = (f32[1,5,384,384]{2,3,1,0:T(8,128)S(1)}, f32[1,5,384,384]{2,3,1,0:T(8,128)}, u32[]{:S(2)}) copy-start(f32[1,5,384,384]{2,3,1,0:T(8,128)} %copy-done.3) | copy-start | bytes 8847364
  76.6 5.1 %copy-start.5 = (f32[1,5,384,384]{2,3,1,0:T(8,128)S(1)}, f32[1,5,384,384]{2,3,1,0:T(8,128)}, u32[]{:S(2)}) copy-start(f32[1,5,384,384]{2,3,1,0:T(8,128)} %convolution_bitcast_fusion.1) | copy-start | bytes 8847364
  85.1 3.1 %copy-start.15 = (bf16[384,320]{0,1:T(8,128)(2,1)S(1)}, bf16[384,320]{0,1:T(8,128)(2,1)}, u32[]{:S(2)}) copy-start(bf16[384,320]{0,1:T(8,128)(2,1)} %copy-done.14) | copy-start | bytes 737284
  88.5 0.7 copy-start.9
  89.8 3.8 %copy-start.18 = (bf16[384,320]{0,1:T(8,128)(2,1)S(1)}, bf16[384,320]{0,1:T(8,128)(2,1)}, u32[]{:S(2)}) copy-start(bf16[384,320]{0,1:T(8,128)(2,1)} %param.13) | copy-start | bytes 737284
  101.1 14.1 %copy-start.19 = (bf16[384,320]{0,1:T(8,128)(2,1)S(1)}, bf16[384,320]{0,1:T(8,128)(2,1)}, u32[]{:S(2)}) copy-start(bf16[384,320]{0,1:T(8,128)(2,1)} %param.13) | copy-start | bytes 737284
  102.4 14.9 %copy-start.10 = (bf16[1,384,5,64]{1,3,2,0:T(8,128)(2,1)S(1)}, bf16[1,384,5,64]{1,3,2,0:T(8,128)(2,1)}, u32[]{:S(2)}) copy-start(bf16[1,384,5,64]{1,3,2,0:T(8,128)(2,1)} %copy-done.9) | copy-start | bytes 737284
  102.4 52.2 %all-to-all-start.1 = ((bf16[128,40,128]{2,1,0:T(8,128)(2,1)}), bf16[128,40,128]{2,1,0:T(8,128)(2,1)S(1)}, u32[]{:S(2)}, u32[]{:S(2)}) async-start(bf16[128,40,128]{2,1,0:T(8,128)(2,1)} %bitcast.61), calls=%async_computation.1 | async-start | bytes 2621440 | tf_op jit(solution)/shard_map/all_to_all | solution.py:145
  115.2 2.1 %copy-start.20 = (bf16[1280,320]{0,1:T(8,128)(2,1)S(1)}, bf16[1280,320]{0,1:T(8,128)(2,1)}, u32[]{:S(2)}) copy-start(bf16[1280,320]{0,1:T(8,128)(2,1)} %param.9) | copy-start | bytes 2457604
  115.2 2.8 %copy-start.11 = (bf16[5,64,384]{2,1,0:T(8,128)(2,1)S(1)}, bf16[5,64,384]{2,1,0:T(8,128)(2,1)}, u32[]{:S(2)}) copy-start(bf16[5,64,384]{2,1,0:T(8,128)(2,1)} %fusion.22) | copy-start | bytes 737284
  118.0 1.1 copy-start.8
  123.3 4.3 %collective-permute-start = (bf16[384,2,320]{0,2,1:T(8,128)(2,1)}, bf16[384,2,320]{0,2,1:T(8,128)(2,1)}, u32[]{:S(2)}, u32[]{:S(2)}) collective-permute-start(bf16[384,2,320]{0,2,1:T(8,128)(2,1)} %dynamic-slice_bitcast_fusion), channel_id=1, source_target_pairs={{0,1},{1,0},{2,3},{3,2},{4,5},{5,4},{6,7},{7,6},{8,9},{9,8},{10,11... | collective-permute-start | bytes 1474568 | tf_op jit(solution)/shard_map/ppermute | solution.py:152
  125.6 5.1 %copy-start.6 = (bf16[1,5,384,768]{2,3,1,0:T(8,128)(2,1)S(1)}, bf16[1,5,384,768]{2,3,1,0:T(8,128)(2,1)}, u32[]{:S(2)}) copy-start(bf16[1,5,384,768]{2,3,1,0:T(8,128)(2,1)} %get-tuple-element.6) | copy-start | bytes 8847364
  125.6 5.1 %copy-start.13 = (bf16[384,320]{0,1:T(8,128)(2,1)S(1)}, bf16[384,320]{0,1:T(8,128)(2,1)}, u32[]{:S(2)}) copy-start(bf16[384,320]{0,1:T(8,128)(2,1)} %copy-done.12) | copy-start | bytes 737284
  128.7 25.1 %collective-permute-start.1 = (bf16[384,320]{0,1:T(8,128)(2,1)S(1)}, bf16[384,320]{0,1:T(8,128)(2,1)S(1)}, u32[]{:S(2)}, u32[]{:S(2)}) collective-permute-start(bf16[384,320]{0,1:T(8,128)(2,1)S(1)} %dynamic-slice_bitcast_fusion.1), channel_id=1, source_target_pairs={{0,2},{2,0},{1,3},{3,1},{4,6},{6,4},{5,7},{7,5},{8,10},{10,8},{9,1... | collective-permute-start | bytes 737288 | tf_op jit(solution)/shard_map/ppermute | solution.py:157

commit v2 on v1

v2 whole, which is shorter than its diff:
```python
import functools
import math

import jax
import jax.numpy as jnp
from jax import lax
from jax.experimental import pallas as pl
from jax.experimental.pallas import tpu as pltpu
from jax.sharding import Mesh
from jax.sharding import PartitionSpec as P

E = 64
P_SIZE = 384
HEADS = 5
WIDTH = HEADS * E
FRAMES = ("x", "y", "z")
TENSOR = ("h", "c")
NX, NYZ = 4, 32
REF_ROWS = 3
ROWS_OUT = 10
HALF_ROWS = ROWS_OUT // 2
LANES = 128
GROUPS = 2 * WIDTH // LANES
SCALE = 1.0 / math.sqrt(E)
F32 = jnp.float32
BF16 = jnp.bfloat16


def dot(a, b, a_dim, b_dim):
    return lax.dot_general(a, b, (((a_dim,), (b_dim,)), ((), ())), preferred_element_type=F32)


def attention_kernel(
    q_ref, k_ref, v_ref, r_ref, g_ref, tok_ref, o_ref, dq_ref, dk_ref, dv_ref, pack_ref,
    ot_ref, dqt_ref, sums_ref, dw_ref,
):
    for head in range(HEADS):
        lo, hi = head * E, head * E + E
        q, g = q_ref[:, lo:hi], g_ref[:, lo:hi]
        k = jnp.concatenate([k_ref[:, lo:hi], r_ref[:, lo:hi]], 0)
        v = jnp.concatenate([v_ref[:, lo:hi], r_ref[:, WIDTH + lo : WIDTH + hi]], 0)
        s = dot(k, q, 1, 1)
        s = jnp.exp2((s - jnp.max(s, axis=0, keepdims=True)) * (SCALE * math.log2(math.e)))
        p = s * (1.0 / jnp.sum(s, axis=0, keepdims=True))
        p_low = p.astype(BF16)
        ot_ref[lo:hi, :] = dot(v, p_low, 0, 0)
        dp = dot(v, g, 1, 1)
        ds = (p * (dp - jnp.sum(p * dp, axis=0, keepdims=True))).astype(BF16)
        dqt_ref[lo:hi, :] = dot(k, ds, 0, 0) * SCALE
        dk = dot(ds, q, 1, 0) * SCALE
        dv = dot(p_low, g, 1, 0)
        dk_ref[:, lo:hi] = dk[:P_SIZE].astype(BF16)
        dv_ref[:, lo:hi] = dv[:P_SIZE].astype(BF16)
        for col, part in ((lo, dk), (WIDTH + lo, dv)):
            at = col % LANES
            sums_ref[col // LANES, :, at : at + E] = part[P_SIZE:]
    o_ref[...] = ot_ref[...].T.astype(BF16)
    dq = dqt_ref[...].T.astype(BF16)
    dq_ref[...] = dq
    for x in range(NX):
        for row in range(REF_ROWS):
            first = x * REF_ROWS * NYZ + row
            for group in range(GROUPS):
                pack_ref[x, NYZ * row : NYZ * (row + 1), LANES * group : LANES * (group + 1)] = (
                    sums_ref[group, pl.ds(first, NYZ, stride=REF_ROWS), :].astype(BF16)
                )
        dw = dot(tok_ref[x * WIDTH : (x + 1) * WIDTH, :], dq, 1, 0)
        dw_ref[0], dw_ref[1] = dw[:, :LANES], dw[:, LANES : 2 * LANES]
        dw_ref[2, :, :E] = dw[:, 2 * LANES :]
        for row in range(HALF_ROWS):
            at = NYZ * (REF_ROWS + row)
            left, right = [
                [dw_ref[group, pl.ds(first, NYZ, stride=ROWS_OUT), :] for group in range(3)]
                for first in (row, row + HALF_ROWS)
            ]
            last = jnp.concatenate([left[2][:, :E], right[2][:, :E]], axis=1)
            for group, part in enumerate((left[0], left[1], right[0], right[1], last)):
                pack_ref[x, at : at + NYZ, LANES * group : LANES * (group + 1)] = part.astype(BF16)


def attention(q, k, v, ref_pair, g, tok):
    rows = REF_ROWS + HALF_ROWS
    full = jax.ShapeDtypeStruct((P_SIZE, WIDTH), BF16)
    return pl.pallas_call(
        attention_kernel,
        out_shape=(full,) * 4 + (jax.ShapeDtypeStruct((NX, NYZ * rows, 2 * WIDTH), BF16),),
        scratch_shapes=[
            pltpu.VMEM((WIDTH, P_SIZE), F32),
            pltpu.VMEM((WIDTH, P_SIZE), F32),
            pltpu.VMEM((GROUPS, P_SIZE, LANES), F32),
            pltpu.VMEM((3, WIDTH, LANES), F32),
        ],
        compiler_params=pltpu.CompilerParams(vmem_limit_bytes=48 * 1024 * 1024),
    )(q, k, v, ref_pair, g, tok)


def regroup_kernel(in_ref, out_ref, held_ref):
    rows = REF_ROWS + HALF_ROWS
    for row in range(rows):
        at = NYZ * row
        part = in_ref[0, at : at + NYZ, :].astype(F32)
        for x in range(1, NX):
            part = part + in_ref[x, at : at + NYZ, :].astype(F32)
        for group in range(GROUPS):
            held_ref[group, pl.ds(row, NYZ, stride=rows), :] = part[
                :, LANES * group : LANES * (group + 1)
            ]
    for group in range(GROUPS):
        out_ref[:, LANES * group : LANES * (group + 1)] = held_ref[group].astype(BF16)


def regroup(parts):
    rows = REF_ROWS + HALF_ROWS
    return pl.pallas_call(
        regroup_kernel,
        out_shape=jax.ShapeDtypeStruct((NYZ * rows, 2 * WIDTH), BF16),
        scratch_shapes=[pltpu.VMEM((GROUPS, NYZ * rows, LANES), F32)],
    )(parts)


def per_device(
    tokens, reference_image, query_weight, key_weight, value_weight, ref_weight, cotangent
):
    start_col = lax.axis_index(TENSOR) * WIDTH
    source_cols = lax.dynamic_slice_in_dim(reference_image, start_col, WIDTH, 1)
    ref_cols = (source_cols.astype(F32) + dot(reference_image, ref_weight, 1, 0)).astype(BF16)
    ref_block = jnp.pad(ref_cols, ((0, 16 - REF_ROWS), (0, P_SIZE - WIDTH)))
    gathered = lax.all_gather(
        jnp.concatenate([tokens.T, ref_block], axis=0), TENSOR, axis=0, tiled=False
    )
    ref_hidden = gathered[:, WIDTH : WIDTH + REF_ROWS, :WIDTH].transpose(1, 0, 2)
    ref_hidden = ref_hidden.reshape(REF_ROWS, 4 * WIDTH)
    ref_pair = jnp.concatenate(
        [dot(ref_hidden, key_weight, 1, 0), dot(ref_hidden, value_weight, 1, 0)], axis=1
    ).astype(BF16)
    n_frames = NX * NYZ
    ref_pair = jnp.broadcast_to(ref_pair.reshape(1, -1, 128), (n_frames, REF_ROWS * 5, 128))
    ref_all = lax.all_to_all(ref_pair, FRAMES, 0, 0, tiled=True).reshape(P_SIZE, 2 * WIDTH)
    tok = gathered[:, :WIDTH].reshape(4 * WIDTH, P_SIZE)
    queries = dot(tok, query_weight, 0, 0).astype(BF16)
    keys = dot(tok, key_weight, 0, 0).astype(BF16)
    values = dot(tok, value_weight, 0, 0).astype(BF16)
    attended, query_grads, key_grads, value_grads, pack = attention(
        queries, keys, values, ref_all, cotangent, tok
    )
    pack = lax.all_to_all(pack, "x", 0, 0, tiled=True)
    token_part = (
        dot(query_weight, query_grads, 1, 1)
        + dot(key_weight, key_grads, 1, 1)
        + dot(value_weight, value_grads, 1, 1)
    )
    token_blocks = token_part.astype(BF16).reshape(2, 2, WIDTH, P_SIZE)
    core, half = lax.axis_index("c"), lax.axis_index("h")
    kept = lax.dynamic_index_in_dim(token_blocks, core, 1, False)
    sent = lax.dynamic_index_in_dim(token_blocks, 1 - core, 1, False)
    got = lax.ppermute(sent, "c", [(0, 1), (1, 0)])
    paired = (kept.astype(F32) + got.astype(F32)).astype(BF16)
    pack, _ = lax.optimization_barrier((pack, paired))
    pack = regroup(pack).reshape(NYZ, REF_ROWS + HALF_ROWS, 2 * WIDTH)
    pack = lax.all_to_all(pack, ("y", "z"), 0, 0, tiled=True)
    sums = jnp.sum(pack.astype(F32), axis=0)
    left = jnp.concatenate([sums[REF_ROWS:, : 2 * LANES], sums[REF_ROWS:, 4 * LANES : 4 * LANES + E]], 1)
    right = jnp.concatenate([sums[REF_ROWS:, 2 * LANES : 4 * LANES], sums[REF_ROWS:, 4 * LANES + E :]], 1)
    weight_grad = jnp.concatenate([left, right], axis=0)
    kept = lax.dynamic_index_in_dim(paired, half, 0, False)
    sent = lax.dynamic_index_in_dim(paired, 1 - half, 0, False)
    got = lax.ppermute(sent, "h", [(0, 1), (1, 0)])
    token_grads = (kept.astype(F32) + got.astype(F32)).astype(BF16).T
    return (
        attended,
        token_grads,
        weight_grad,
        sums[:REF_ROWS, :WIDTH].astype(BF16),
        sums[:REF_ROWS, WIDTH:].astype(BF16),
    )


def solution(mesh):
    mesh = Mesh(mesh.devices.reshape(4, 8, 4, 2, 2), FRAMES + TENSOR)
    return jax.shard_map(
        per_device,
        mesh=mesh,
        in_specs=(
            P(FRAMES, TENSOR),
            P(FRAMES, None),
            P(None, TENSOR),
            P(None, TENSOR),
            P(None, TENSOR),
            P(None, TENSOR),
            P(FRAMES, TENSOR),
        ),
        out_specs=(P(FRAMES, TENSOR),) * 5,
        check_vma=False,
    )
```

time: 159 us -> 126 us (0.79); the launches traced: 156 us -> 125 us
  blocking collectives: 44.6 us -> 18.9 us
  matrix products: 26.8 us -> 8.49 us
  starting transfers between devices: 29.1 us -> 42.7 us
  local copies, waits for them, and re-layouts: 20.5 us -> 9.55 us
  Pallas kernels: 0 us -> 10.5 us
  other arithmetic: 12.1 us -> 2.68 us
  waiting for transfers between devices: 22.1 us -> 31.2 us
    all_gather x2 -> x1, blocking collectives: 44.6 us -> 18.9 us  [per_device(): lax.all_gather(jnp.concatenate([tokens.T, ref_block], axis=0), TENSOR, ax...]
    dot_general x22 -> x9, matrix products: 26.8 us -> 8.49 us  [dot(): lax.dot_general(a, b, (((a_dim,), (b_dim,)), ((), ())), preferred_element...]
    pallas_call x0 -> x2, Pallas kernels: none -> 10.5 us  [the longest x1 8.11 us: attention(): pl.pallas_call(attention_kernel, out_shape=(full,) * 4 + (jax.ShapeDtypeS...]
    all_to_all x1, waiting for transfers between devices: 0.01 us -> 9.44 us  [per_device(): lax.all_to_all(ref_pair, FRAMES, 0, 0, tiled=True)]
    ppermute x1, waiting for transfers between devices: 22.1 us -> 13.1 us  [per_device(): got = lax.ppermute(sent, 'h', [(0, 1), (1, 0)])]
    all_to_all x1, starting transfers between devices: 12 us -> 19.8 us  [per_device(): lax.all_to_all(ref_pair, FRAMES, 0, 0, tiled=True)]
    all_to_all x1 -> x2, waiting for transfers between devices: 0.01 us -> 7.2 us  [the longest x1 7.2 us: per_device(): pack = lax.all_to_all(pack, 'x', 0, 0, tiled=True)]
    reduce_sum x3 -> x1, other arithmetic: 6.27 us -> 0.06 us  [per_device(): sums = jnp.sum(pack.astype(F32), axis=0)]
  transfers between devices with their start and end apart: 4 -> 5, of which waited for: 1 -> 4; matrix products, arithmetic and copies ran while one was open for 13% -> 9% of each run, Pallas kernels for 0% -> 0%
where the time goes in v2:
time: 126 us; the launch traced here: 125 us
  starting transfers between devices  42.7 us (34%)
  waiting for transfers between devices  31.2 us (25%)
  blocking collectives  18.9 us (15%)
  Pallas kernels  10.5 us (8%)
  local copies, waits for them, and re-layouts  9.55 us (8%)
  matrix products  8.49 us (7%)
  other arithmetic  2.68 us (2%)
    all_to_all x1, starting transfers between devices, per_device(): lax.all_to_all(ref_pair, FRAMES, 0, 0, tiled=True)  19.8 us
    all_gather x1, blocking collectives, per_device(): lax.all_gather(jnp.concatenate([tokens.T, ref_block], axis=0), TENSOR, ax...  18.9 us
    ppermute x1, waiting for transfers between devices, per_device(): got = lax.ppermute(sent, 'h', [(0, 1), (1, 0)])  13.1 us
    all_to_all x1, waiting for transfers between devices, per_device(): lax.all_to_all(ref_pair, FRAMES, 0, 0, tiled=True)  9.44 us
    dot_general x9, matrix products, dot(): lax.dot_general(a, b, (((a_dim,), (b_dim,)), ((), ())), preferred_element...  8.49 us
    pallas_call x1, Pallas kernels, attention(): pl.pallas_call(attention_kernel, out_shape=(full,) * 4 + (jax.ShapeDtypeS...  8.11 us
    all_to_all x1, starting transfers between devices, per_device(): pack = lax.all_to_all(pack, ('y', 'z'), 0, 0, tiled=True)  7.92 us
    all_to_all x1, waiting for transfers between devices, per_device(): pack = lax.all_to_all(pack, 'x', 0, 0, tiled=True)  7.2 us
  transfers between devices with their start and end apart: 5, of which 4 were waited for; matrix products, arithmetic and copies ran while one was open for 9% of the time, Pallas kernels for 0%

profile of v2, /device:TPU:1, one launch (start us, length us, event | category | flops | bytes accessed | tf_op | source)
XLA Modules:
  0.0 125.0 jit_solution(7020167981692982894)
XLA Ops:
  0.6 0.0 copy-start
  0.6 0.0 copy-start.8
  0.7 1.6 %fusion.2 = bf16[3,320]{1,0:T(4,128)(2,1)S(1)} fusion(bf16[3,1280]{1,0:T(4,128)(2,1)} %param.8, bf16[1280,320]{0,1:T(8,128)(2,1)} %param.12, s32[]{:T(128)S(6)} %select_n.17), kind=kOutput, calls=%fused_computation.8 | convolution fusion | flops 2460480 | bytes 834436 | tf_op jit(solution)/shard_map/dot_general | solution.py:30
  2.3 1.0 fusion.6
  3.3 18.9 %all-gather = bf16[1344,384]{1,0:T(8,128)(2,1)S(1)} all-gather(bf16[336,384]{1,0:T(8,128)(2,1)S(1)} %fusion.6), channel_id=2, replica_groups=mesh['x'=4,'y'=8,'z'=4,'h'=2,'c'=2] {'h','c'}, dimensions={0}, use_global_device_ids=true | all-gather | bytes 1290240 | tf_op jit(solution)/shard_map/all_gather | solution.py:128
  22.2 0.1 reshape.37
  22.3 0.0 copy-done.8
  22.3 0.3 convolution_convert_fusion.3
  22.6 0.0 copy-done
  22.6 0.3 convolution_convert_fusion.4
  22.9 0.1 pad_maximum_fusion
  23.1 0.9 broadcast_in_dim.2
  24.0 19.8 %all-to-all-start = ((bf16[128,15,128]{2,1,0:T(8,128)(2,1)}), bf16[128,15,128]{2,1,0:T(8,128)(2,1)}, u32[]{:S(2)}, u32[]{:S(2)}) async-start(bf16[128,15,128]{2,1,0:T(8,128)(2,1)} %broadcast_in_dim.2), calls=%async_computation | async-start | bytes 1048576 | tf_op jit(solution)/shard_map/all_to_all | solution.py:138
  43.7 0.1 slice.34
  43.8 1.7 %convolution_convert_fusion.2 = bf16[384,320]{0,1:T(8,128)(2,1)S(1)} fusion(bf16[1280,320]{0,1:T(8,128)(2,1)} %param.9, bf16[1280,384]{1,0:T(8,128)(2,1)S(1)} %bitcast.40), kind=kOutput, calls=%fused_computation.6 | convolution fusion | flops 314695680 | bytes 2048000 | tf_op jit(solution)/shard_map/dot_general | solution.py:30
  45.6 0.0 copy-start.9
  45.6 0.2 copy.27.q_ref
  45.8 1.3 %convolution_convert_fusion.1 = bf16[384,320]{0,1:T(8,128)(2,1)} fusion(bf16[1280,320]{0,1:T(8,128)(2,1)S(1)} %copy-done, bf16[1280,384]{1,0:T(8,128)(2,1)S(1)} %bitcast.41), kind=kOutput, calls=%fused_computation.5 | convolution fusion | flops 314695680 | bytes 2048000 | tf_op jit(solution)/shard_map/dot_general | solution.py:30
  47.1 0.0 copy-start.12
  47.1 1.2 copy.28.k_ref
  48.3 0.0 copy-done.9
  48.3 1.3 %convolution_convert_fusion = bf16[384,320]{0,1:T(8,128)(2,1)} fusion(bf16[1280,320]{0,1:T(8,128)(2,1)S(1)} %copy-done.9, bf16[1280,384]{1,0:T(8,128)(2,1)S(1)} %bitcast.42), kind=kOutput, calls=%fused_computation.4 | convolution fusion | flops 314695680 | bytes 2048000 | tf_op jit(solution)/shard_map/dot_general | solution.py:30
  49.6 1.1 copy.29.v_ref
  50.7 0.0 copy-done.12
  50.8 0.2 copy.30.g_ref
  51.0 9.4 %all-to-all-done = bf16[128,15,128]{2,1,0:T(8,128)(2,1)} async-done(((bf16[128,15,128]{2,1,0:T(8,128)(2,1)}), bf16[128,15,128]{2,1,0:T(8,128)(2,1)}, u32[]{:S(2)}, u32[]{:S(2)}) %all-to-all-start) | async-done | bytes 491552 | tf_op jit(solution)/shard_map/all_to_all | solution.py:138
  60.4 1.5 %reshape.38.r_ref = bf16[384,640]{1,0:T(8,128)(2,1)S(1)} reshape(bf16[128,15,128]{2,1,0:T(8,128)(2,1)} %all-to-all-done) | data formatting | bytes 983040 | tf_op jit(solution)/shard_map/reshape | solution.py:138
  61.9 0.0 copy-start.11
  61.9 8.1 %shard_map.110 = (bf16[384,320]{1,0:T(8,128)(2,1)S(1)}, bf16[384,320]{1,0:T(8,128)(2,1)S(1)}, bf16[384,320]{1,0:T(8,128)(2,1)S(1)}, bf16[384,320]{1,0:T(8,128)(2,1)S(1)}, bf16[4,256,640]{2,1,0:T(8,128)(2,1)S(1)}) custom-call(bf16[384,320]{1,0:T(8,128)(2,1)S(1)} %copy.27.q_ref, bf16[384,320]{1,0:T(8,128)(2,1)S(1)} %copy.28.k_ref, ...), custom_call_target="tpu_custom_call" | custom-call | tf_op jit(solution)/shard_map/pallas_call | solution.py:84
  70.0 0.0 copy-start.2
  70.0 0.7 copy-done.2
  70.7 0.0 copy-start.1
  70.7 0.0 copy-done.11
  70.7 0.7 fusion.11
  71.4 0.4 copy-done.1
  71.8 0.1 copy-done.4
  71.9 0.1 copy-done.6
  72.0 4.7 %all-to-all-start.1 = ((bf16[4,256,640]{2,1,0:T(8,128)(2,1)}), bf16[4,256,640]{2,1,0:T(8,128)(2,1)}, u32[]{:S(2)}, u32[]{:S(2)}) async-start(bf16[4,256,640]{2,1,0:T(8,128)(2,1)} %copy-done.1), calls=%async_computation.1 | async-start | bytes 2621440 | tf_op jit(solution)/shard_map/all_to_all | solution.py:146
  76.6 0.0 copy-done.3
  76.6 0.0 copy-start.7
  76.6 0.0 copy-start.10
  76.7 0.7 convolution_add_fusion.1
  77.3 0.3 copy-done.7
  77.6 0.3 copy-done.10
  77.9 0.7 fusion.1
  78.6 0.7 copy.31
  79.2 0.1 dynamic-slice_bitcast_fusion
  79.3 4.1 %collective-permute-start = (bf16[2,320,384]{2,1,0:T(8,128)(2,1)S(1)}, bf16[2,320,384]{2,1,0:T(8,128)(2,1)S(1)}, u32[]{:S(2)}, u32[]{:S(2)}) collective-permute-start(bf16[2,320,384]{2,1,0:T(8,128)(2,1)S(1)} %dynamic-slice_bitcast_fusion), channel_id=1, source_target_pairs={{0,1},{1,0},{2,3},{3,2},{4,5},{5,4},{6,7},{7,6},{8,9},{9,8},{10,11... | collective-permute-start | bytes 1474568 | tf_op jit(solution)/shard_map/ppermute | solution.py:156
  83.4 0.0 copy-start.5
  83.4 1.5 %collective-permute-done = bf16[2,320,384]{2,1,0:T(8,128)(2,1)S(1)} collective-permute-done((bf16[2,320,384]{2,1,0:T(8,128)(2,1)S(1)}, bf16[2,320,384]{2,1,0:T(8,128)(2,1)S(1)}, u32[]{:S(2)}, u32[]{:S(2)}) %collective-permute-start) | collective-permute-done | bytes 491552 | tf_op jit(solution)/shard_map/ppermute | solution.py:156
  84.9 0.1 fusion.3
  85.0 7.2 %all-to-all-done.1.in_ref = bf16[4,256,640]{2,1,0:T(8,128)(2,1)} async-done(((bf16[4,256,640]{2,1,0:T(8,128)(2,1)}), bf16[4,256,640]{2,1,0:T(8,128)(2,1)}, u32[]{:S(2)}, u32[]{:S(2)}) %all-to-all-start.1) | async-done | bytes 1310752 | tf_op jit(solution)/shard_map/all_to_all | solution.py:146
  92.2 2.3 %shard_map.111 = bf16[256,640]{1,0:T(8,128)(2,1)} custom-call(bf16[4,256,640]{2,1,0:T(8,128)(2,1)} %all-to-all-done.1.in_ref), custom_call_target="tpu_custom_call" | custom-call | tf_op jit(solution)/shard_map/pallas_call | solution.py:114
  94.5 7.9 %all-to-all-start.2 = ((bf16[32,8,640]{2,1,0:T(8,128)(2,1)}), bf16[32,8,640]{2,1,0:T(8,128)(2,1)S(1)}, u32[]{:S(2)}, u32[]{:S(2)}) async-start(bf16[32,8,640]{2,1,0:T(8,128)(2,1)} %bitcast.48), calls=%async_computation.2 | async-start | bytes 655360 | tf_op jit(solution)/shard_map/all_to_all | solution.py:160
  102.5 6.3 %collective-permute-start.1 = (bf16[320,384]{1,0:T(8,128)(2,1)S(1)}, bf16[320,384]{1,0:T(8,128)(2,1)S(1)}, u32[]{:S(2)}, u32[]{:S(2)}) collective-permute-start(bf16[320,384]{1,0:T(8,128)(2,1)S(1)} %dynamic-slice_bitcast_fusion.1), channel_id=1, source_target_pairs={{0,2},{2,0},{1,3},{3,1},{4,6},{6,4},{5,7},{7,5},{8,10},{10,8},{9,1... | collective-permute-start | bytes 737288 | tf_op jit(solution)/shard_map/ppermute | solution.py:167
  108.8 0.0 copy-done.5
  108.8 0.9 copy.32
  109.7 13.1 %collective-permute-done.1 = bf16[320,384]{1,0:T(8,128)(2,1)S(1)} collective-permute-done((bf16[320,384]{1,0:T(8,128)(2,1)S(1)}, bf16[320,384]{1,0:T(8,128)(2,1)S(1)}, u32[]{:S(2)}, u32[]{:S(2)}) %collective-permute-start.1) | collective-permute-done | bytes 245792 | tf_op jit(solution)/shard_map/ppermute | solution.py:167
  122.8 0.8 fusion.7
  123.5 0.0 all-to-all-done.2
  123.5 0.1 convert_reduce_fusion
  123.6 0.1 fusion.9
  123.7 0.7 fusion.10
  124.4 0.6 maximum_maximum_fusion
  (9 shorter events, 0.1 us)
Async XLA Ops:
  0.6 22.0 %copy-start = (bf16[1280,320]{0,1:T(8,128)(2,1)S(1)}, bf16[1280,320]{0,1:T(8,128)(2,1)}, u32[]{:S(2)}) copy-start(bf16[1280,320]{0,1:T(8,128)(2,1)} %param.10) | copy-start | bytes 2457604
  0.6 21.7 %copy-start.8 = (bf16[1280,320]{0,1:T(8,128)(2,1)S(1)}, bf16[1280,320]{0,1:T(8,128)(2,1)}, u32[]{:S(2)}) copy-start(bf16[1280,320]{0,1:T(8,128)(2,1)} %param.11) | copy-start | bytes 2457604
  24.0 36.5 %all-to-all-start = ((bf16[128,15,128]{2,1,0:T(8,128)(2,1)}), bf16[128,15,128]{2,1,0:T(8,128)(2,1)}, u32[]{:S(2)}, u32[]{:S(2)}) async-start(bf16[128,15,128]{2,1,0:T(8,128)(2,1)} %broadcast_in_dim.2), calls=%async_computation | async-start | bytes 1048576 | tf_op jit(solution)/shard_map/all_to_all | solution.py:138
  45.6 2.7 %copy-start.9 = (bf16[1280,320]{0,1:T(8,128)(2,1)S(1)}, bf16[1280,320]{0,1:T(8,128)(2,1)}, u32[]{:S(2)}) copy-start(bf16[1280,320]{0,1:T(8,128)(2,1)} %param.11) | copy-start | bytes 2457604
  47.1 3.7 %copy-start.12 = (bf16[384,320]{0,1:T(8,128)(2,1)S(1)}, bf16[384,320]{0,1:T(8,128)(2,1)}, u32[]{:S(2)}) copy-start(bf16[384,320]{0,1:T(8,128)(2,1)} %param.13) | copy-start | bytes 737284
  61.9 8.8 %copy-start.11 = (bf16[1280,320]{0,1:T(8,128)(2,1)S(1)}, bf16[1280,320]{0,1:T(8,128)(2,1)}, u32[]{:S(2)}) copy-start(bf16[1280,320]{0,1:T(8,128)(2,1)} %param.9) | copy-start | bytes 2457604
  70.0 0.7 copy-start.2
  70.7 1.1 copy-start.1
  70.7 1.1 copy-start.4
  70.7 1.2 copy-start.6
  72.0 4.7 %copy-start.3 = (bf16[384,320]{1,0:T(8,128)(2,1)S(1)}, bf16[384,320]{1,0:T(8,128)(2,1)}, u32[]{:S(2)}) copy-start(bf16[384,320]{1,0:T(8,128)(2,1)} %copy-done.2) | copy-start | bytes 737284
  72.0 20.2 %all-to-all-start.1 = ((bf16[4,256,640]{2,1,0:T(8,128)(2,1)}), bf16[4,256,640]{2,1,0:T(8,128)(2,1)}, u32[]{:S(2)}, u32[]{:S(2)}) async-start(bf16[4,256,640]{2,1,0:T(8,128)(2,1)} %copy-done.1), calls=%async_computation.1 | async-start | bytes 2621440 | tf_op jit(solution)/shard_map/all_to_all | solution.py:146
  76.6 1.0 copy-start.7
  76.6 1.2 copy-start.10
  79.3 5.6 %collective-permute-start = (bf16[2,320,384]{2,1,0:T(8,128)(2,1)S(1)}, bf16[2,320,384]{2,1,0:T(8,128)(2,1)S(1)}, u32[]{:S(2)}, u32[]{:S(2)}) collective-permute-start(bf16[2,320,384]{2,1,0:T(8,128)(2,1)S(1)} %dynamic-slice_bitcast_fusion), channel_id=1, source_target_pairs={{0,1},{1,0},{2,3},{3,2},{4,5},{5,4},{6,7},{7,6},{8,9},{9,8},{10,11... | collective-permute-start | bytes 1474568 | tf_op jit(solution)/shard_map/ppermute | solution.py:156
  83.4 25.4 %copy-start.5 = (bf16[384,320]{1,0:T(8,128)(2,1)S(1)}, bf16[384,320]{1,0:T(8,128)(2,1)}, u32[]{:S(2)}) copy-start(bf16[384,320]{1,0:T(8,128)(2,1)} %copy-done.4) | copy-start | bytes 737284
  94.5 29.0 %all-to-all-start.2 = ((bf16[32,8,640]{2,1,0:T(8,128)(2,1)}), bf16[32,8,640]{2,1,0:T(8,128)(2,1)S(1)}, u32[]{:S(2)}, u32[]{:S(2)}) async-start(bf16[32,8,640]{2,1,0:T(8,128)(2,1)} %bitcast.48), calls=%async_computation.2 | async-start | bytes 655360 | tf_op jit(solution)/shard_map/all_to_all | solution.py:160
  102.5 20.3 %collective-permute-start.1 = (bf16[320,384]{1,0:T(8,128)(2,1)S(1)}, bf16[320,384]{1,0:T(8,128)(2,1)S(1)}, u32[]{:S(2)}, u32[]{:S(2)}) collective-permute-start(bf16[320,384]{1,0:T(8,128)(2,1)S(1)} %dynamic-slice_bitcast_fusion.1), channel_id=1, source_target_pairs={{0,2},{2,0},{1,3},{3,1},{4,6},{6,4},{5,7},{7,5},{8,10},{10,8},{9,1... | collective-permute-start | bytes 737288 | tf_op jit(solution)/shard_map/ppermute | solution.py:167

commit v3 on v2

v3 whole, which is shorter than its diff:
```python
import math

import jax
import jax.numpy as jnp
from jax import lax
from jax.experimental import pallas as pl
from jax.experimental.pallas import tpu as pltpu
from jax.sharding import Mesh
from jax.sharding import PartitionSpec as P

E = 64
P_SIZE = 384
HEADS = 5
WIDTH = HEADS * E
FRAMES = ("x", "y", "z")
TENSOR = ("h", "c")
NX, NYZ = 4, 32
REF_ROWS = 3
ROWS_OUT = 10
HALF_ROWS = ROWS_OUT // 2
LANES = 128
VMEM_BYTES = 24 * 1024 * 1024
GROUPS = 2 * WIDTH // LANES
SCALE = 1.0 / math.sqrt(E)
F32 = jnp.float32
BF16 = jnp.bfloat16


def dot(a, b, a_dim, b_dim):
    return lax.dot_general(a, b, (((a_dim,), (b_dim,)), ((), ())), preferred_element_type=F32)


def project_kernel(half_ref, t_ref, wq_ref, wk_ref, wv_ref, tok_ref, q_ref, k_ref, v_ref):
    half = half_ref[0]
    for core in range(2):
        for slot in range(2):
            at = pl.multiple_of((2 * lax.rem(half + slot, 2) + core) * WIDTH, E)
            tok_ref[pl.ds(at, WIDTH), :] = t_ref[core, slot]
    tok = tok_ref[...]
    for w_ref, out_ref in ((wq_ref, q_ref), (wk_ref, k_ref), (wv_ref, v_ref)):
        out_ref[...] = dot(w_ref[...], tok, 1, 0).T.astype(BF16)


def project(half, parts, wq, wk, wv):
    full = jax.ShapeDtypeStruct((P_SIZE, WIDTH), BF16)
    vmem = pl.BlockSpec(memory_space=pltpu.VMEM)
    return pl.pallas_call(
        project_kernel,
        out_shape=(jax.ShapeDtypeStruct((4 * WIDTH, P_SIZE), BF16),) + (full,) * 3,
        in_specs=[pl.BlockSpec(memory_space=pltpu.SMEM)] + [vmem] * 4,
        out_specs=[vmem] * 4,
        compiler_params=pltpu.CompilerParams(vmem_limit_bytes=VMEM_BYTES),
    )(half.reshape(1), parts, wq, wk, wv)


def attention_kernel(
    q_ref, k_ref, v_ref, pair_ref, gt_ref, tok_ref, ot_ref, dq_ref, dk_ref, dv_ref, pack_ref,
    wide_ref, r_ref, dqt_ref, dw_ref,
):
    n_frames = NX * NYZ
    wide_ref[...] = pair_ref[...].astype(F32)
    for row in range(REF_ROWS):
        for group in range(GROUPS):
            r_ref[n_frames * row : n_frames * (row + 1), LANES * group : LANES * (group + 1)] = (
                wide_ref[pl.ds(row * GROUPS + group, n_frames, stride=16), :].astype(BF16)
            )
    g_all = gt_ref[...].astype(F32).T.astype(BF16)
    for head in range(HEADS):
        lo, hi = head * E, head * E + E
        q, g = q_ref[:, lo:hi], g_all[:, lo:hi]
        k = jnp.concatenate([k_ref[:, lo:hi], r_ref[:, lo:hi]], 0)
        v = jnp.concatenate([v_ref[:, lo:hi], r_ref[:, WIDTH + lo : WIDTH + hi]], 0)
        s = dot(k, q, 1, 1)
        s = jnp.exp2((s - jnp.max(s, axis=0, keepdims=True)) * (SCALE * math.log2(math.e)))
        p = s * (1.0 / jnp.sum(s, axis=0, keepdims=True))
        p_low = p.astype(BF16)
        ot_ref[lo:hi, :] = dot(v, p_low, 0, 0).astype(BF16)
        dp = dot(v, gt_ref[lo:hi, :], 1, 0)
        ds = (p * (dp - jnp.sum(p * dp, axis=0, keepdims=True))).astype(BF16)
        dqt_ref[lo:hi, :] = dot(k, ds, 0, 0) * SCALE
        dk = dot(ds, q, 1, 0) * SCALE
        dv = dot(p_low, g, 1, 0)
        dk_ref[:, lo:hi] = dk[:P_SIZE].astype(BF16)
        dv_ref[:, lo:hi] = dv[:P_SIZE].astype(BF16)
        for col, part in ((lo, dk), (WIDTH + lo, dv)):
            for x in range(NX):
                for row in range(REF_ROWS):
                    at = P_SIZE + n_frames * row + NYZ * x
                    pack_ref[x, NYZ * row : NYZ * (row + 1), col : col + E] = part[
                        at : at + NYZ
                    ].astype(BF16)
    dq = dqt_ref[...].T.astype(BF16)
    dq_ref[...] = dq
    for x in range(NX):
        dw = dot(tok_ref[x * WIDTH : (x + 1) * WIDTH, :], dq, 1, 0)
        dw_ref[0], dw_ref[1] = dw[:, :LANES], dw[:, LANES : 2 * LANES]
        dw_ref[2, :, :E] = dw[:, 2 * LANES :]
        for row in range(HALF_ROWS):
            at = NYZ * (REF_ROWS + row)
            left, right = [
                [dw_ref[group, pl.ds(first, NYZ, stride=ROWS_OUT), :] for group in range(3)]
                for first in (row, row + HALF_ROWS)
            ]
            last = jnp.concatenate([left[2][:, :E], right[2][:, :E]], axis=1)
            for group, part in enumerate((left[0], left[1], right[0], right[1], last)):
                pack_ref[x, at : at + NYZ, LANES * group : LANES * (group + 1)] = part.astype(BF16)


def attention(q, k, v, pair, gt, tok):
    rows = REF_ROWS + HALF_ROWS
    full = jax.ShapeDtypeStruct((P_SIZE, WIDTH), BF16)
    return pl.pallas_call(
        attention_kernel,
        out_shape=(jax.ShapeDtypeStruct((WIDTH, P_SIZE), BF16),)
        + (full,) * 3
        + (jax.ShapeDtypeStruct((NX, NYZ * rows, 2 * WIDTH), BF16),),
        scratch_shapes=[
            pltpu.VMEM((NX * NYZ * 16, LANES), F32),
            pltpu.VMEM((P_SIZE, 2 * WIDTH), BF16),
            pltpu.VMEM((WIDTH, P_SIZE), F32),
            pltpu.VMEM((3, WIDTH, LANES), F32),
        ],
        compiler_params=pltpu.CompilerParams(vmem_limit_bytes=VMEM_BYTES),
    )(q, k, v, pair, gt, tok)


def token_kernel(core_ref, dq_ref, dk_ref, dv_ref, wq_ref, wk_ref, wv_ref, kept_ref, sent_ref):
    core = core_ref[0]
    total = dot(dq_ref[...], wq_ref[...], 1, 0)
    total = total + dot(dk_ref[...], wk_ref[...], 1, 0)
    total = total + dot(dv_ref[...], wv_ref[...], 1, 0)
    total = total.T.astype(BF16)
    for half in range(2):
        zero, one = [total[(2 * half + c) * WIDTH : (2 * half + c + 1) * WIDTH] for c in range(2)]
        kept_ref[half] = jnp.where(core == 0, zero, one)
        sent_ref[half] = jnp.where(core == 0, one, zero)


def token_parts(core, dq, dk, dv, wq, wk, wv):
    vmem = pl.BlockSpec(memory_space=pltpu.VMEM)
    return pl.pallas_call(
        token_kernel,
        out_shape=(jax.ShapeDtypeStruct((2, WIDTH, P_SIZE), BF16),) * 2,
        in_specs=[pl.BlockSpec(memory_space=pltpu.SMEM)] + [vmem] * 6,
        out_specs=[vmem] * 2,
        compiler_params=pltpu.CompilerParams(vmem_limit_bytes=VMEM_BYTES),
    )(core.reshape(1), dq, dk, dv, wq, wk, wv)


def regroup_kernel(in_ref, out_ref, held_ref):
    rows = REF_ROWS + HALF_ROWS
    for row in range(rows):
        at = NYZ * row
        part = in_ref[0, at : at + NYZ, :].astype(F32)
        for x in range(1, NX):
            part = part + in_ref[x, at : at + NYZ, :].astype(F32)
        for group in range(GROUPS):
            held_ref[group, pl.ds(row, NYZ, stride=rows), :] = part[
                :, LANES * group : LANES * (group + 1)
            ]
    for group in range(GROUPS):
        out_ref[:, LANES * group : LANES * (group + 1)] = held_ref[group].astype(BF16)


def regroup(parts):
    rows = REF_ROWS + HALF_ROWS
    return pl.pallas_call(
        regroup_kernel,
        out_shape=jax.ShapeDtypeStruct((NYZ * rows, 2 * WIDTH), BF16),
        scratch_shapes=[pltpu.VMEM((GROUPS, NYZ * rows, LANES), F32)],
    )(parts)


def per_device(
    tokens, reference_image, query_weight, key_weight, value_weight, ref_weight, cotangent
):
    core, half = lax.axis_index("c"), lax.axis_index("h")
    swap = [(0, 1), (1, 0)]
    wq, wk, wv = query_weight.T, key_weight.T, value_weight.T
    own = tokens.T
    other = lax.ppermute(own, "h", swap)
    start_col = (2 * half + core) * WIDTH
    source_cols = lax.dynamic_slice_in_dim(reference_image, start_col, WIDTH, 1)
    ref_cols = (source_cols.astype(F32) + dot(reference_image, ref_weight, 1, 0)).astype(BF16)
    ref_hidden = lax.all_gather(ref_cols, TENSOR, axis=1, tiled=True)
    pair = jnp.concatenate([dot(ref_hidden, wk, 1, 1), dot(ref_hidden, wv, 1, 1)], axis=1)
    pair = pair.astype(BF16).reshape(1, REF_ROWS * GROUPS, LANES)
    pair = jnp.pad(pair, ((0, 0), (0, 16 - REF_ROWS * GROUPS), (0, 0)))
    pair = lax.all_to_all(
        jnp.broadcast_to(pair, (NYZ, 16, LANES)), ("y", "z"), 0, 0, tiled=True
    ).reshape(1, NYZ * 16, LANES)
    pair = lax.all_to_all(jnp.broadcast_to(pair, (NX, NYZ * 16, LANES)), "x", 0, 0, tiled=True)
    parts = lax.all_gather(jnp.stack([own, other]), "c", axis=0, tiled=False)
    tok, queries, keys, values = project(half, parts, wq, wk, wv)
    attended, query_grads, key_grads, value_grads, pack = attention(
        queries, keys, values, pair.reshape(NX * NYZ * 16, LANES), cotangent.T, tok
    )
    pack = lax.all_to_all(pack, "x", 0, 0, tiled=True)
    kept, sent = token_parts(core, query_grads, key_grads, value_grads, wq, wk, wv)
    got = lax.ppermute(sent, "c", swap)
    paired = (kept.astype(F32) + got.astype(F32)).astype(BF16)
    kept = lax.dynamic_index_in_dim(paired, half, 0, False)
    sent = lax.dynamic_index_in_dim(paired, 1 - half, 0, False)
    got = lax.ppermute(sent, "h", swap)
    token_grads = (kept.astype(F32) + got.astype(F32)).astype(BF16).T
    pack = regroup(pack)
    pack, _ = lax.optimization_barrier((pack, got))
    pack = pack.reshape(NYZ, REF_ROWS + HALF_ROWS, 2 * WIDTH)
    pack = lax.all_to_all(pack, ("y", "z"), 0, 0, tiled=True)
    sums = jnp.sum(pack.astype(F32), axis=0)
    low, tail = sums[REF_ROWS:, : 4 * LANES], sums[REF_ROWS:, 4 * LANES :]
    left = jnp.concatenate([low[:, : 2 * LANES], tail[:, :E]], axis=1)
    right = jnp.concatenate([low[:, 2 * LANES :], tail[:, E:]], axis=1)
    return (
        attended.T,
        token_grads,
        jnp.concatenate([left, right], axis=0),
        sums[:REF_ROWS, :WIDTH].astype(BF16),
        sums[:REF_ROWS, WIDTH:].astype(BF16),
    )


def solution(mesh):
    mesh = Mesh(mesh.devices.reshape(4, 8, 4, 2, 2), FRAMES + TENSOR)
    return jax.shard_map(
        per_device,
        mesh=mesh,
        in_specs=(
            P(FRAMES, TENSOR),
            P(FRAMES, None),
            P(None, TENSOR),
            P(None, TENSOR),
            P(None, TENSOR),
            P(None, TENSOR),
            P(FRAMES, TENSOR),
        ),
        out_specs=(P(FRAMES, TENSOR),) * 5,
        check_vma=False,
    )
```

time: 126 us -> 127 us (level); the launches traced: 125 us -> 124 us
  waiting for transfers between devices: 31.2 us -> 22.5 us
  matrix products: 8.49 us -> 2.82 us
  Pallas kernels: 10.5 us -> 15.6 us
  local copies, waits for them, and re-layouts: 9.55 us -> 14.5 us
  starting transfers between devices: 42.7 us -> 45.4 us
    ppermute x2 -> x3, waiting for transfers between devices: 14.6 us -> 0.95 us  [the longest x1 0.95 us: per_device(): other = lax.ppermute(own, 'h', swap)]
    all_to_all x1, waiting for transfers between devices: 0.01 us -> 11.1 us  [per_device(): pack = lax.all_to_all(pack, ('y', 'z'), 0, 0, tiled=True)]
    unnamed x29 -> x39, local copies, waits for them, and re-layouts: 2.96 us -> 12.2 us
    all_to_all x1 -> x2, starting transfers between devices: 19.8 us -> 11.8 us  [the longest x1 7.72 us: per_device(): lax.all_to_all(jnp.broadcast_to(pair, (NYZ, 16, LANES)), ('y', 'z'), 0, 0...]
    ppermute x2 -> x3, starting transfers between devices: 10.4 us -> 17.7 us  [the longest x1 7.84 us: per_device(): got = lax.ppermute(sent, 'h', swap)]
    all_to_all x1 -> x2, waiting for transfers between devices: 9.44 us -> 2.63 us  [the longest x1 2.63 us: per_device(): lax.all_to_all(jnp.broadcast_to(pair, (NYZ, 16, LANES)), ('y', 'z'), 0, 0...]
    dot_general x9 -> x3, matrix products: 8.49 us -> 2.82 us  [dot(): lax.dot_general(a, b, (((a_dim,), (b_dim,)), ((), ())), preferred_element...]
    pallas_call x1 -> x3, Pallas kernels: 8.11 us -> 13.2 us  [the longest x1 9.1 us: attention(): pl.pallas_call(attention_kernel, out_shape=(jax.ShapeDtypeStruct((WIDTH,...]
  transfers between devices with their start and end apart: 5 -> 7, of which waited for: 4 -> 4; matrix products, arithmetic and copies ran while one was open for 9% -> 3% of each run, Pallas kernels for 0% -> 3%
where the time goes in v3:
time: 127 us; the launch traced here: 124 us
  starting transfers between devices  45.4 us (36%)
  waiting for transfers between devices  22.5 us (18%)
  blocking collectives  19.1 us (15%)
  Pallas kernels  15.6 us (12%)
  local copies, waits for them, and re-layouts  14.5 us (11%)
  other arithmetic  3.71 us (3%)
  matrix products  2.82 us (2%)
    all_gather x1, blocking collectives, per_device(): ref_hidden = lax.all_gather(ref_cols, TENSOR, axis=1, tiled=True)  15.8 us
    unnamed x39, local copies, waits for them, and re-layouts  12.2 us
    all_to_all x1, starting transfers between devices, per_device(): pack = lax.all_to_all(pack, ('y', 'z'), 0, 0, tiled=True)  11.3 us
    all_to_all x1, waiting for transfers between devices, per_device(): pack = lax.all_to_all(pack, ('y', 'z'), 0, 0, tiled=True)  11.1 us
    pallas_call x1, Pallas kernels, attention(): pl.pallas_call(attention_kernel, out_shape=(jax.ShapeDtypeStruct((WIDTH,...  9.1 us
    ppermute x1, starting transfers between devices, per_device(): got = lax.ppermute(sent, 'h', swap)  7.84 us
    all_to_all x1, waiting for transfers between devices, per_device(): pack = lax.all_to_all(pack, 'x', 0, 0, tiled=True)  7.75 us
    all_to_all x1, starting transfers between devices, per_device(): lax.all_to_all(jnp.broadcast_to(pair, (NYZ, 16, LANES)), ('y', 'z'), 0, 0...  7.72 us
  transfers between devices with their start and end apart: 7, of which 4 were waited for; matrix products, arithmetic and copies ran while one was open for 3% of the time, Pallas kernels for 3%

profile of v3, /device:TPU:1, one launch (start us, length us, event | category | flops | bytes accessed | tf_op | source)
XLA Modules:
  0.0 124.4 jit_solution(16144658003930371949)
XLA Ops:
  0.6 0.0 copy-start
  0.6 0.0 copy-start.1
  0.7 1.1 copy-done
  1.8 0.0 copy-start.18
  1.8 1.1 fusion.1
  2.9 15.8 %all-gather.1 = bf16[4,320,3]{1,2,0:T(4,128)(2,1)S(1)} all-gather(bf16[1,320,3]{1,2,0:T(4,128)(2,1)S(1)} %fusion.1), channel_id=1, replica_groups=mesh['x'=4,'y'=8,'z'=4,'h'=2,'c'=2] {'h','c'}, dimensions={0}, use_global_device_ids=true | all-gather | bytes 9600 | tf_op jit(solution)/shard_map/all_gather | solution.py:185
  18.6 0.1 reshape.45
  18.7 1.4 %convolution_convert_fusion = bf16[3,320]{1,0:T(4,128)(2,1)S(1)} fusion(bf16[1280,3]{0,1:T(4,128)(2,1)S(1)} %reshape.45, bf16[1280,320]{0,1:T(8,128)(2,1)} %param.11), kind=kOutput, calls=%fused_computation.2 | convolution fusion | flops 2458560 | bytes 828800 | tf_op jit(solution)/shard_map/dot_general | solution.py:30
  20.1 0.0 copy-done.1
  20.1 0.3 convolution_convert_fusion.1
  20.5 0.1 pad_maximum_fusion.1
  20.6 0.7 broadcast_in_dim.15
  21.3 7.7 %all-to-all-start = ((bf16[32,16,128]{2,1,0:T(8,128)(2,1)}), bf16[32,16,128]{2,1,0:T(8,128)(2,1)S(1)}, u32[]{:S(2)}, u32[]{:S(2)}) async-start(bf16[32,16,128]{2,1,0:T(8,128)(2,1)} %broadcast_in_dim.15), calls=%async_computation | async-start | bytes 262144 | tf_op jit(solution)/shard_map/all_to_all | solution.py:189
  29.0 0.0 copy-done.18
  29.1 7.5 %collective-permute-start = (bf16[320,384]{1,0:T(8,128)(2,1)S(1)}, bf16[320,384]{1,0:T(8,128)(2,1)}, u32[]{:S(2)}, u32[]{:S(2)}) collective-permute-start(bf16[320,384]{1,0:T(8,128)(2,1)S(1)} %bitcast.46), channel_id=1, source_target_pairs={{0,2},{2,0},{1,3},{3,1},{4,6},{6,4},{5,7},{7,5},{8,10},{10,8},{9,1... | collective-permute-start | bytes 737288 | tf_op jit(solution)/shard_map/ppermute | solution.py:181
  36.5 2.6 %all-to-all-done = bf16[32,16,128]{2,1,0:T(8,128)(2,1)S(1)} async-done(((bf16[32,16,128]{2,1,0:T(8,128)(2,1)}), bf16[32,16,128]{2,1,0:T(8,128)(2,1)S(1)}, u32[]{:S(2)}, u32[]{:S(2)}) %all-to-all-start) | async-done | bytes 131104 | tf_op jit(solution)/shard_map/all_to_all | solution.py:189
  39.2 0.9 broadcast_in_dim.17
  40.0 4.1 %all-to-all-start.1 = ((bf16[4,512,128]{2,1,0:T(8,128)(2,1)}), bf16[4,512,128]{2,1,0:T(8,128)(2,1)}, u32[]{:S(2)}, u32[]{:S(2)}) async-start(bf16[4,512,128]{2,1,0:T(8,128)(2,1)} %broadcast_in_dim.17), calls=%async_computation.1 | async-start | bytes 1048576 | tf_op jit(solution)/shard_map/all_to_all | solution.py:192
  44.2 0.0 copy-start.2
  44.2 0.0 copy-start.3
  44.2 0.9 collective-permute-done
  45.1 1.0 pad_maximum_fusion
  46.1 3.3 %all-gather = bf16[4,320,384]{2,1,0:T(8,128)(2,1)S(1)} all-gather(bf16[2,320,384]{2,1,0:T(8,128)(2,1)S(1)} %pad_maximum_fusion), channel_id=2, replica_groups=mesh['x'=4,'y'=8,'z'=4,'h'=2,'c'=2] {'c'}, dimensions={0}, use_global_device_ids=true | all-gather | bytes 1474560 | tf_op jit(solution)/shard_map/all_gather | solution.py:193
  49.5 0.0 copy-done.2
  49.5 0.0 copy-done.3
  49.5 0.0 copy-start.15
  49.5 1.6 %shard_map.110 = (bf16[1280,384]{1,0:T(8,128)(2,1)S(1)}, bf16[384,320]{1,0:T(8,128)(2,1)S(1)}, bf16[384,320]{1,0:T(8,128)(2,1)S(1)}, bf16[384,320]{1,0:T(8,128)(2,1)S(1)}) custom-call(s32[1]{0:T(128)} %bitcast.half_ref, bf16[2,2,320,384]{3,2,1,0:T(8,128)(2,1)S(1)} %bitcast.40, bf16[320,1280]{1,0:T(8,128)(2,1)S(1)} %bitcast.41, ...), custom_call_target="tpu_custom_call" | custom-call | tf_op jit(solution)/shard_map/pallas_call | solution.py:47
  51.1 0.0 copy-start.5
  51.1 0.9 copy-done.5
  52.0 0.0 copy-start.9
  52.0 0.7 copy-done.9
  52.7 0.0 copy-start.11
  52.7 0.7 copy-done.11
  53.5 0.7 copy-done.13
  54.2 0.0 all-to-all-done.1
  54.2 0.0 copy-done.15
  54.2 1.2 copy-done.6
  55.4 1.0 copy-done.10
  56.3 1.0 copy-done.12
  57.3 1.0 copy-done.14
  58.3 9.1 %shard_map.111 = (bf16[320,384]{1,0:T(8,128)(2,1)}, bf16[384,320]{1,0:T(8,128)(2,1)S(1)}, bf16[384,320]{1,0:T(8,128)(2,1)S(1)}, bf16[384,320]{1,0:T(8,128)(2,1)S(1)}, bf16[4,256,640]{2,1,0:T(8,128)(2,1)S(1)}) custom-call(bf16[384,320]{1,0:T(8,128)(2,1)S(1)} %copy-done.10, bf16[384,320]{1,0:T(8,128)(2,1)S(1)} %copy-done.12, bf16[384,320]{1,0:T(8,128)(2,1)S(1)} %copy-done.14, ...), custom_call_target="tpu_custom_call" | custom-call | tf_op jit(solution)/shard_map/pallas_call | solution.py:112
  67.4 0.0 copy-start.4
  67.4 1.1 copy-done.4
  68.5 2.5 %shard_map.112 = (bf16[2,320,384]{2,1,0:T(8,128)(2,1)S(1)}, bf16[2,320,384]{2,1,0:T(8,128)(2,1)}) custom-call(s32[1]{0:T(128)} %bitcast.15.core_ref, bf16[384,320]{1,0:T(8,128)(2,1)S(1)} %get-tuple-element.22.dq_ref, bf16[384,320]{1,0:T(8,128)(2,1)S(1)} %get-tuple-element.23.dk_ref, bf16[384,320]{1,0:T(8,128)(2,1)S(1)} %get-tuple-element.24.dv_ref, ...), custom_call_target="tpu_custom_call" | custom-call | tf_op jit(solution)/shard_map/pallas_call | solution.py:141
  71.0 0.8 copy-done.7
  71.8 2.4 %collective-permute-start.1 = (bf16[2,320,384]{2,1,0:T(8,128)(2,1)}, bf16[2,320,384]{2,1,0:T(8,128)(2,1)S(1)}, u32[]{:S(2)}, u32[]{:S(2)}) collective-permute-start(bf16[2,320,384]{2,1,0:T(8,128)(2,1)} %get-tuple-element.26), channel_id=1, source_target_pairs={{0,1},{1,0},{2,3},{3,2},{4,5},{5,4},{6,7},{7,6},{8,9},{9,8},{10,11... | collective-permute-start | bytes 1474568 | tf_op jit(solution)/shard_map/ppermute | solution.py:200
  74.2 0.0 copy-start.8
  74.2 4.5 %all-to-all-start.2 = ((bf16[4,256,640]{2,1,0:T(8,128)(2,1)}), bf16[4,256,640]{2,1,0:T(8,128)(2,1)S(1)}, u32[]{:S(2)}, u32[]{:S(2)}) async-start(bf16[4,256,640]{2,1,0:T(8,128)(2,1)} %copy-done.4), calls=%async_computation.2 | async-start | bytes 2621440 | tf_op jit(solution)/shard_map/all_to_all | solution.py:198
  78.7 0.0 collective-permute-done.1
  78.7 0.8 copy-done.17
  79.5 0.0 copy-done.8
  79.5 1.2 add_convert_fusion
  80.7 7.8 %collective-permute-start.2 = (bf16[320,384]{1,0:T(8,128)(2,1)S(1)}, bf16[320,384]{1,0:T(8,128)(2,1)S(1)}, u32[]{:S(2)}, u32[]{:S(2)}) collective-permute-start(bf16[320,384]{1,0:T(8,128)(2,1)S(1)} %dynamic-slice_bitcast_fusion), channel_id=1, source_target_pairs={{0,2},{2,0},{1,3},{3,1},{4,6},{6,4},{5,7},{7,5},{8,10},{10,8},{9,1... | collective-permute-start | bytes 737288 | tf_op jit(solution)/shard_map/ppermute | solution.py:204
  88.6 7.7 %all-to-all-done.2.in_ref = bf16[4,256,640]{2,1,0:T(8,128)(2,1)S(1)} async-done(((bf16[4,256,640]{2,1,0:T(8,128)(2,1)}), bf16[4,256,640]{2,1,0:T(8,128)(2,1)S(1)}, u32[]{:S(2)}, u32[]{:S(2)}) %all-to-all-start.2) | async-done | bytes 1310752 | tf_op jit(solution)/shard_map/all_to_all | solution.py:198
  96.3 1.1 copy-done.16
  97.4 2.3 %shard_map.113 = bf16[256,640]{1,0:T(8,128)(2,1)} custom-call(bf16[4,256,640]{2,1,0:T(8,128)(2,1)} %copy-done.16), custom_call_target="tpu_custom_call" | custom-call | tf_op jit(solution)/shard_map/pallas_call | solution.py:167
  99.7 0.0 collective-permute-done.2
  99.7 11.3 %all-to-all-start.3 = ((bf16[32,8,640]{2,1,0:T(8,128)(2,1)}), bf16[32,8,640]{2,1,0:T(8,128)(2,1)S(1)}, u32[]{:S(2)}, u32[]{:S(2)}) async-start(bf16[32,8,640]{2,1,0:T(8,128)(2,1)} %bitcast.44), calls=%async_computation.3 | async-start | bytes 655360 | tf_op jit(solution)/shard_map/all_to_all | solution.py:209
  111.1 0.8 fusion.3
  111.8 11.1 %all-to-all-done.3 = bf16[32,8,640]{2,1,0:T(8,128)(2,1)S(1)} async-done(((bf16[32,8,640]{2,1,0:T(8,128)(2,1)}), bf16[32,8,640]{2,1,0:T(8,128)(2,1)S(1)}, u32[]{:S(2)}, u32[]{:S(2)}) %all-to-all-start.3) | async-done | bytes 327712 | tf_op jit(solution)/shard_map/all_to_all | solution.py:209
  122.9 0.1 convert_reduce_fusion
  123.0 0.1 fusion.5
  123.1 0.7 fusion.6
  123.7 0.6 maximum_maximum_fusion
  (14 shorter events, 0.1 us)
Async XLA Ops:
  0.6 1.2 copy-start
  0.6 19.5 %copy-start.1 = (bf16[1280,320]{0,1:T(8,128)(2,1)S(1)}, bf16[1280,320]{0,1:T(8,128)(2,1)}, u32[]{:S(2)}) copy-start(bf16[1280,320]{0,1:T(8,128)(2,1)} %param.10) | copy-start | bytes 2457604
  1.8 27.3 %copy-start.18 = (bf16[384,320]{0,1:T(8,128)(2,1)S(1)}, bf16[384,320]{0,1:T(8,128)(2,1)}, u32[]{:S(2)}) copy-start(bf16[384,320]{0,1:T(8,128)(2,1)} %param.7) | copy-start | bytes 737284
  21.3 17.9 %all-to-all-start = ((bf16[32,16,128]{2,1,0:T(8,128)(2,1)}), bf16[32,16,128]{2,1,0:T(8,128)(2,1)S(1)}, u32[]{:S(2)}, u32[]{:S(2)}) async-start(bf16[32,16,128]{2,1,0:T(8,128)(2,1)} %broadcast_in_dim.15), calls=%async_computation | async-start | bytes 262144 | tf_op jit(solution)/shard_map/all_to_all | solution.py:189
  29.1 16.1 %collective-permute-start = (bf16[320,384]{1,0:T(8,128)(2,1)S(1)}, bf16[320,384]{1,0:T(8,128)(2,1)}, u32[]{:S(2)}, u32[]{:S(2)}) collective-permute-start(bf16[320,384]{1,0:T(8,128)(2,1)S(1)} %bitcast.46), channel_id=1, source_target_pairs={{0,2},{2,0},{1,3},{3,1},{4,6},{6,4},{5,7},{7,5},{8,10},{10,8},{9,1... | collective-permute-start | bytes 737288 | tf_op jit(solution)/shard_map/ppermute | solution.py:181
  40.0 14.1 %all-to-all-start.1 = ((bf16[4,512,128]{2,1,0:T(8,128)(2,1)}), bf16[4,512,128]{2,1,0:T(8,128)(2,1)}, u32[]{:S(2)}, u32[]{:S(2)}) async-start(bf16[4,512,128]{2,1,0:T(8,128)(2,1)} %broadcast_in_dim.17), calls=%async_computation.1 | async-start | bytes 1048576 | tf_op jit(solution)/shard_map/all_to_all | solution.py:192
  44.2 5.3 %copy-start.2 = (bf16[1280,320]{0,1:T(8,128)(2,1)S(1)}, bf16[1280,320]{0,1:T(8,128)(2,1)}, u32[]{:S(2)}) copy-start(bf16[1280,320]{0,1:T(8,128)(2,1)} %param.11) | copy-start | bytes 2457604
  44.2 5.3 %copy-start.3 = (bf16[1280,320]{0,1:T(8,128)(2,1)S(1)}, bf16[1280,320]{0,1:T(8,128)(2,1)}, u32[]{:S(2)}) copy-start(bf16[1280,320]{0,1:T(8,128)(2,1)} %param.9) | copy-start | bytes 2457604
  49.5 4.7 %copy-start.15 = (bf16[384,320]{0,1:T(8,128)(2,1)S(1)}, bf16[384,320]{0,1:T(8,128)(2,1)}, u32[]{:S(2)}) copy-start(bf16[384,320]{0,1:T(8,128)(2,1)} %param.13) | copy-start | bytes 737284
  51.1 1.0 copy-start.5
  52.0 0.7 copy-start.9
  52.7 0.7 copy-start.11
  53.5 0.7 copy-start.13
  54.2 1.2 copy-start.6
  55.4 1.0 copy-start.10
  56.3 1.0 copy-start.12
  57.3 1.0 copy-start.14
  67.4 1.1 copy-start.4
  71.0 0.8 copy-start.7
  71.8 6.9 %collective-permute-start.1 = (bf16[2,320,384]{2,1,0:T(8,128)(2,1)}, bf16[2,320,384]{2,1,0:T(8,128)(2,1)S(1)}, u32[]{:S(2)}, u32[]{:S(2)}) collective-permute-start(bf16[2,320,384]{2,1,0:T(8,128)(2,1)} %get-tuple-element.26), channel_id=1, source_target_pairs={{0,1},{1,0},{2,3},{3,2},{4,5},{5,4},{6,7},{7,6},{8,9},{9,8},{10,11... | collective-permute-start | bytes 1474568 | tf_op jit(solution)/shard_map/ppermute | solution.py:200
  74.2 5.3 %copy-start.8 = (bf16[2,320,384]{2,1,0:T(8,128)(2,1)S(1)}, bf16[2,320,384]{2,1,0:T(8,128)(2,1)}, u32[]{:S(2)}) copy-start(bf16[2,320,384]{2,1,0:T(8,128)(2,1)} %copy-done.7) | copy-start | bytes 1474564
  74.2 22.1 %all-to-all-start.2 = ((bf16[4,256,640]{2,1,0:T(8,128)(2,1)}), bf16[4,256,640]{2,1,0:T(8,128)(2,1)S(1)}, u32[]{:S(2)}, u32[]{:S(2)}) async-start(bf16[4,256,640]{2,1,0:T(8,128)(2,1)} %copy-done.4), calls=%async_computation.2 | async-start | bytes 2621440 | tf_op jit(solution)/shard_map/all_to_all | solution.py:198
  78.7 0.8 copy-start.17
  80.7 19.0 %collective-permute-start.2 = (bf16[320,384]{1,0:T(8,128)(2,1)S(1)}, bf16[320,384]{1,0:T(8,128)(2,1)S(1)}, u32[]{:S(2)}, u32[]{:S(2)}) collective-permute-start(bf16[320,384]{1,0:T(8,128)(2,1)S(1)} %dynamic-slice_bitcast_fusion), channel_id=1, source_target_pairs={{0,2},{2,0},{1,3},{3,1},{4,6},{6,4},{5,7},{7,5},{8,10},{10,8},{9,1... | collective-permute-start | bytes 737288 | tf_op jit(solution)/shard_map/ppermute | solution.py:204
  96.3 1.1 copy-start.16
  99.7 23.2 %all-to-all-start.3 = ((bf16[32,8,640]{2,1,0:T(8,128)(2,1)}), bf16[32,8,640]{2,1,0:T(8,128)(2,1)S(1)}, u32[]{:S(2)}, u32[]{:S(2)}) async-start(bf16[32,8,640]{2,1,0:T(8,128)(2,1)} %bitcast.44), calls=%async_computation.3 | async-start | bytes 655360 | tf_op jit(solution)/shard_map/all_to_all | solution.py:209

commit v4 on v3

--- a/solution.py
+++ b/solution.py
@@ -30,34 +30,54 @@
     return lax.dot_general(a, b, (((a_dim,), (b_dim,)), ((), ())), preferred_element_type=F32)
 
 
-def project_kernel(half_ref, t_ref, wq_ref, wk_ref, wv_ref, tok_ref, q_ref, k_ref, v_ref):
+def project_kernel(
+    half_ref, t_ref, wq_ref, wk_ref, wv_ref, tok_out, q_out, k_out, v_out,
+    tok_ref, q_ref, k_ref, v_ref, sem,
+):
     half = half_ref[0]
+    pairs = ((tok_ref, tok_out), (q_ref, q_out), (k_ref, k_out), (v_ref, v_out))
+    copies = [pltpu.make_async_copy(a, b, sem.at[i]) for i, (a, b) in enumerate(pairs)]
     for core in range(2):
         for slot in range(2):
             at = pl.multiple_of((2 * lax.rem(half + slot, 2) + core) * WIDTH, E)
             tok_ref[pl.ds(at, WIDTH), :] = t_ref[core, slot]
+    copies[0].start()
     tok = tok_ref[...]
-    for w_ref, out_ref in ((wq_ref, q_ref), (wk_ref, k_ref), (wv_ref, v_ref)):
+    for i, (w_ref, out_ref) in enumerate(((wq_ref, q_ref), (wk_ref, k_ref), (wv_ref, v_ref))):
         out_ref[...] = dot(w_ref[...], tok, 1, 0).T.astype(BF16)
+        copies[i + 1].start()
+    for copy in copies:
+        copy.wait()
 
 
 def project(half, parts, wq, wk, wv):
-    full = jax.ShapeDtypeStruct((P_SIZE, WIDTH), BF16)
     vmem = pl.BlockSpec(memory_space=pltpu.VMEM)
     return pl.pallas_call(
         project_kernel,
-        out_shape=(jax.ShapeDtypeStruct((4 * WIDTH, P_SIZE), BF16),) + (full,) * 3,
+        out_shape=(pltpu.HBM((4 * WIDTH, P_SIZE), BF16),)
+        + (pltpu.HBM((P_SIZE, WIDTH), BF16),) * 3,
         in_specs=[pl.BlockSpec(memory_space=pltpu.SMEM)] + [vmem] * 4,
-        out_specs=[vmem] * 4,
+        out_specs=[pl.BlockSpec(memory_space=pltpu.HBM)] * 4,
+        scratch_shapes=[pltpu.VMEM((4 * WIDTH, P_SIZE), BF16)]
+        + [pltpu.VMEM((P_SIZE, WIDTH), BF16)] * 3
+        + [pltpu.SemaphoreType.DMA((4,))],
         compiler_params=pltpu.CompilerParams(vmem_limit_bytes=VMEM_BYTES),
     )(half.reshape(1), parts, wq, wk, wv)
 
 
 def attention_kernel(
-    q_ref, k_ref, v_ref, pair_ref, gt_ref, tok_ref, ot_ref, dq_ref, dk_ref, dv_ref, pack_ref,
-    wide_ref, r_ref, dqt_ref, dw_ref,
+    q_in, k_in, v_in, pair_in, tok_in, gt_ref, ot_out, dq_out, dk_out, dv_out, pack_out,
+    q_ref, k_ref, v_ref, pair_ref, tok_ref, wide_ref, r_ref, dqt_ref, dw_ref,
+    ot_ref, dq_ref, dk_ref, dv_ref, pack_ref, in_sem, out_sem,
 ):
     n_frames = NX * NYZ
+    pairs = (
+        (pair_in, pair_ref), (k_in, k_ref), (q_in, q_ref), (v_in, v_ref), (tok_in, tok_ref)
+    )
+    loads = [pltpu.make_async_copy(a, b, in_sem.at[i]) for i, (a, b) in enumerate(pairs)]
+    for load in loads:
+        load.start()
+    loads[0].wait()
     wide_ref[...] = pair_ref[...].astype(F32)
     for row in range(REF_ROWS):
         for group in range(GROUPS):
@@ -65,6 +85,8 @@
                 wide_ref[pl.ds(row * GROUPS + group, n_frames, stride=16), :].astype(BF16)
             )
     g_all = gt_ref[...].astype(F32).T.astype(BF16)
+    for load in loads[1:4]:
+        load.wait()
     for head in range(HEADS):
         lo, hi = head * E, head * E + E
         q, g = q_ref[:, lo:hi], g_all[:, lo:hi]
@@ -91,6 +113,11 @@
                     ].astype(BF16)
     dq = dqt_ref[...].T.astype(BF16)
     dq_ref[...] = dq
+    loads[4].wait()
+    pairs = ((ot_ref, ot_out), (dq_ref, dq_out), (dk_ref, dk_out), (dv_ref, dv_out))
+    stores = [pltpu.make_async_copy(a, b, out_sem.at[NX + i]) for i, (a, b) in enumerate(pairs)]
+    for store in stores:
+        store.start()
     for x in range(NX):
         dw = dot(tok_ref[x * WIDTH : (x + 1) * WIDTH, :], dq, 1, 0)
         dw_ref[0], dw_ref[1] = dw[:, :LANES], dw[:, LANES : 2 * LANES]
@@ -104,24 +131,40 @@
             last = jnp.concatenate([left[2][:, :E], right[2][:, :E]], axis=1)
             for group, part in enumerate((left[0], left[1], right[0], right[1], last)):
                 pack_ref[x, at : at + NYZ, LANES * group : LANES * (group + 1)] = part.astype(BF16)
+        stores.append(pltpu.make_async_copy(pack_ref.at[x], pack_out.at[x], out_sem.at[x]))
+        stores[-1].start()
+    for store in stores:
+        store.wait()
 
 
 def attention(q, k, v, pair, gt, tok):
+    hbm, vmem = [pl.BlockSpec(memory_space=space) for space in (pltpu.HBM, pltpu.VMEM)]
     rows = REF_ROWS + HALF_ROWS
-    full = jax.ShapeDtypeStruct((P_SIZE, WIDTH), BF16)
     return pl.pallas_call(
         attention_kernel,
-        out_shape=(jax.ShapeDtypeStruct((WIDTH, P_SIZE), BF16),)
-        + (full,) * 3
-        + (jax.ShapeDtypeStruct((NX, NYZ * rows, 2 * WIDTH), BF16),),
-        scratch_shapes=[
+        out_shape=(pltpu.HBM((WIDTH, P_SIZE), BF16),)
+        + (pltpu.HBM((P_SIZE, WIDTH), BF16),) * 3
+        + (pltpu.HBM((NX, NYZ * rows, 2 * WIDTH), BF16),),
+        in_specs=[hbm] * 5 + [vmem],
+        out_specs=[hbm] * 5,
+        scratch_shapes=[pltpu.VMEM((P_SIZE, WIDTH), BF16)] * 3
+        + [
+            pltpu.VMEM((NX * NYZ * 16, LANES), BF16),
+            pltpu.VMEM((4 * WIDTH, P_SIZE), BF16),
             pltpu.VMEM((NX * NYZ * 16, LANES), F32),
             pltpu.VMEM((P_SIZE, 2 * WIDTH), BF16),
             pltpu.VMEM((WIDTH, P_SIZE), F32),
             pltpu.VMEM((3, WIDTH, LANES), F32),
+            pltpu.VMEM((WIDTH, P_SIZE), BF16),
+            pltpu.VMEM((P_SIZE, WIDTH), BF16),
+            pltpu.VMEM((P_SIZE, WIDTH), BF16),
+            pltpu.VMEM((P_SIZE, WIDTH), BF16),
+            pltpu.VMEM((NX, NYZ * rows, 2 * WIDTH), BF16),
+            pltpu.SemaphoreType.DMA((5,)),
+            pltpu.SemaphoreType.DMA((NX + 4,)),
         ],
         compiler_params=pltpu.CompilerParams(vmem_limit_bytes=VMEM_BYTES),
-    )(q, k, v, pair, gt, tok)
+    )(*[pltpu.with_memory_space_constraint(a, pltpu.HBM) for a in (q, k, v, pair, tok)], gt)
 
 
 def token_kernel(core_ref, dq_ref, dk_ref, dv_ref, wq_ref, wk_ref, wv_ref, kept_ref, sent_ref):
@@ -168,6 +211,7 @@
         regroup_kernel,
         out_shape=jax.ShapeDtypeStruct((NYZ * rows, 2 * WIDTH), BF16),
         scratch_shapes=[pltpu.VMEM((GROUPS, NYZ * rows, LANES), F32)],
+        compiler_params=pltpu.CompilerParams(vmem_limit_bytes=8 * 1024 * 1024),
     )(parts)
 
 
@@ -185,6 +229,7 @@
     ref_hidden = lax.all_gather(ref_cols, TENSOR, axis=1, tiled=True)
     pair = jnp.concatenate([dot(ref_hidden, wk, 1, 1), dot(ref_hidden, wv, 1, 1)], axis=1)
     pair = pair.astype(BF16).reshape(1, REF_ROWS * GROUPS, LANES)
+    pair, other = lax.optimization_barrier((pair, other))
     pair = jnp.pad(pair, ((0, 0), (0, 16 - REF_ROWS * GROUPS), (0, 0)))
     pair = lax.all_to_all(
         jnp.broadcast_to(pair, (NYZ, 16, LANES)), ("y", "z"), 0, 0, tiled=True
@@ -204,7 +249,7 @@
     got = lax.ppermute(sent, "h", swap)
     token_grads = (kept.astype(F32) + got.astype(F32)).astype(BF16).T
     pack = regroup(pack)
-    pack, _ = lax.optimization_barrier((pack, got))
+    pack, _ = lax.optimization_barrier((pack, sent))
     pack = pack.reshape(NYZ, REF_ROWS + HALF_ROWS, 2 * WIDTH)
     pack = lax.all_to_all(pack, ("y", "z"), 0, 0, tiled=True)
     sums = jnp.sum(pack.astype(F32), axis=0)

time: 127 us -> 121 us (0.953); the launches traced: 124 us -> 120 us
  blocking collectives: 19.1 us -> 35.1 us
  starting transfers between devices: 45.4 us -> 35.5 us
  local copies, waits for them, and re-layouts: 14.5 us -> 5.53 us
  waiting for transfers between devices: 22.5 us -> 18.4 us
  Pallas kernels: 15.6 us -> 18.2 us
    all_to_all x0 -> x1, blocking collectives: none -> 21 us  [per_device(): lax.all_to_all(jnp.broadcast_to(pair, (NYZ, 16, LANES)), ('y', 'z'), 0, 0...]
    ppermute x1, waiting for transfers between devices: 0.01 us -> 13.9 us  [per_device(): got = lax.ppermute(sent, 'h', swap)]
    all_to_all x1, waiting for transfers between devices: 11.1 us -> 0.01 us  [per_device(): pack = lax.all_to_all(pack, ('y', 'z'), 0, 0, tiled=True)]
    unnamed x39 -> x23, local copies, waits for them, and re-layouts: 12.2 us -> 3.83 us
    all_to_all x1 -> x0, starting transfers between devices: 7.72 us -> none  [per_device(): lax.all_to_all(jnp.broadcast_to(pair, (NYZ, 16, LANES)), ('y', 'z'), 0, 0...]
    all_to_all x1, starting transfers between devices: 11.3 us -> 3.87 us  [per_device(): pack = lax.all_to_all(pack, ('y', 'z'), 0, 0, tiled=True)]
    all_gather x1, blocking collectives: 15.8 us -> 9.94 us  [per_device(): ref_hidden = lax.all_gather(ref_cols, TENSOR, axis=1, tiled=True)]
    all_to_all x1, waiting for transfers between devices: 7.75 us -> 2.83 us  [per_device(): pack = lax.all_to_all(pack, 'x', 0, 0, tiled=True)]
  transfers between devices with their start and end apart: 7 -> 6, of which waited for: 4 -> 3; matrix products, arithmetic and copies ran while one was open for 3% -> 5% of each run, Pallas kernels for 3% -> 4%
where the time goes in v4:
time: 121 us; the launch traced here: 120 us
  starting transfers between devices  35.5 us (29%)
  blocking collectives  35.1 us (29%)
  waiting for transfers between devices  18.4 us (15%)
  Pallas kernels  18.2 us (15%)
  local copies, waits for them, and re-layouts  5.53 us (5%)
  other arithmetic  3.83 us (3%)
  matrix products  2.79 us (2%)
    all_to_all x1, blocking collectives, per_device(): lax.all_to_all(jnp.broadcast_to(pair, (NYZ, 16, LANES)), ('y', 'z'), 0, 0...  21 us
    ppermute x1, waiting for transfers between devices, per_device(): got = lax.ppermute(sent, 'h', swap)  13.9 us
    ppermute x1, starting transfers between devices, per_device(): other = lax.ppermute(own, 'h', swap)  11.6 us
    pallas_call x1, Pallas kernels, attention(): pl.pallas_call(attention_kernel, out_shape=(pltpu.HBM((WIDTH, P_SIZE), BF...  10.7 us
    all_gather x1, blocking collectives, per_device(): ref_hidden = lax.all_gather(ref_cols, TENSOR, axis=1, tiled=True)  9.94 us
    ppermute x1, starting transfers between devices, per_device(): got = lax.ppermute(sent, 'h', swap)  7.04 us
    all_to_all x1, starting transfers between devices, per_device(): pack = lax.all_to_all(pack, 'x', 0, 0, tiled=True)  4.53 us
    ppermute x1, starting transfers between devices, per_device(): got = lax.ppermute(sent, 'c', swap)  4.32 us
  transfers between devices with their start and end apart: 6, of which 3 were waited for; matrix products, arithmetic and copies ran while one was open for 5% of the time, Pallas kernels for 4%

profile of v4, /device:TPU:1, one launch (start us, length us, event | category | flops | bytes accessed | tf_op | source)
XLA Modules:
  0.0 120.2 jit_solution(14916027780773840993)
XLA Ops:
  0.6 0.0 copy-start
  0.6 0.0 copy-start.1
  0.7 11.6 %collective-permute-start = (bf16[320,384]{1,0:T(8,128)(2,1)}, bf16[320,384]{1,0:T(8,128)(2,1)S(1)}, u32[]{:S(2)}, u32[]{:S(2)}) collective-permute-start(bf16[320,384]{1,0:T(8,128)(2,1)} %bitcast.45), channel_id=1, source_target_pairs={{0,2},{2,0},{1,3},{3,1},{4,6},{6,4},{5,7},{7,5},{8,10},{10,8},{9,1... | collective-permute-start | bytes 737288 | tf_op jit(solution)/shard_map/ppermute | solution.py:225
  12.3 0.0 copy-done
  12.3 1.1 fusion.1
  13.4 9.9 %all-gather.1 = bf16[4,320,3]{1,2,0:T(4,128)(2,1)S(1)} all-gather(bf16[1,320,3]{1,2,0:T(4,128)(2,1)S(1)} %fusion.1), channel_id=1, replica_groups=mesh['x'=4,'y'=8,'z'=4,'h'=2,'c'=2] {'h','c'}, dimensions={0}, use_global_device_ids=true | all-gather | bytes 9600 | tf_op jit(solution)/shard_map/all_gather | solution.py:229
  23.3 0.1 reshape.45
  23.4 1.4 %convolution_convert_fusion = bf16[3,320]{1,0:T(4,128)(2,1)S(1)} fusion(bf16[1280,3]{0,1:T(4,128)(2,1)S(1)} %reshape.45, bf16[1280,320]{0,1:T(8,128)(2,1)} %param.11), kind=kOutput, calls=%fused_computation.2 | convolution fusion | flops 2458560 | bytes 828800 | tf_op jit(solution)/shard_map/dot_general | solution.py:30
  24.8 0.0 copy-done.1
  24.8 0.0 copy-start.9
  24.9 0.3 convolution_convert_fusion.1
  25.2 0.1 pad_maximum_fusion.1
  25.3 0.0 collective-permute-done
  25.3 0.0 copy-start.10
  25.4 21.0 %all_to_all.20 = bf16[32,16,128]{2,1,0:T(8,128)(2,1)S(1)} all-to-all(bf16[32,16,128]{2,1,0:T(8,128)(2,1)S(1)} %broadcast_in_dim.15), channel_id=1, replica_groups=mesh['x'=4,'y'=8,'z'=4,'h'=2,'c'=2] {'y','z'}, dimensions={0} | all-to-all | bytes 262144 | tf_op jit(solution)/shard_map/all_to_all | solution.py:234
  46.4 0.9 broadcast_in_dim.17
  47.3 0.0 copy-done.10
  47.3 4.1 %all-to-all-start.1 = ((bf16[4,512,128]{2,1,0:T(8,128)(2,1)}), bf16[4,512,128]{2,1,0:T(8,128)(2,1)}, u32[]{:S(2)}, u32[]{:S(2)}) async-start(bf16[4,512,128]{2,1,0:T(8,128)(2,1)} %broadcast_in_dim.17), calls=%async_computation.1 | async-start | bytes 1048576 | tf_op jit(solution)/shard_map/all_to_all | solution.py:237
  51.4 0.0 copy-start.2
  51.4 0.0 copy-start.3
  51.4 0.0 copy-done.9
  51.4 1.1 pad_maximum_fusion
  52.6 4.2 %all-gather = bf16[4,320,384]{2,1,0:T(8,128)(2,1)S(1)} all-gather(bf16[2,320,384]{2,1,0:T(8,128)(2,1)S(1)} %pad_maximum_fusion), channel_id=2, replica_groups=mesh['x'=4,'y'=8,'z'=4,'h'=2,'c'=2] {'c'}, dimensions={0}, use_global_device_ids=true | all-gather | bytes 1474560 | tf_op jit(solution)/shard_map/all_gather | solution.py:238
  56.7 0.0 copy-done.2
  56.7 0.0 copy-done.3
  56.7 0.0 copy-start.8
  56.8 2.6 %shard_map.110 = (bf16[1280,384]{1,0:T(8,128)(2,1)}, bf16[384,320]{1,0:T(8,128)(2,1)}, bf16[384,320]{1,0:T(8,128)(2,1)}, bf16[384,320]{1,0:T(8,128)(2,1)}) custom-call(s32[1]{0:T(128)} %bitcast.half_ref, bf16[2,2,320,384]{3,2,1,0:T(8,128)(2,1)S(1)} %bitcast.40, bf16[320,1280]{1,0:T(8,128)(2,1)S(1)} %bitcast.41, bf16[320,1280]{1,0:T(8,128)(2,1)S(1)} %bitcast.36, ...), custom_call_target="tpu_custom_call" | custom-call | tf_op jit(solution)/shard_map/pallas_call | solution.py:55
  59.4 0.0 all-to-all-done.1
  59.4 0.0 copy-done.8
  59.4 10.7 %shard_map.111 = (bf16[320,384]{1,0:T(8,128)(2,1)}, bf16[384,320]{1,0:T(8,128)(2,1)}, bf16[384,320]{1,0:T(8,128)(2,1)}, bf16[384,320]{1,0:T(8,128)(2,1)}, bf16[4,256,640]{2,1,0:T(8,128)(2,1)}) custom-call(bf16[384,320]{1,0:T(8,128)(2,1)} %get-tuple-element.20.q_in, bf16[384,320]{1,0:T(8,128)(2,1)} %get-tuple-element.21.k_in, ...), custom_call_target="tpu_custom_call" | custom-call | tf_op jit(solution)/shard_map/pallas_call | solution.py:143
  70.1 4.5 %all-to-all-start.2 = ((bf16[4,256,640]{2,1,0:T(8,128)(2,1)}), bf16[4,256,640]{2,1,0:T(8,128)(2,1)}, u32[]{:S(2)}, u32[]{:S(2)}) async-start(bf16[4,256,640]{2,1,0:T(8,128)(2,1)} %get-tuple-element.31), calls=%async_computation.2 | async-start | bytes 2621440 | tf_op jit(solution)/shard_map/all_to_all | solution.py:243
  74.6 0.0 copy-start.5
  74.6 1.0 copy-done.5
  75.6 0.0 copy-start.6
  75.6 1.0 copy-done.6
  76.6 0.0 copy-start.7
  76.6 1.0 copy-done.7
  77.5 2.5 %shard_map.112 = (bf16[2,320,384]{2,1,0:T(8,128)(2,1)S(1)}, bf16[2,320,384]{2,1,0:T(8,128)(2,1)}) custom-call(s32[1]{0:T(128)} %bitcast.15.core_ref, bf16[384,320]{1,0:T(8,128)(2,1)S(1)} %copy-done.5, bf16[384,320]{1,0:T(8,128)(2,1)S(1)} %copy-done.6, bf16[384,320]{1,0:T(8,128)(2,1)S(1)} %copy-done.7, bf16[320,1280]{1,0:T(8,128)(2,1)S(1)} %bitcast.42, ...), custom_call_target="tpu_custom_call" | custom-call | tf_op jit(solution)/shard_map/pallas_call | solution.py:184
  80.1 0.0 copy-start.4
  80.1 0.8 copy-done.4
  80.9 4.3 %collective-permute-start.1 = (bf16[2,320,384]{2,1,0:T(8,128)(2,1)}, bf16[2,320,384]{2,1,0:T(8,128)(2,1)S(1)}, u32[]{:S(2)}, u32[]{:S(2)}) collective-permute-start(bf16[2,320,384]{2,1,0:T(8,128)(2,1)} %get-tuple-element.30), channel_id=1, source_target_pairs={{0,1},{1,0},{2,3},{3,2},{4,5},{5,4},{6,7},{7,6},{8,9},{9,8},{10,11... | collective-permute-start | bytes 1474568 | tf_op jit(solution)/shard_map/ppermute | solution.py:245
  85.2 1.7 %collective-permute-done.1 = bf16[2,320,384]{2,1,0:T(8,128)(2,1)S(1)} collective-permute-done((bf16[2,320,384]{2,1,0:T(8,128)(2,1)}, bf16[2,320,384]{2,1,0:T(8,128)(2,1)S(1)}, u32[]{:S(2)}, u32[]{:S(2)}) %collective-permute-start.1) | collective-permute-done | bytes 491552 | tf_op jit(solution)/shard_map/ppermute | solution.py:245
  86.9 1.1 add_convert_fusion
  88.1 2.8 %all-to-all-done.2.in_ref = bf16[4,256,640]{2,1,0:T(8,128)(2,1)} async-done(((bf16[4,256,640]{2,1,0:T(8,128)(2,1)}), bf16[4,256,640]{2,1,0:T(8,128)(2,1)}, u32[]{:S(2)}, u32[]{:S(2)}) %all-to-all-start.2) | async-done | bytes 1310752 | tf_op jit(solution)/shard_map/all_to_all | solution.py:243
  90.9 2.3 %shard_map.113 = bf16[256,640]{1,0:T(8,128)(2,1)} custom-call(bf16[4,256,640]{2,1,0:T(8,128)(2,1)} %all-to-all-done.2.in_ref), custom_call_target="tpu_custom_call" | custom-call | tf_op jit(solution)/shard_map/pallas_call | solution.py:210
  93.2 3.9 %all-to-all-start.3 = ((bf16[32,8,640]{2,1,0:T(8,128)(2,1)}), bf16[32,8,640]{2,1,0:T(8,128)(2,1)S(1)}, u32[]{:S(2)}, u32[]{:S(2)}) async-start(bf16[32,8,640]{2,1,0:T(8,128)(2,1)} %bitcast.19), calls=%async_computation.3 | async-start | bytes 655360 | tf_op jit(solution)/shard_map/all_to_all | solution.py:254
  97.1 7.0 %collective-permute-start.2 = (bf16[320,384]{1,0:T(8,128)(2,1)S(1)}, bf16[320,384]{1,0:T(8,128)(2,1)S(1)}, u32[]{:S(2)}, u32[]{:S(2)}) collective-permute-start(bf16[320,384]{1,0:T(8,128)(2,1)S(1)} %dynamic-slice_bitcast_fusion), channel_id=1, source_target_pairs={{0,2},{2,0},{1,3},{3,1},{4,6},{6,4},{5,7},{7,5},{8,10},{10,8},{9,1... | collective-permute-start | bytes 737288 | tf_op jit(solution)/shard_map/ppermute | solution.py:249
  104.2 13.9 %collective-permute-done.2 = bf16[320,384]{1,0:T(8,128)(2,1)S(1)} collective-permute-done((bf16[320,384]{1,0:T(8,128)(2,1)S(1)}, bf16[320,384]{1,0:T(8,128)(2,1)S(1)}, u32[]{:S(2)}, u32[]{:S(2)}) %collective-permute-start.2) | collective-permute-done | bytes 245792 | tf_op jit(solution)/shard_map/ppermute | solution.py:249
  118.0 0.8 fusion.3
  118.8 0.0 all-to-all-done.3
  118.8 0.1 convert_reduce_fusion
  118.9 0.1 fusion.5
  118.9 0.7 fusion.6
  119.6 0.6 maximum_maximum_fusion
  (7 shorter events, 0.1 us)
Async XLA Ops:
  0.6 11.6 %copy-start = (bf16[1280,320]{0,1:T(8,128)(2,1)S(1)}, bf16[1280,320]{0,1:T(8,128)(2,1)}, u32[]{:S(2)}) copy-start(bf16[1280,320]{0,1:T(8,128)(2,1)} %param.12) | copy-start | bytes 2457604
  0.6 24.2 %copy-start.1 = (bf16[1280,320]{0,1:T(8,128)(2,1)S(1)}, bf16[1280,320]{0,1:T(8,128)(2,1)}, u32[]{:S(2)}) copy-start(bf16[1280,320]{0,1:T(8,128)(2,1)} %param.10) | copy-start | bytes 2457604
  0.7 24.7 %collective-permute-start = (bf16[320,384]{1,0:T(8,128)(2,1)}, bf16[320,384]{1,0:T(8,128)(2,1)S(1)}, u32[]{:S(2)}, u32[]{:S(2)}) collective-permute-start(bf16[320,384]{1,0:T(8,128)(2,1)} %bitcast.45), channel_id=1, source_target_pairs={{0,2},{2,0},{1,3},{3,1},{4,6},{6,4},{5,7},{7,5},{8,10},{10,8},{9,1... | collective-permute-start | bytes 737288 | tf_op jit(solution)/shard_map/ppermute | solution.py:225
  24.8 26.6 %copy-start.9 = (bf16[384,320]{0,1:T(8,128)(2,1)S(1)}, bf16[384,320]{0,1:T(8,128)(2,1)}, u32[]{:S(2)}) copy-start(bf16[384,320]{0,1:T(8,128)(2,1)} %param.7) | copy-start | bytes 737284
  25.3 21.9 %copy-start.10 = (bf16[320,384]{1,0:T(8,128)(2,1)}, bf16[320,384]{1,0:T(8,128)(2,1)S(1)}, u32[]{:S(2)}) copy-start(bf16[320,384]{1,0:T(8,128)(2,1)S(1)} %collective-permute-done) | copy-start | bytes 737284
  47.3 12.1 %all-to-all-start.1 = ((bf16[4,512,128]{2,1,0:T(8,128)(2,1)}), bf16[4,512,128]{2,1,0:T(8,128)(2,1)}, u32[]{:S(2)}, u32[]{:S(2)}) async-start(bf16[4,512,128]{2,1,0:T(8,128)(2,1)} %broadcast_in_dim.17), calls=%async_computation.1 | async-start | bytes 1048576 | tf_op jit(solution)/shard_map/all_to_all | solution.py:237
  51.4 5.3 %copy-start.2 = (bf16[1280,320]{0,1:T(8,128)(2,1)S(1)}, bf16[1280,320]{0,1:T(8,128)(2,1)}, u32[]{:S(2)}) copy-start(bf16[1280,320]{0,1:T(8,128)(2,1)} %param.11) | copy-start | bytes 2457604
  51.4 5.3 %copy-start.3 = (bf16[1280,320]{0,1:T(8,128)(2,1)S(1)}, bf16[1280,320]{0,1:T(8,128)(2,1)}, u32[]{:S(2)}) copy-start(bf16[1280,320]{0,1:T(8,128)(2,1)} %param.9) | copy-start | bytes 2457604
  56.7 2.7 %copy-start.8 = (bf16[384,320]{0,1:T(8,128)(2,1)S(1)}, bf16[384,320]{0,1:T(8,128)(2,1)}, u32[]{:S(2)}) copy-start(bf16[384,320]{0,1:T(8,128)(2,1)} %param.13) | copy-start | bytes 737284
  70.1 20.8 %all-to-all-start.2 = ((bf16[4,256,640]{2,1,0:T(8,128)(2,1)}), bf16[4,256,640]{2,1,0:T(8,128)(2,1)}, u32[]{:S(2)}, u32[]{:S(2)}) async-start(bf16[4,256,640]{2,1,0:T(8,128)(2,1)} %get-tuple-element.31), calls=%async_computation.2 | async-start | bytes 2621440 | tf_op jit(solution)/shard_map/all_to_all | solution.py:243
  74.6 1.0 copy-start.5
  75.6 1.0 copy-start.6
  76.6 1.0 copy-start.7
  80.1 0.8 copy-start.4
  80.9 6.0 %collective-permute-start.1 = (bf16[2,320,384]{2,1,0:T(8,128)(2,1)}, bf16[2,320,384]{2,1,0:T(8,128)(2,1)S(1)}, u32[]{:S(2)}, u32[]{:S(2)}) collective-permute-start(bf16[2,320,384]{2,1,0:T(8,128)(2,1)} %get-tuple-element.30), channel_id=1, source_target_pairs={{0,1},{1,0},{2,3},{3,2},{4,5},{5,4},{6,7},{7,6},{8,9},{9,8},{10,11... | collective-permute-start | bytes 1474568 | tf_op jit(solution)/shard_map/ppermute | solution.py:245
  93.2 25.6 %all-to-all-start.3 = ((bf16[32,8,640]{2,1,0:T(8,128)(2,1)}), bf16[32,8,640]{2,1,0:T(8,128)(2,1)S(1)}, u32[]{:S(2)}, u32[]{:S(2)}) async-start(bf16[32,8,640]{2,1,0:T(8,128)(2,1)} %bitcast.19), calls=%async_computation.3 | async-start | bytes 655360 | tf_op jit(solution)/shard_map/all_to_all | solution.py:254
  97.1 20.9 %collective-permute-start.2 = (bf16[320,384]{1,0:T(8,128)(2,1)S(1)}, bf16[320,384]{1,0:T(8,128)(2,1)S(1)}, u32[]{:S(2)}, u32[]{:S(2)}) collective-permute-start(bf16[320,384]{1,0:T(8,128)(2,1)S(1)} %dynamic-slice_bitcast_fusion), channel_id=1, source_target_pairs={{0,2},{2,0},{1,3},{3,1},{4,6},{6,4},{5,7},{7,5},{8,10},{10,8},{9,1... | collective-permute-start | bytes 737288 | tf_op jit(solution)/shard_map/ppermute | solution.py:249

commit v5 on v4

--- a/solution.py
+++ b/solution.py
@@ -19,6 +19,7 @@
 ROWS_OUT = 10
 HALF_ROWS = ROWS_OUT // 2
 LANES = 128
+CUT = 128
 VMEM_BYTES = 24 * 1024 * 1024
 GROUPS = 2 * WIDTH // LANES
 SCALE = 1.0 / math.sqrt(E)
@@ -63,6 +64,35 @@
         + [pltpu.SemaphoreType.DMA((4,))],
         compiler_params=pltpu.CompilerParams(vmem_limit_bytes=VMEM_BYTES),
     )(half.reshape(1), parts, wq, wk, wv)
+
+
+def ref_kernel(half_ref, p_ref, wk_ref, wv_ref, out_ref, rows_ref):
+    first = half_ref[0] == 0
+    blocks = []
+    for half in range(2):
+        for core in range(2):
+            own, other = p_ref[core, 0].astype(F32), p_ref[core, 1].astype(F32)
+            blocks.append(jnp.where(first, own, other) if half == 0 else jnp.where(first, other, own))
+    hidden = jnp.concatenate(blocks, axis=1).astype(BF16)
+    pair = jnp.concatenate([dot(hidden, wk_ref[...], 1, 1), dot(hidden, wv_ref[...], 1, 1)], axis=1)
+    rows_ref[...] = jnp.zeros_like(rows_ref)
+    for row in range(REF_ROWS):
+        for group in range(GROUPS):
+            at = row * GROUPS + group
+            rows_ref[at : at + 1, :] = pair[row : row + 1, LANES * group : LANES * (group + 1)]
+    out_ref[...] = jnp.broadcast_to(rows_ref[...].astype(BF16)[None], out_ref.shape)
+
+
+def ref_pair(half, parts, wk, wv):
+    vmem = pl.BlockSpec(memory_space=pltpu.VMEM)
+    return pl.pallas_call(
+        ref_kernel,
+        out_shape=jax.ShapeDtypeStruct((NYZ, 16, LANES), BF16),
+        in_specs=[pl.BlockSpec(memory_space=pltpu.SMEM)] + [vmem] * 3,
+        out_specs=vmem,
+        scratch_shapes=[pltpu.VMEM((16, LANES), F32)],
+        compiler_params=pltpu.CompilerParams(vmem_limit_bytes=12 * 1024 * 1024),
+    )(half.reshape(1), parts, wk, wv)
 
 
 def attention_kernel(
@@ -221,19 +251,17 @@
     core, half = lax.axis_index("c"), lax.axis_index("h")
     swap = [(0, 1), (1, 0)]
     wq, wk, wv = query_weight.T, key_weight.T, value_weight.T
-    own = tokens.T
-    other = lax.ppermute(own, "h", swap)
     start_col = (2 * half + core) * WIDTH
     source_cols = lax.dynamic_slice_in_dim(reference_image, start_col, WIDTH, 1)
     ref_cols = (source_cols.astype(F32) + dot(reference_image, ref_weight, 1, 0)).astype(BF16)
-    ref_hidden = lax.all_gather(ref_cols, TENSOR, axis=1, tiled=True)
-    pair = jnp.concatenate([dot(ref_hidden, wk, 1, 1), dot(ref_hidden, wv, 1, 1)], axis=1)
-    pair = pair.astype(BF16).reshape(1, REF_ROWS * GROUPS, LANES)
+    ref_cols = jnp.pad(ref_cols, ((0, 16 - REF_ROWS), (0, 0)))
+    ref_other = lax.ppermute(ref_cols, "h", swap)
+    own, _ = lax.optimization_barrier((tokens.T, ref_cols))
+    other = lax.ppermute(own, "h", swap)
+    ref_parts = lax.all_gather(jnp.stack([ref_cols, ref_other]), "c", axis=0, tiled=False)
+    pair = ref_pair(half, ref_parts, wk, wv)
     pair, other = lax.optimization_barrier((pair, other))
-    pair = jnp.pad(pair, ((0, 0), (0, 16 - REF_ROWS * GROUPS), (0, 0)))
-    pair = lax.all_to_all(
-        jnp.broadcast_to(pair, (NYZ, 16, LANES)), ("y", "z"), 0, 0, tiled=True
-    ).reshape(1, NYZ * 16, LANES)
+    pair = lax.all_to_all(pair, ("y", "z"), 0, 0, tiled=True).reshape(1, NYZ * 16, LANES)
     pair = lax.all_to_all(jnp.broadcast_to(pair, (NX, NYZ * 16, LANES)), "x", 0, 0, tiled=True)
     parts = lax.all_gather(jnp.stack([own, other]), "c", axis=0, tiled=False)
     tok, queries, keys, values = project(half, parts, wq, wk, wv)
@@ -242,14 +270,18 @@
     )
     pack = lax.all_to_all(pack, "x", 0, 0, tiled=True)
     kept, sent = token_parts(core, query_grads, key_grads, value_grads, wq, wk, wv)
-    got = lax.ppermute(sent, "c", swap)
-    paired = (kept.astype(F32) + got.astype(F32)).astype(BF16)
-    kept = lax.dynamic_index_in_dim(paired, half, 0, False)
-    sent = lax.dynamic_index_in_dim(paired, 1 - half, 0, False)
-    got = lax.ppermute(sent, "h", swap)
-    token_grads = (kept.astype(F32) + got.astype(F32)).astype(BF16).T
+    pieces = []
+    for low, high in ((0, CUT), (CUT, WIDTH)):
+        got = lax.ppermute(sent[:, low:high], "c", swap)
+        both = (kept[:, low:high].astype(F32) + got.astype(F32)).astype(BF16)
+        mine = lax.dynamic_index_in_dim(both, half, 0, False)
+        theirs = lax.dynamic_index_in_dim(both, 1 - half, 0, False)
+        got = lax.ppermute(theirs, "h", swap)
+        pieces.append((mine.astype(F32) + got.astype(F32)).astype(BF16))
+        if low == 0:
+            pack, _ = lax.optimization_barrier((pack, got))
+    token_grads = jnp.concatenate(pieces, axis=0).T
     pack = regroup(pack)
-    pack, _ = lax.optimization_barrier((pack, sent))
     pack = pack.reshape(NYZ, REF_ROWS + HALF_ROWS, 2 * WIDTH)
     pack = lax.all_to_all(pack, ("y", "z"), 0, 0, tiled=True)
     sums = jnp.sum(pack.astype(F32), axis=0)

time: 121 us -> 131 us (1.083)
  starting transfers between devices: 35.5 us -> 46.4 us
  blocking collectives: 35.1 us -> 29.6 us
  local copies, waits for them, and re-layouts: 5.53 us -> 9.43 us
  matrix products: 2.79 us -> 1.06 us
  waiting for transfers between devices: 18.4 us -> 19.8 us
    ppermute x2 -> x5, starting transfers between devices: 11.4 us -> 21.1 us  [the longest x2 12.9 us: per_device(): got = lax.ppermute(theirs, 'h', swap)]
    all_gather x1, blocking collectives: 9.94 us -> 5.21 us  [per_device(): lax.all_gather(jnp.stack([ref_cols, ref_other]), 'c', axis=0, tiled=False)]
    ppermute x2 -> x5, waiting for transfers between devices: 15.5 us -> 19.8 us  [the longest x2 13.2 us: per_device(): got = lax.ppermute(theirs, 'h', swap)]
    unnamed x23 -> x26, local copies, waits for them, and re-layouts: 3.83 us -> 6.73 us
    all_to_all x1, waiting for transfers between devices: 2.83 us -> 0.01 us  [per_device(): pack = lax.all_to_all(pack, 'x', 0, 0, tiled=True)]
    dot_general x3 -> x1, matrix products: 2.79 us -> 1.06 us  [dot(): lax.dot_general(a, b, (((a_dim,), (b_dim,)), ((), ())), preferred_element...]
  transfers between devices with their start and end apart: 6 -> 9, of which waited for: 3 -> 3; matrix products, arithmetic and copies ran while one was open for 5% -> 3% of each run, Pallas kernels for 4% -> 4%
where the time goes in v5:
time: 131 us; the launch traced here: 129 us
  starting transfers between devices  46.4 us (35%)
  blocking collectives  29.6 us (23%)
  waiting for transfers between devices  19.8 us (15%)
  Pallas kernels  18.1 us (14%)
  local copies, waits for them, and re-layouts  9.43 us (7%)
  other arithmetic  3.67 us (3%)
    all_to_all x1, blocking collectives, per_device(): lax.all_to_all(pair, ('y', 'z'), 0, 0, tiled=True)  20.1 us
    ppermute x2, waiting for transfers between devices, per_device(): got = lax.ppermute(theirs, 'h', swap)  13.2 us
    ppermute x2, starting transfers between devices, per_device(): got = lax.ppermute(theirs, 'h', swap)  12.9 us
    ppermute x1, starting transfers between devices, per_device(): other = lax.ppermute(own, 'h', swap)  11.5 us
    pallas_call x1, Pallas kernels, attention(): pl.pallas_call(attention_kernel, out_shape=(pltpu.HBM((WIDTH, P_SIZE), BF...  10.7 us
    unnamed x26, local copies, waits for them, and re-layouts  6.73 us
    ppermute x1, waiting for transfers between devices, per_device(): ref_other = lax.ppermute(ref_cols, 'h', swap)  6.52 us
    ppermute x2, starting transfers between devices, per_device(): got = lax.ppermute(sent[:, low:high], 'c', swap)  6.24 us
  transfers between devices with their start and end apart: 9, of which 3 were waited for; matrix products, arithmetic and copies ran while one was open for 3% of the time, Pallas kernels for 4%

profile of v5, /device:TPU:1, one launch (start us, length us, event | category | flops | bytes accessed | tf_op | source)
XLA Modules:
  0.0 129.0 jit_solution(7480409455939722882)
XLA Ops:
  0.6 0.0 copy-start
  0.6 0.0 copy-start.1
  0.7 1.1 copy-done
  1.8 1.1 fusion
  2.9 11.5 %collective-permute-start.1 = (bf16[320,384]{1,0:T(8,128)(2,1)}, bf16[320,384]{1,0:T(8,128)(2,1)}, u32[]{:S(2)}, u32[]{:S(2)}) collective-permute-start(bf16[320,384]{1,0:T(8,128)(2,1)} %bitcast.44), channel_id=1, source_target_pairs={{0,2},{2,0},{1,3},{3,1},{4,6},{6,4},{5,7},{7,5},{8,10},{10,8},{9,1... | collective-permute-start | bytes 737288 | tf_op jit(solution)/shard_map/ppermute | solution.py:260
  14.4 1.9 %collective-permute-start = (bf16[16,320]{1,0:T(8,128)(2,1)S(1)}, bf16[16,320]{1,0:T(8,128)(2,1)S(1)}, u32[]{:S(2)}, u32[]{:S(2)}) collective-permute-start(bf16[16,320]{1,0:T(8,128)(2,1)S(1)} %get-tuple-element.42), channel_id=1, source_target_pairs={{0,2},{2,0},{1,3},{3,1},{4,6},{6,4},{5,7},{7,5},{8,10},{10,8},{9,1... | collective-permute-start | bytes 30728 | tf_op jit(solution)/shard_map/ppermute | solution.py:258
  16.3 6.5 %collective-permute-done = bf16[16,320]{1,0:T(8,128)(2,1)S(1)} collective-permute-done((bf16[16,320]{1,0:T(8,128)(2,1)S(1)}, bf16[16,320]{1,0:T(8,128)(2,1)S(1)}, u32[]{:S(2)}, u32[]{:S(2)}) %collective-permute-start) | collective-permute-done | bytes 10272 | tf_op jit(solution)/shard_map/ppermute | solution.py:258
  22.8 5.2 %all-gather = bf16[4,16,320]{2,1,0:T(8,128)(2,1)S(1)} all-gather(bf16[2,16,320]{2,1,0:T(8,128)(2,1)S(1)} %pad_maximum_fusion.1), channel_id=2, replica_groups=mesh['x'=4,'y'=8,'z'=4,'h'=2,'c'=2] {'c'}, dimensions={0}, use_global_device_ids=true | all-gather | bytes 61440 | tf_op jit(solution)/shard_map/all_gather | solution.py:261
  28.0 0.0 copy-done.1
  28.0 0.0 copy-start.2
  28.0 1.1 copy-done.2
  29.2 0.7 shard_map.110
  29.8 0.0 copy-start.12
  29.9 0.0 collective-permute-done.1
  29.9 20.1 %all_to_all.20 = bf16[32,16,128]{2,1,0:T(8,128)(2,1)S(1)} all-to-all(bf16[32,16,128]{2,1,0:T(8,128)(2,1)S(1)} %shard_map.110), channel_id=1, replica_groups=mesh['x'=4,'y'=8,'z'=4,'h'=2,'c'=2] {'y','z'}, dimensions={0} | all-to-all | bytes 262144 | tf_op jit(solution)/shard_map/all_to_all | solution.py:264
  50.0 0.9 broadcast_in_dim.8
  50.8 4.1 %all-to-all-start.1 = ((bf16[4,512,128]{2,1,0:T(8,128)(2,1)}), bf16[4,512,128]{2,1,0:T(8,128)(2,1)}, u32[]{:S(2)}, u32[]{:S(2)}) async-start(bf16[4,512,128]{2,1,0:T(8,128)(2,1)} %broadcast_in_dim.8), calls=%async_computation.1 | async-start | bytes 1048576 | tf_op jit(solution)/shard_map/all_to_all | solution.py:265
  55.0 0.0 copy-start.3
  55.0 0.0 copy-start.4
  55.0 0.0 copy-done.12
  55.0 1.1 pad_maximum_fusion
  56.2 4.3 %all-gather.1 = bf16[4,320,384]{2,1,0:T(8,128)(2,1)S(1)} all-gather(bf16[2,320,384]{2,1,0:T(8,128)(2,1)S(1)} %pad_maximum_fusion), channel_id=3, replica_groups=mesh['x'=4,'y'=8,'z'=4,'h'=2,'c'=2] {'c'}, dimensions={0}, use_global_device_ids=true | all-gather | bytes 1474560 | tf_op jit(solution)/shard_map/all_gather | solution.py:266
  60.5 0.0 copy-done.3
  60.5 0.0 copy-done.4
  60.5 0.0 copy-start.11
  60.5 2.6 %shard_map.111 = (bf16[1280,384]{1,0:T(8,128)(2,1)}, bf16[384,320]{1,0:T(8,128)(2,1)}, bf16[384,320]{1,0:T(8,128)(2,1)}, bf16[384,320]{1,0:T(8,128)(2,1)}) custom-call(s32[1]{0:T(128)} %bitcast.half_ref, bf16[2,2,320,384]{3,2,1,0:T(8,128)(2,1)S(1)} %bitcast.38, bf16[320,1280]{1,0:T(8,128)(2,1)S(1)} %bitcast.39, bf16[320,1280]{1,0:T(8,128)(2,1)S(1)} %bitcast.33, ...), custom_call_target="tpu_custom_call" | custom-call | tf_op jit(solution)/shard_map/pallas_call | solution.py:56
  63.2 0.0 all-to-all-done.1
  63.2 0.0 copy-done.11
  63.2 10.7 %shard_map.112 = (bf16[320,384]{1,0:T(8,128)(2,1)}, bf16[384,320]{1,0:T(8,128)(2,1)}, bf16[384,320]{1,0:T(8,128)(2,1)}, bf16[384,320]{1,0:T(8,128)(2,1)}, bf16[4,256,640]{2,1,0:T(8,128)(2,1)}) custom-call(bf16[384,320]{1,0:T(8,128)(2,1)} %get-tuple-element.22.q_in, bf16[384,320]{1,0:T(8,128)(2,1)} %get-tuple-element.23.k_in, ...), custom_call_target="tpu_custom_call" | custom-call | tf_op jit(solution)/shard_map/pallas_call | solution.py:173
  73.9 4.5 %all-to-all-start.2 = ((bf16[4,256,640]{2,1,0:T(8,128)(2,1)}), bf16[4,256,640]{2,1,0:T(8,128)(2,1)}, u32[]{:S(2)}, u32[]{:S(2)}) async-start(bf16[4,256,640]{2,1,0:T(8,128)(2,1)} %get-tuple-element.33), calls=%async_computation.2 | async-start | bytes 2621440 | tf_op jit(solution)/shard_map/all_to_all | solution.py:271
  78.4 0.0 copy-start.8
  78.4 1.0 copy-done.8
  79.3 0.0 copy-start.9
  79.3 1.0 copy-done.9
  80.3 0.0 copy-start.10
  80.3 1.0 copy-done.10
  81.3 1.8 %shard_map.113 = (bf16[2,320,384]{2,1,0:T(8,128)(2,1)S(1)}, bf16[2,320,384]{2,1,0:T(8,128)(2,1)S(1)}) custom-call(s32[1]{0:T(128)} %bitcast.15.core_ref, bf16[384,320]{1,0:T(8,128)(2,1)S(1)} %copy-done.8, bf16[384,320]{1,0:T(8,128)(2,1)S(1)} %copy-done.9, bf16[384,320]{1,0:T(8,128)(2,1)S(1)} %copy-done.10, bf16[320,1280]{1,0:T(8,128)(2,1)S(1)} %bitcast.40, ...), custom_call_target="tpu_custom_call" | custom-call | tf_op jit(solution)/shard_map/pallas_call | solution.py:214
  83.0 0.0 copy-start.5
  83.0 0.8 copy-done.5
  83.8 0.0 copy-start.7
  83.8 0.8 copy-done.7
  84.6 0.0 copy-start.6
  84.6 4.3 %collective-permute-start.2 = (bf16[2,128,384]{2,1,0:T(8,128)(2,1)S(1)}, bf16[2,128,384]{2,1,0:T(8,128)(2,1)S(1)}, u32[]{:S(2)}, u32[]{:S(2)}) collective-permute-start(bf16[2,128,384]{2,1,0:T(8,128)(2,1)S(1)} %slice.39), channel_id=1, source_target_pairs={{0,1},{1,0},{2,3},{3,2},{4,5},{5,4},{6,7},{7,6},{8,9},{9,8},{10,11... | collective-permute-start | bytes 589832 | tf_op jit(solution)/shard_map/ppermute | solution.py:275
  88.9 1.0 slice.41
  89.9 1.9 %collective-permute-start.4 = (bf16[2,192,384]{2,1,0:T(8,128)(2,1)S(1)}, bf16[2,192,384]{2,1,0:T(8,128)(2,1)S(1)}, u32[]{:S(2)}, u32[]{:S(2)}) collective-permute-start(bf16[2,192,384]{2,1,0:T(8,128)(2,1)S(1)} %slice.41), channel_id=1, source_target_pairs={{0,1},{1,0},{2,3},{3,2},{4,5},{5,4},{6,7},{7,6},{8,9},{9,8},{10,11... | collective-permute-start | bytes 884744 | tf_op jit(solution)/shard_map/ppermute | solution.py:275
  91.9 0.0 collective-permute-done.2
  91.9 1.0 add_convert_fusion.1
  92.9 6.5 %collective-permute-start.3 = (bf16[128,384]{1,0:T(8,128)(2,1)S(1)}, bf16[128,384]{1,0:T(8,128)(2,1)S(1)}, u32[]{:S(2)}, u32[]{:S(2)}) collective-permute-start(bf16[128,384]{1,0:T(8,128)(2,1)S(1)} %dynamic-slice_bitcast_fusion.1), channel_id=1, source_target_pairs={{0,2},{2,0},{1,3},{3,1},{4,6},{6,4},{5,7},{7,5},{8,10},{10,8},{9,1... | collective-permute-start | bytes 294920 | tf_op jit(solution)/shard_map/ppermute | solution.py:279
  99.5 0.0 collective-permute-done.4
  99.5 0.0 copy-done.6
  99.5 0.1 add_convert_fusion
  99.6 3.0 %collective-permute-done.3 = bf16[128,384]{1,0:T(8,128)(2,1)S(1)} collective-permute-done((bf16[128,384]{1,0:T(8,128)(2,1)S(1)}, bf16[128,384]{1,0:T(8,128)(2,1)S(1)}, u32[]{:S(2)}, u32[]{:S(2)}) %collective-permute-start.3) | collective-permute-done | bytes 98336 | tf_op jit(solution)/shard_map/ppermute | solution.py:279
  102.6 0.0 all-to-all-done.2.in_ref
  102.6 2.3 %shard_map.114 = bf16[256,640]{1,0:T(8,128)(2,1)} custom-call(bf16[4,256,640]{2,1,0:T(8,128)(2,1)} %all-to-all-done.2.in_ref), custom_call_target="tpu_custom_call" | custom-call | tf_op jit(solution)/shard_map/pallas_call | solution.py:240
  104.9 5.1 %all-to-all-start.3 = ((bf16[32,8,640]{2,1,0:T(8,128)(2,1)}), bf16[32,8,640]{2,1,0:T(8,128)(2,1)S(1)}, u32[]{:S(2)}, u32[]{:S(2)}) async-start(bf16[32,8,640]{2,1,0:T(8,128)(2,1)} %bitcast.21), calls=%async_computation.3 | async-start | bytes 655360 | tf_op jit(solution)/shard_map/all_to_all | solution.py:286
  110.1 6.4 %collective-permute-start.5 = (bf16[192,384]{1,0:T(8,128)(2,1)S(1)}, bf16[192,384]{1,0:T(8,128)(2,1)S(1)}, u32[]{:S(2)}, u32[]{:S(2)}) collective-permute-start(bf16[192,384]{1,0:T(8,128)(2,1)S(1)} %dynamic-slice_bitcast_fusion), channel_id=1, source_target_pairs={{0,2},{2,0},{1,3},{3,1},{4,6},{6,4},{5,7},{7,5},{8,10},{10,8},{9,1... | collective-permute-start | bytes 442376 | tf_op jit(solution)/shard_map/ppermute | solution.py:279
  116.5 10.2 %collective-permute-done.5 = bf16[192,384]{1,0:T(8,128)(2,1)S(1)} collective-permute-done((bf16[192,384]{1,0:T(8,128)(2,1)S(1)}, bf16[192,384]{1,0:T(8,128)(2,1)S(1)}, u32[]{:S(2)}, u32[]{:S(2)}) %collective-permute-start.5) | collective-permute-done | bytes 147488 | tf_op jit(solution)/shard_map/ppermute | solution.py:279
  126.8 0.7 maximum_bitcast_fusion
  127.5 0.0 all-to-all-done.3
  127.5 0.1 convert_reduce_fusion
  127.6 0.1 fusion.4
  127.7 0.7 fusion.5
  128.4 0.6 maximum_maximum_fusion
  (9 shorter events, 0.2 us)
Async XLA Ops:
  0.6 1.2 copy-start
  0.6 27.4 %copy-start.1 = (bf16[1280,320]{0,1:T(8,128)(2,1)S(1)}, bf16[1280,320]{0,1:T(8,128)(2,1)}, u32[]{:S(2)}) copy-start(bf16[1280,320]{0,1:T(8,128)(2,1)} %param.10) | copy-start | bytes 2457604
  2.9 27.0 %collective-permute-start.1 = (bf16[320,384]{1,0:T(8,128)(2,1)}, bf16[320,384]{1,0:T(8,128)(2,1)}, u32[]{:S(2)}, u32[]{:S(2)}) collective-permute-start(bf16[320,384]{1,0:T(8,128)(2,1)} %bitcast.44), channel_id=1, source_target_pairs={{0,2},{2,0},{1,3},{3,1},{4,6},{6,4},{5,7},{7,5},{8,10},{10,8},{9,1... | collective-permute-start | bytes 737288 | tf_op jit(solution)/shard_map/ppermute | solution.py:260
  14.4 8.4 %collective-permute-start = (bf16[16,320]{1,0:T(8,128)(2,1)S(1)}, bf16[16,320]{1,0:T(8,128)(2,1)S(1)}, u32[]{:S(2)}, u32[]{:S(2)}) collective-permute-start(bf16[16,320]{1,0:T(8,128)(2,1)S(1)} %get-tuple-element.42), channel_id=1, source_target_pairs={{0,2},{2,0},{1,3},{3,1},{4,6},{6,4},{5,7},{7,5},{8,10},{10,8},{9,1... | collective-permute-start | bytes 30728 | tf_op jit(solution)/shard_map/ppermute | solution.py:258
  28.0 1.1 copy-start.2
  29.8 25.2 %copy-start.12 = (bf16[384,320]{0,1:T(8,128)(2,1)S(1)}, bf16[384,320]{0,1:T(8,128)(2,1)}, u32[]{:S(2)}) copy-start(bf16[384,320]{0,1:T(8,128)(2,1)} %param.7) | copy-start | bytes 737284
  50.8 12.3 %all-to-all-start.1 = ((bf16[4,512,128]{2,1,0:T(8,128)(2,1)}), bf16[4,512,128]{2,1,0:T(8,128)(2,1)}, u32[]{:S(2)}, u32[]{:S(2)}) async-start(bf16[4,512,128]{2,1,0:T(8,128)(2,1)} %broadcast_in_dim.8), calls=%async_computation.1 | async-start | bytes 1048576 | tf_op jit(solution)/shard_map/all_to_all | solution.py:265
  55.0 5.5 %copy-start.3 = (bf16[1280,320]{0,1:T(8,128)(2,1)S(1)}, bf16[1280,320]{0,1:T(8,128)(2,1)}, u32[]{:S(2)}) copy-start(bf16[1280,320]{0,1:T(8,128)(2,1)} %param.11) | copy-start | bytes 2457604
  55.0 5.5 %copy-start.4 = (bf16[1280,320]{0,1:T(8,128)(2,1)S(1)}, bf16[1280,320]{0,1:T(8,128)(2,1)}, u32[]{:S(2)}) copy-start(bf16[1280,320]{0,1:T(8,128)(2,1)} %param.9) | copy-start | bytes 2457604
  60.5 2.7 %copy-start.11 = (bf16[384,320]{0,1:T(8,128)(2,1)S(1)}, bf16[384,320]{0,1:T(8,128)(2,1)}, u32[]{:S(2)}) copy-start(bf16[384,320]{0,1:T(8,128)(2,1)} %param.13) | copy-start | bytes 737284
  73.9 28.7 %all-to-all-start.2 = ((bf16[4,256,640]{2,1,0:T(8,128)(2,1)}), bf16[4,256,640]{2,1,0:T(8,128)(2,1)}, u32[]{:S(2)}, u32[]{:S(2)}) async-start(bf16[4,256,640]{2,1,0:T(8,128)(2,1)} %get-tuple-element.33), calls=%async_computation.2 | async-start | bytes 2621440 | tf_op jit(solution)/shard_map/all_to_all | solution.py:271
  78.4 1.0 copy-start.8
  79.3 1.0 copy-start.9
  80.3 1.0 copy-start.10
  83.0 0.8 copy-start.5
  83.8 0.8 copy-start.7
  84.6 14.9 %copy-start.6 = (bf16[2,320,384]{2,1,0:T(8,128)(2,1)S(1)}, bf16[2,320,384]{2,1,0:T(8,128)(2,1)}, u32[]{:S(2)}) copy-start(bf16[2,320,384]{2,1,0:T(8,128)(2,1)} %copy-done.5) | copy-start | bytes 1474564
  84.6 7.3 %collective-permute-start.2 = (bf16[2,128,384]{2,1,0:T(8,128)(2,1)S(1)}, bf16[2,128,384]{2,1,0:T(8,128)(2,1)S(1)}, u32[]{:S(2)}, u32[]{:S(2)}) collective-permute-start(bf16[2,128,384]{2,1,0:T(8,128)(2,1)S(1)} %slice.39), channel_id=1, source_target_pairs={{0,1},{1,0},{2,3},{3,2},{4,5},{5,4},{6,7},{7,6},{8,9},{9,8},{10,11... | collective-permute-start | bytes 589832 | tf_op jit(solution)/shard_map/ppermute | solution.py:275
  89.9 9.5 %collective-permute-start.4 = (bf16[2,192,384]{2,1,0:T(8,128)(2,1)S(1)}, bf16[2,192,384]{2,1,0:T(8,128)(2,1)S(1)}, u32[]{:S(2)}, u32[]{:S(2)}) collective-permute-start(bf16[2,192,384]{2,1,0:T(8,128)(2,1)S(1)} %slice.41), channel_id=1, source_target_pairs={{0,1},{1,0},{2,3},{3,2},{4,5},{5,4},{6,7},{7,6},{8,9},{9,8},{10,11... | collective-permute-start | bytes 884744 | tf_op jit(solution)/shard_map/ppermute | solution.py:275
  92.9 9.7 %collective-permute-start.3 = (bf16[128,384]{1,0:T(8,128)(2,1)S(1)}, bf16[128,384]{1,0:T(8,128)(2,1)S(1)}, u32[]{:S(2)}, u32[]{:S(2)}) collective-permute-start(bf16[128,384]{1,0:T(8,128)(2,1)S(1)} %dynamic-slice_bitcast_fusion.1), channel_id=1, source_target_pairs={{0,2},{2,0},{1,3},{3,1},{4,6},{6,4},{5,7},{7,5},{8,10},{10,8},{9,1... | collective-permute-start | bytes 294920 | tf_op jit(solution)/shard_map/ppermute | solution.py:279
  104.9 22.6 %all-to-all-start.3 = ((bf16[32,8,640]{2,1,0:T(8,128)(2,1)}), bf16[32,8,640]{2,1,0:T(8,128)(2,1)S(1)}, u32[]{:S(2)}, u32[]{:S(2)}) async-start(bf16[32,8,640]{2,1,0:T(8,128)(2,1)} %bitcast.21), calls=%async_computation.3 | async-start | bytes 655360 | tf_op jit(solution)/shard_map/all_to_all | solution.py:286
  110.1 16.7 %collective-permute-start.5 = (bf16[192,384]{1,0:T(8,128)(2,1)S(1)}, bf16[192,384]{1,0:T(8,128)(2,1)S(1)}, u32[]{:S(2)}, u32[]{:S(2)}) collective-permute-start(bf16[192,384]{1,0:T(8,128)(2,1)S(1)} %dynamic-slice_bitcast_fusion), channel_id=1, source_target_pairs={{0,2},{2,0},{1,3},{3,1},{4,6},{6,4},{5,7},{7,5},{8,10},{10,8},{9,1... | collective-permute-start | bytes 442376 | tf_op jit(solution)/shard_map/ppermute | solution.py:279

commit v6 on v4

--- a/solution.py
+++ b/solution.py
@@ -19,6 +19,7 @@
 ROWS_OUT = 10
 HALF_ROWS = ROWS_OUT // 2
 LANES = 128
+REGROUP_COST = 10**10
 VMEM_BYTES = 24 * 1024 * 1024
 GROUPS = 2 * WIDTH // LANES
 SCALE = 1.0 / math.sqrt(E)
@@ -31,16 +32,12 @@
 
 
 def project_kernel(
-    half_ref, t_ref, wq_ref, wk_ref, wv_ref, tok_out, q_out, k_out, v_out,
-    tok_ref, q_ref, k_ref, v_ref, sem,
+    g_ref, wq_ref, wk_ref, wv_ref, tok_out, q_out, k_out, v_out, tok_ref, q_ref, k_ref, v_ref, sem
 ):
-    half = half_ref[0]
     pairs = ((tok_ref, tok_out), (q_ref, q_out), (k_ref, k_out), (v_ref, v_out))
     copies = [pltpu.make_async_copy(a, b, sem.at[i]) for i, (a, b) in enumerate(pairs)]
-    for core in range(2):
-        for slot in range(2):
-            at = pl.multiple_of((2 * lax.rem(half + slot, 2) + core) * WIDTH, E)
-            tok_ref[pl.ds(at, WIDTH), :] = t_ref[core, slot]
+    for t in range(4):
+        tok_ref[t * WIDTH : (t + 1) * WIDTH, :] = g_ref[t, :WIDTH, :]
     copies[0].start()
     tok = tok_ref[...]
     for i, (w_ref, out_ref) in enumerate(((wq_ref, q_ref), (wk_ref, k_ref), (wv_ref, v_ref))):
@@ -50,19 +47,38 @@
         copy.wait()
 
 
-def project(half, parts, wq, wk, wv):
-    vmem = pl.BlockSpec(memory_space=pltpu.VMEM)
+def project(gathered, wq, wk, wv):
     return pl.pallas_call(
         project_kernel,
         out_shape=(pltpu.HBM((4 * WIDTH, P_SIZE), BF16),)
         + (pltpu.HBM((P_SIZE, WIDTH), BF16),) * 3,
-        in_specs=[pl.BlockSpec(memory_space=pltpu.SMEM)] + [vmem] * 4,
         out_specs=[pl.BlockSpec(memory_space=pltpu.HBM)] * 4,
         scratch_shapes=[pltpu.VMEM((4 * WIDTH, P_SIZE), BF16)]
         + [pltpu.VMEM((P_SIZE, WIDTH), BF16)] * 3
         + [pltpu.SemaphoreType.DMA((4,))],
         compiler_params=pltpu.CompilerParams(vmem_limit_bytes=VMEM_BYTES),
-    )(half.reshape(1), parts, wq, wk, wv)
+    )(gathered, wq, wk, wv)
+
+
+def ref_kernel(g_ref, wk_ref, wv_ref, out_ref, rows_ref):
+    hidden = [g_ref[t, WIDTH : WIDTH + 16, :WIDTH].astype(F32) for t in range(4)]
+    hidden = jnp.concatenate(hidden, axis=1).astype(BF16)
+    pair = jnp.concatenate([dot(hidden, wk_ref[...], 1, 1), dot(hidden, wv_ref[...], 1, 1)], axis=1)
+    rows_ref[...] = jnp.zeros_like(rows_ref)
+    for row in range(REF_ROWS):
+        for group in range(GROUPS):
+            at = row * GROUPS + group
+            rows_ref[at : at + 1, :] = pair[row : row + 1, LANES * group : LANES * (group + 1)]
+    out_ref[...] = jnp.broadcast_to(rows_ref[...].astype(BF16)[None], out_ref.shape)
+
+
+def ref_pair(gathered, wk, wv):
+    return pl.pallas_call(
+        ref_kernel,
+        out_shape=jax.ShapeDtypeStruct((NYZ, 16, LANES), BF16),
+        scratch_shapes=[pltpu.VMEM((16, LANES), F32)],
+        compiler_params=pltpu.CompilerParams(vmem_limit_bytes=12 * 1024 * 1024),
+    )(gathered, wk, wv)
 
 
 def attention_kernel(
@@ -167,27 +183,53 @@
     )(*[pltpu.with_memory_space_constraint(a, pltpu.HBM) for a in (q, k, v, pair, tok)], gt)
 
 
-def token_kernel(core_ref, dq_ref, dk_ref, dv_ref, wq_ref, wk_ref, wv_ref, kept_ref, sent_ref):
+def token_kernel(
+    core_ref, dq_in, dk_in, dv_in, wq_ref, wk_ref, wv_ref, kept_out, sent_out,
+    dq_ref, dk_ref, dv_ref, kept_ref, sent_ref, in_sem, out_sem,
+):
+    pairs = ((dq_in, dq_ref), (dk_in, dk_ref), (dv_in, dv_ref))
+    loads = [pltpu.make_async_copy(a, b, in_sem.at[i]) for i, (a, b) in enumerate(pairs)]
+    for load in loads:
+        load.start()
     core = core_ref[0]
-    total = dot(dq_ref[...], wq_ref[...], 1, 0)
-    total = total + dot(dk_ref[...], wk_ref[...], 1, 0)
-    total = total + dot(dv_ref[...], wv_ref[...], 1, 0)
+    total = None
+    for load, (d_ref, w_ref) in zip(
+        loads, ((dq_ref, wq_ref), (dk_ref, wk_ref), (dv_ref, wv_ref))
+    ):
+        load.wait()
+        part = dot(d_ref[...], w_ref[...], 1, 0)
+        total = part if total is None else total + part
     total = total.T.astype(BF16)
+    stores = []
     for half in range(2):
         zero, one = [total[(2 * half + c) * WIDTH : (2 * half + c + 1) * WIDTH] for c in range(2)]
+        sent_ref[half] = jnp.where(core == 0, one, zero)
         kept_ref[half] = jnp.where(core == 0, zero, one)
-        sent_ref[half] = jnp.where(core == 0, one, zero)
+        for i, (a, b) in enumerate(((sent_ref, sent_out), (kept_ref, kept_out))):
+            store = pltpu.make_async_copy(a.at[half], b.at[half], out_sem.at[2 * half + i])
+            store.start()
+            stores.append(store)
+    for store in stores:
+        store.wait()
 
 
 def token_parts(core, dq, dk, dv, wq, wk, wv):
-    vmem = pl.BlockSpec(memory_space=pltpu.VMEM)
+    hbm, vmem = [pl.BlockSpec(memory_space=space) for space in (pltpu.HBM, pltpu.VMEM)]
     return pl.pallas_call(
         token_kernel,
-        out_shape=(jax.ShapeDtypeStruct((2, WIDTH, P_SIZE), BF16),) * 2,
-        in_specs=[pl.BlockSpec(memory_space=pltpu.SMEM)] + [vmem] * 6,
-        out_specs=[vmem] * 2,
+        out_shape=(pltpu.HBM((2, WIDTH, P_SIZE), BF16),) * 2,
+        in_specs=[pl.BlockSpec(memory_space=pltpu.SMEM)] + [hbm] * 3 + [vmem] * 3,
+        out_specs=[hbm] * 2,
+        scratch_shapes=[pltpu.VMEM((P_SIZE, WIDTH), BF16)] * 3
+        + [pltpu.VMEM((2, WIDTH, P_SIZE), BF16)] * 2
+        + [pltpu.SemaphoreType.DMA((3,)), pltpu.SemaphoreType.DMA((4,))],
+        cost_estimate=pl.CostEstimate(flops=1, bytes_accessed=1, transcendentals=0),
         compiler_params=pltpu.CompilerParams(vmem_limit_bytes=VMEM_BYTES),
-    )(core.reshape(1), dq, dk, dv, wq, wk, wv)
+    )(
+        core.reshape(1),
+        *[pltpu.with_memory_space_constraint(a, pltpu.HBM) for a in (dq, dk, dv)],
+        wq, wk, wv,
+    )
 
 
 def regroup_kernel(in_ref, out_ref, held_ref):
@@ -211,6 +253,34 @@
         regroup_kernel,
         out_shape=jax.ShapeDtypeStruct((NYZ * rows, 2 * WIDTH), BF16),
         scratch_shapes=[pltpu.VMEM((GROUPS, NYZ * rows, LANES), F32)],
+        cost_estimate=pl.CostEstimate(
+            flops=REGROUP_COST, bytes_accessed=REGROUP_COST, transcendentals=0
+        ),
+        compiler_params=pltpu.CompilerParams(vmem_limit_bytes=8 * 1024 * 1024),
+    )(parts)
+
+
+def finish_kernel(in_ref, grad_ref, key_ref, value_ref):
+    total = in_ref[0].astype(F32)
+    for j in range(1, NYZ):
+        total = total + in_ref[j].astype(F32)
+    key_ref[...] = total[:REF_ROWS, :WIDTH].astype(BF16)
+    value_ref[...] = total[:REF_ROWS, WIDTH:].astype(BF16)
+    low, tail = total[:, : 4 * LANES], total[:, 4 * LANES :]
+    left = jnp.concatenate([low[:, : 2 * LANES], tail[:, :E]], axis=1)
+    right = jnp.concatenate([low[:, 2 * LANES :], tail[:, E:]], axis=1)
+    grad_ref[:HALF_ROWS, :] = left[REF_ROWS:]
+    grad_ref[HALF_ROWS:, :] = right[REF_ROWS:]
+
+
+def finish(parts):
+    return pl.pallas_call(
+        finish_kernel,
+        out_shape=(
+            jax.ShapeDtypeStruct((ROWS_OUT, WIDTH), F32),
+            jax.ShapeDtypeStruct((REF_ROWS, WIDTH), BF16),
+            jax.ShapeDtypeStruct((REF_ROWS, WIDTH), BF16),
+        ),
         compiler_params=pltpu.CompilerParams(vmem_limit_bytes=8 * 1024 * 1024),
     )(parts)
 
@@ -221,22 +291,17 @@
     core, half = lax.axis_index("c"), lax.axis_index("h")
     swap = [(0, 1), (1, 0)]
     wq, wk, wv = query_weight.T, key_weight.T, value_weight.T
-    own = tokens.T
-    other = lax.ppermute(own, "h", swap)
     start_col = (2 * half + core) * WIDTH
     source_cols = lax.dynamic_slice_in_dim(reference_image, start_col, WIDTH, 1)
     ref_cols = (source_cols.astype(F32) + dot(reference_image, ref_weight, 1, 0)).astype(BF16)
-    ref_hidden = lax.all_gather(ref_cols, TENSOR, axis=1, tiled=True)
-    pair = jnp.concatenate([dot(ref_hidden, wk, 1, 1), dot(ref_hidden, wv, 1, 1)], axis=1)
-    pair = pair.astype(BF16).reshape(1, REF_ROWS * GROUPS, LANES)
-    pair, other = lax.optimization_barrier((pair, other))
-    pair = jnp.pad(pair, ((0, 0), (0, 16 - REF_ROWS * GROUPS), (0, 0)))
-    pair = lax.all_to_all(
-        jnp.broadcast_to(pair, (NYZ, 16, LANES)), ("y", "z"), 0, 0, tiled=True
-    ).reshape(1, NYZ * 16, LANES)
+    ref_block = jnp.pad(ref_cols, ((0, 16 - REF_ROWS), (0, P_SIZE - WIDTH)))
+    gathered = lax.all_gather(
+        jnp.concatenate([tokens.T, ref_block], axis=0), TENSOR, axis=0, tiled=False
+    )
+    pair = ref_pair(gathered, wk, wv)
+    pair = lax.all_to_all(pair, ("y", "z"), 0, 0, tiled=True).reshape(1, NYZ * 16, LANES)
     pair = lax.all_to_all(jnp.broadcast_to(pair, (NX, NYZ * 16, LANES)), "x", 0, 0, tiled=True)
-    parts = lax.all_gather(jnp.stack([own, other]), "c", axis=0, tiled=False)
-    tok, queries, keys, values = project(half, parts, wq, wk, wv)
+    tok, queries, keys, values = project(gathered, wq, wk, wv)
     attended, query_grads, key_grads, value_grads, pack = attention(
         queries, keys, values, pair.reshape(NX * NYZ * 16, LANES), cotangent.T, tok
     )
@@ -249,20 +314,11 @@
     got = lax.ppermute(sent, "h", swap)
     token_grads = (kept.astype(F32) + got.astype(F32)).astype(BF16).T
     pack = regroup(pack)
-    pack, _ = lax.optimization_barrier((pack, sent))
+    pack, _ = lax.optimization_barrier((pack, got))
     pack = pack.reshape(NYZ, REF_ROWS + HALF_ROWS, 2 * WIDTH)
     pack = lax.all_to_all(pack, ("y", "z"), 0, 0, tiled=True)
-    sums = jnp.sum(pack.astype(F32), axis=0)
-    low, tail = sums[REF_ROWS:, : 4 * LANES], sums[REF_ROWS:, 4 * LANES :]
-    left = jnp.concatenate([low[:, : 2 * LANES], tail[:, :E]], axis=1)
-    right = jnp.concatenate([low[:, 2 * LANES :], tail[:, E:]], axis=1)
-    return (
-        attended.T,
-        token_grads,
-        jnp.concatenate([left, right], axis=0),
-        sums[:REF_ROWS, :WIDTH].astype(BF16),
-        sums[:REF_ROWS, WIDTH:].astype(BF16),
-    )
+    query_weight_grad, ref_key_grads, ref_value_grads = finish(pack)
+    return attended.T, token_grads, query_weight_grad, ref_key_grads, ref_value_grads
 
 
 def solution(mesh):

time: 121 us -> 126 us (1.041)
  the two profiles are of different devices: /device:TPU:1 before, /device:TPU:2 now
where the time goes in v6:
time: 126 us; the launch traced here: 125 us
  blocking collectives  44 us (35%)
  waiting for transfers between devices  28.5 us (23%)
  starting transfers between devices  23 us (18%)
  Pallas kernels  20.9 us (17%)
  local copies, waits for them, and re-layouts  4.13 us (3%)
  other arithmetic  2.91 us (2%)
    all_to_all x1, blocking collectives, per_device(): lax.all_to_all(pair, ('y', 'z'), 0, 0, tiled=True)  26.4 us
    all_gather x1, blocking collectives, per_device(): lax.all_gather(jnp.concatenate([tokens.T, ref_block], axis=0), TENSOR, ax...  17.6 us
    all_to_all x1, waiting for transfers between devices, per_device(): pack = lax.all_to_all(pack, ('y', 'z'), 0, 0, tiled=True)  13 us
    pallas_call x1, Pallas kernels, attention(): pl.pallas_call(attention_kernel, out_shape=(pltpu.HBM((WIDTH, P_SIZE), BF...  10.7 us
    ppermute x1, waiting for transfers between devices, per_device(): got = lax.ppermute(sent, 'h', swap)  10.2 us
    ppermute x1, starting transfers between devices, per_device(): got = lax.ppermute(sent, 'h', swap)  6.56 us
    all_to_all x1, starting transfers between devices, per_device(): pack = lax.all_to_all(pack, 'x', 0, 0, tiled=True)  5.86 us
    all_to_all x1, starting transfers between devices, per_device(): lax.all_to_all(jnp.broadcast_to(pair, (NX, NYZ * 16, LANES)), 'x', 0, 0,...  4.82 us
  transfers between devices with their start and end apart: 5, of which 4 were waited for; matrix products, arithmetic and copies ran while one was open for 2% of the time, Pallas kernels for 7%

profile of v6, /device:TPU:2, one launch (start us, length us, event | category | flops | bytes accessed | tf_op | source)
XLA Modules:
  0.0 125.3 jit_solution(14542232861610666258)
XLA Ops:
  0.6 0.0 copy-start
  0.7 1.1 copy-done
  1.8 0.0 copy-start.1
  1.8 0.0 copy-start.2
  1.8 1.1 fusion
  2.9 1.0 fusion.3
  3.9 17.6 %all-gather = bf16[1344,384]{1,0:T(8,128)(2,1)S(1)} all-gather(bf16[336,384]{1,0:T(8,128)(2,1)S(1)} %fusion.3), channel_id=2, replica_groups=mesh['x'=4,'y'=8,'z'=4,'h'=2,'c'=2] {'h','c'}, dimensions={0}, use_global_device_ids=true | all-gather | bytes 1290240 | tf_op jit(solution)/shard_map/all_gather | solution.py:298
  21.5 0.0 copy-done.1
  21.5 0.0 copy-done.2
  21.5 0.7 shard_map.111
  22.2 26.4 %all_to_all.20 = bf16[32,16,128]{2,1,0:T(8,128)(2,1)S(1)} all-to-all(bf16[32,16,128]{2,1,0:T(8,128)(2,1)S(1)} %shard_map.111), channel_id=1, replica_groups=mesh['x'=4,'y'=8,'z'=4,'h'=2,'c'=2] {'y','z'}, dimensions={0} | all-to-all | bytes 262144 | tf_op jit(solution)/shard_map/all_to_all | solution.py:302
  48.6 0.9 broadcast_in_dim.8
  49.4 4.8 %all-to-all-start.1 = ((bf16[4,512,128]{2,1,0:T(8,128)(2,1)}), bf16[4,512,128]{2,1,0:T(8,128)(2,1)}, u32[]{:S(2)}, u32[]{:S(2)}) async-start(bf16[4,512,128]{2,1,0:T(8,128)(2,1)} %broadcast_in_dim.8), calls=%async_computation.1 | async-start | bytes 1048576 | tf_op jit(solution)/shard_map/all_to_all | solution.py:303
  54.2 0.0 copy-start.3
  54.2 1.1 copy-done.3
  55.4 2.6 %shard_map.110 = (bf16[1280,384]{1,0:T(8,128)(2,1)}, bf16[384,320]{1,0:T(8,128)(2,1)}, bf16[384,320]{1,0:T(8,128)(2,1)}, bf16[384,320]{1,0:T(8,128)(2,1)}) custom-call(bf16[4,336,384]{2,1,0:T(8,128)(2,1)S(1)} %bitcast.21, bf16[320,1280]{1,0:T(8,128)(2,1)S(1)} %bitcast.28, bf16[320,1280]{1,0:T(8,128)(2,1)S(1)} %bitcast.23, bf16[320,1280]{1,0:T(8,128)(2,1)S(1)} %bitcast.26), custom_call_target="tpu_custom_call" | custom-call | tf_op jit(solution)/shard_map/pallas_call | solution.py:51
  58.0 3.2 %all-to-all-done.1 = bf16[4,512,128]{2,1,0:T(8,128)(2,1)} async-done(((bf16[4,512,128]{2,1,0:T(8,128)(2,1)}), bf16[4,512,128]{2,1,0:T(8,128)(2,1)}, u32[]{:S(2)}, u32[]{:S(2)}) %all-to-all-start.1) | async-done | bytes 524320 | tf_op jit(solution)/shard_map/all_to_all | solution.py:303
  61.3 0.0 copy-start.5
  61.3 0.9 copy-done.5
  62.2 10.7 %shard_map.112 = (bf16[320,384]{1,0:T(8,128)(2,1)}, bf16[384,320]{1,0:T(8,128)(2,1)}, bf16[384,320]{1,0:T(8,128)(2,1)}, bf16[384,320]{1,0:T(8,128)(2,1)}, bf16[4,256,640]{2,1,0:T(8,128)(2,1)}) custom-call(bf16[384,320]{1,0:T(8,128)(2,1)} %get-tuple-element.20.q_in, bf16[384,320]{1,0:T(8,128)(2,1)} %get-tuple-element.21.k_in, ...), custom_call_target="tpu_custom_call" | custom-call | tf_op jit(solution)/shard_map/pallas_call | solution.py:159
  72.9 0.0 copy-start.4
  72.9 5.9 %all-to-all-start.2 = ((bf16[4,256,640]{2,1,0:T(8,128)(2,1)}), bf16[4,256,640]{2,1,0:T(8,128)(2,1)}, u32[]{:S(2)}, u32[]{:S(2)}) async-start(bf16[4,256,640]{2,1,0:T(8,128)(2,1)} %get-tuple-element.30), calls=%async_computation.2 | async-start | bytes 2621440 | tf_op jit(solution)/shard_map/all_to_all | solution.py:308
  78.8 0.0 copy-done.4
  78.8 3.9 %shard_map.113 = (bf16[2,320,384]{2,1,0:T(8,128)(2,1)}, bf16[2,320,384]{2,1,0:T(8,128)(2,1)}) custom-call(s32[1]{0:T(128)} %bitcast.9.core_ref, bf16[384,320]{1,0:T(8,128)(2,1)} %get-tuple-element.25.dq_in, bf16[384,320]{1,0:T(8,128)(2,1)} %get-tuple-element.26.dk_in, bf16[384,320]{1,0:T(8,128)(2,1)} %get-tuple-element.27.dv_in, ...), custom_call_target="tpu_custom_call" | custom-call | flops 1 | bytes 1 | tf_op jit(solution)/shard_map/pallas_call | solution.py:218
  82.7 1.9 %collective-permute-start = (bf16[2,320,384]{2,1,0:T(8,128)(2,1)}, bf16[2,320,384]{2,1,0:T(8,128)(2,1)S(1)}, u32[]{:S(2)}, u32[]{:S(2)}) collective-permute-start(bf16[2,320,384]{2,1,0:T(8,128)(2,1)} %get-tuple-element.29), channel_id=1, source_target_pairs={{0,1},{1,0},{2,3},{3,2},{4,5},{5,4},{6,7},{7,6},{8,9},{9,8},{10,11... | collective-permute-start | bytes 1474568 | tf_op jit(solution)/shard_map/ppermute | solution.py:310
  84.6 2.0 %collective-permute-done = bf16[2,320,384]{2,1,0:T(8,128)(2,1)S(1)} collective-permute-done((bf16[2,320,384]{2,1,0:T(8,128)(2,1)}, bf16[2,320,384]{2,1,0:T(8,128)(2,1)S(1)}, u32[]{:S(2)}, u32[]{:S(2)}) %collective-permute-start) | collective-permute-done | bytes 491552 | tf_op jit(solution)/shard_map/ppermute | solution.py:310
  86.7 1.2 add_convert_fusion
  87.8 6.6 %collective-permute-start.1 = (bf16[320,384]{1,0:T(8,128)(2,1)S(1)}, bf16[320,384]{1,0:T(8,128)(2,1)S(1)}, u32[]{:S(2)}, u32[]{:S(2)}) collective-permute-start(bf16[320,384]{1,0:T(8,128)(2,1)S(1)} %dynamic-slice_bitcast_fusion), channel_id=1, source_target_pairs={{0,2},{2,0},{1,3},{3,1},{4,6},{6,4},{5,7},{7,5},{8,10},{10,8},{9,1... | collective-permute-start | bytes 737288 | tf_op jit(solution)/shard_map/ppermute | solution.py:314
  94.4 0.0 all-to-all-done.2.in_ref
  94.4 2.3 %shard_map.114 = bf16[256,640]{1,0:T(8,128)(2,1)} custom-call(bf16[4,256,640]{2,1,0:T(8,128)(2,1)} %all-to-all-done.2.in_ref), custom_call_target="tpu_custom_call" | custom-call | flops 10000000000 | bytes 10000000000 | tf_op jit(solution)/shard_map/pallas_call | solution.py:252
  96.8 10.2 %collective-permute-done.1 = bf16[320,384]{1,0:T(8,128)(2,1)S(1)} collective-permute-done((bf16[320,384]{1,0:T(8,128)(2,1)S(1)}, bf16[320,384]{1,0:T(8,128)(2,1)S(1)}, u32[]{:S(2)}, u32[]{:S(2)}) %collective-permute-start.1) | collective-permute-done | bytes 245792 | tf_op jit(solution)/shard_map/ppermute | solution.py:314
  107.0 3.9 %all-to-all-start.3 = ((bf16[32,8,640]{2,1,0:T(8,128)(2,1)}), bf16[32,8,640]{2,1,0:T(8,128)(2,1)S(1)}, u32[]{:S(2)}, u32[]{:S(2)}) async-start(bf16[32,8,640]{2,1,0:T(8,128)(2,1)} %bitcast.13), calls=%async_computation.3 | async-start | bytes 655360 | tf_op jit(solution)/shard_map/all_to_all | solution.py:319
  110.9 0.8 fusion.4
  111.6 13.0 %all-to-all-done.3.in_ref = bf16[32,8,640]{2,1,0:T(8,128)(2,1)S(1)} async-done(((bf16[32,8,640]{2,1,0:T(8,128)(2,1)}), bf16[32,8,640]{2,1,0:T(8,128)(2,1)S(1)}, u32[]{:S(2)}, u32[]{:S(2)}) %all-to-all-start.3) | async-done | bytes 327712 | tf_op jit(solution)/shard_map/all_to_all | solution.py:319
  124.6 0.7 shard_map.115
  (1 shorter events, 0.0 us)
Async XLA Ops:
  0.6 1.2 copy-start
  1.8 19.7 %copy-start.1 = (bf16[1280,320]{0,1:T(8,128)(2,1)S(1)}, bf16[1280,320]{0,1:T(8,128)(2,1)}, u32[]{:S(2)}) copy-start(bf16[1280,320]{0,1:T(8,128)(2,1)} %param.10) | copy-start | bytes 2457604
  1.8 19.7 %copy-start.2 = (bf16[1280,320]{0,1:T(8,128)(2,1)S(1)}, bf16[1280,320]{0,1:T(8,128)(2,1)}, u32[]{:S(2)}) copy-start(bf16[1280,320]{0,1:T(8,128)(2,1)} %param.11) | copy-start | bytes 2457604
  49.4 11.9 %all-to-all-start.1 = ((bf16[4,512,128]{2,1,0:T(8,128)(2,1)}), bf16[4,512,128]{2,1,0:T(8,128)(2,1)}, u32[]{:S(2)}, u32[]{:S(2)}) async-start(bf16[4,512,128]{2,1,0:T(8,128)(2,1)} %broadcast_in_dim.8), calls=%async_computation.1 | async-start | bytes 1048576 | tf_op jit(solution)/shard_map/all_to_all | solution.py:303
  54.2 1.1 copy-start.3
  61.3 0.9 copy-start.5
  72.9 5.9 %copy-start.4 = (bf16[1280,320]{0,1:T(8,128)(2,1)S(1)}, bf16[1280,320]{0,1:T(8,128)(2,1)}, u32[]{:S(2)}) copy-start(bf16[1280,320]{0,1:T(8,128)(2,1)} %param.9) | copy-start | bytes 2457604
  72.9 21.5 %all-to-all-start.2 = ((bf16[4,256,640]{2,1,0:T(8,128)(2,1)}), bf16[4,256,640]{2,1,0:T(8,128)(2,1)}, u32[]{:S(2)}, u32[]{:S(2)}) async-start(bf16[4,256,640]{2,1,0:T(8,128)(2,1)} %get-tuple-element.30), calls=%async_computation.2 | async-start | bytes 2621440 | tf_op jit(solution)/shard_map/all_to_all | solution.py:308
  82.7 4.0 %collective-permute-start = (bf16[2,320,384]{2,1,0:T(8,128)(2,1)}, bf16[2,320,384]{2,1,0:T(8,128)(2,1)S(1)}, u32[]{:S(2)}, u32[]{:S(2)}) collective-permute-start(bf16[2,320,384]{2,1,0:T(8,128)(2,1)} %get-tuple-element.29), channel_id=1, source_target_pairs={{0,1},{1,0},{2,3},{3,2},{4,5},{5,4},{6,7},{7,6},{8,9},{9,8},{10,11... | collective-permute-start | bytes 1474568 | tf_op jit(solution)/shard_map/ppermute | solution.py:310
  87.8 19.2 %collective-permute-start.1 = (bf16[320,384]{1,0:T(8,128)(2,1)S(1)}, bf16[320,384]{1,0:T(8,128)(2,1)S(1)}, u32[]{:S(2)}, u32[]{:S(2)}) collective-permute-start(bf16[320,384]{1,0:T(8,128)(2,1)S(1)} %dynamic-slice_bitcast_fusion), channel_id=1, source_target_pairs={{0,2},{2,0},{1,3},{3,1},{4,6},{6,4},{5,7},{7,5},{8,10},{10,8},{9,1... | collective-permute-start | bytes 737288 | tf_op jit(solution)/shard_map/ppermute | solution.py:314
  107.0 17.6 %all-to-all-start.3 = ((bf16[32,8,640]{2,1,0:T(8,128)(2,1)}), bf16[32,8,640]{2,1,0:T(8,128)(2,1)S(1)}, u32[]{:S(2)}, u32[]{:S(2)}) async-start(bf16[32,8,640]{2,1,0:T(8,128)(2,1)} %bitcast.13), calls=%async_computation.3 | async-start | bytes 655360 | tf_op jit(solution)/shard_map/all_to_all | solution.py:319

commit v7 on v6

--- a/solution.py
+++ b/solution.py
@@ -19,7 +19,7 @@
 ROWS_OUT = 10
 HALF_ROWS = ROWS_OUT // 2
 LANES = 128
-REGROUP_COST = 10**10
+LONG = pl.CostEstimate(flops=10**10, bytes_accessed=10**10, transcendentals=0)
 VMEM_BYTES = 24 * 1024 * 1024
 GROUPS = 2 * WIDTH // LANES
 SCALE = 1.0 / math.sqrt(E)
@@ -32,12 +32,16 @@
 
 
 def project_kernel(
-    g_ref, wq_ref, wk_ref, wv_ref, tok_out, q_out, k_out, v_out, tok_ref, q_ref, k_ref, v_ref, sem
+    half_ref, t_ref, wq_ref, wk_ref, wv_ref, tok_out, q_out, k_out, v_out,
+    tok_ref, q_ref, k_ref, v_ref, sem,
 ):
+    half = half_ref[0]
     pairs = ((tok_ref, tok_out), (q_ref, q_out), (k_ref, k_out), (v_ref, v_out))
     copies = [pltpu.make_async_copy(a, b, sem.at[i]) for i, (a, b) in enumerate(pairs)]
-    for t in range(4):
-        tok_ref[t * WIDTH : (t + 1) * WIDTH, :] = g_ref[t, :WIDTH, :]
+    for core in range(2):
+        for slot in range(2):
+            at = pl.multiple_of((2 * lax.rem(half + slot, 2) + core) * WIDTH, E)
+            tok_ref[pl.ds(at, WIDTH), :] = t_ref[core, slot]
     copies[0].start()
     tok = tok_ref[...]
     for i, (w_ref, out_ref) in enumerate(((wq_ref, q_ref), (wk_ref, k_ref), (wv_ref, v_ref))):
@@ -47,21 +51,24 @@
         copy.wait()
 
 
-def project(gathered, wq, wk, wv):
+def project(half, parts, wq, wk, wv):
+    vmem = pl.BlockSpec(memory_space=pltpu.VMEM)
     return pl.pallas_call(
         project_kernel,
         out_shape=(pltpu.HBM((4 * WIDTH, P_SIZE), BF16),)
         + (pltpu.HBM((P_SIZE, WIDTH), BF16),) * 3,
+        in_specs=[pl.BlockSpec(memory_space=pltpu.SMEM)] + [vmem] * 4,
         out_specs=[pl.BlockSpec(memory_space=pltpu.HBM)] * 4,
         scratch_shapes=[pltpu.VMEM((4 * WIDTH, P_SIZE), BF16)]
         + [pltpu.VMEM((P_SIZE, WIDTH), BF16)] * 3
         + [pltpu.SemaphoreType.DMA((4,))],
+        cost_estimate=LONG,
         compiler_params=pltpu.CompilerParams(vmem_limit_bytes=VMEM_BYTES),
-    )(gathered, wq, wk, wv)
+    )(half.reshape(1), parts, wq, wk, wv)
 
 
 def ref_kernel(g_ref, wk_ref, wv_ref, out_ref, rows_ref):
-    hidden = [g_ref[t, WIDTH : WIDTH + 16, :WIDTH].astype(F32) for t in range(4)]
+    hidden = [g_ref[t].astype(F32) for t in range(4)]
     hidden = jnp.concatenate(hidden, axis=1).astype(BF16)
     pair = jnp.concatenate([dot(hidden, wk_ref[...], 1, 1), dot(hidden, wv_ref[...], 1, 1)], axis=1)
     rows_ref[...] = jnp.zeros_like(rows_ref)
@@ -75,25 +82,23 @@
 def ref_pair(gathered, wk, wv):
     return pl.pallas_call(
         ref_kernel,
-        out_shape=jax.ShapeDtypeStruct((NYZ, 16, LANES), BF16),
+        out_shape=jax.ShapeDtypeStruct((NX * NYZ, 16, LANES), BF16),
         scratch_shapes=[pltpu.VMEM((16, LANES), F32)],
+        cost_estimate=LONG,
         compiler_params=pltpu.CompilerParams(vmem_limit_bytes=12 * 1024 * 1024),
     )(gathered, wk, wv)
 
 
 def attention_kernel(
-    q_in, k_in, v_in, pair_in, tok_in, gt_ref, ot_out, dq_out, dk_out, dv_out, pack_out,
-    q_ref, k_ref, v_ref, pair_ref, tok_ref, wide_ref, r_ref, dqt_ref, dw_ref,
+    q_in, k_in, v_in, tok_in, pair_ref, gt_ref, ot_out, dq_out, dk_out, dv_out, pack_out,
+    q_ref, k_ref, v_ref, tok_ref, wide_ref, r_ref, dqt_ref, dw_ref,
     ot_ref, dq_ref, dk_ref, dv_ref, pack_ref, in_sem, out_sem,
 ):
     n_frames = NX * NYZ
-    pairs = (
-        (pair_in, pair_ref), (k_in, k_ref), (q_in, q_ref), (v_in, v_ref), (tok_in, tok_ref)
-    )
+    pairs = ((k_in, k_ref), (q_in, q_ref), (v_in, v_ref), (tok_in, tok_ref))
     loads = [pltpu.make_async_copy(a, b, in_sem.at[i]) for i, (a, b) in enumerate(pairs)]
     for load in loads:
         load.start()
-    loads[0].wait()
     wide_ref[...] = pair_ref[...].astype(F32)
     for row in range(REF_ROWS):
         for group in range(GROUPS):
@@ -101,7 +106,7 @@
                 wide_ref[pl.ds(row * GROUPS + group, n_frames, stride=16), :].astype(BF16)
             )
     g_all = gt_ref[...].astype(F32).T.astype(BF16)
-    for load in loads[1:4]:
+    for load in loads[:3]:
         load.wait()
     for head in range(HEADS):
         lo, hi = head * E, head * E + E
@@ -129,7 +134,7 @@
                     ].astype(BF16)
     dq = dqt_ref[...].T.astype(BF16)
     dq_ref[...] = dq
-    loads[4].wait()
+    loads[3].wait()
     pairs = ((ot_ref, ot_out), (dq_ref, dq_out), (dk_ref, dk_out), (dv_ref, dv_out))
     stores = [pltpu.make_async_copy(a, b, out_sem.at[NX + i]) for i, (a, b) in enumerate(pairs)]
     for store in stores:
@@ -161,11 +166,10 @@
         out_shape=(pltpu.HBM((WIDTH, P_SIZE), BF16),)
         + (pltpu.HBM((P_SIZE, WIDTH), BF16),) * 3
         + (pltpu.HBM((NX, NYZ * rows, 2 * WIDTH), BF16),),
-        in_specs=[hbm] * 5 + [vmem],
+        in_specs=[hbm] * 4 + [vmem] * 2,
         out_specs=[hbm] * 5,
         scratch_shapes=[pltpu.VMEM((P_SIZE, WIDTH), BF16)] * 3
         + [
-            pltpu.VMEM((NX * NYZ * 16, LANES), BF16),
             pltpu.VMEM((4 * WIDTH, P_SIZE), BF16),
             pltpu.VMEM((NX * NYZ * 16, LANES), F32),
             pltpu.VMEM((P_SIZE, 2 * WIDTH), BF16),
@@ -176,11 +180,11 @@
             pltpu.VMEM((P_SIZE, WIDTH), BF16),
             pltpu.VMEM((P_SIZE, WIDTH), BF16),
             pltpu.VMEM((NX, NYZ * rows, 2 * WIDTH), BF16),
-            pltpu.SemaphoreType.DMA((5,)),
+            pltpu.SemaphoreType.DMA((4,)),
             pltpu.SemaphoreType.DMA((NX + 4,)),
         ],
         compiler_params=pltpu.CompilerParams(vmem_limit_bytes=VMEM_BYTES),
-    )(*[pltpu.with_memory_space_constraint(a, pltpu.HBM) for a in (q, k, v, pair, tok)], gt)
+    )(*[pltpu.with_memory_space_constraint(a, pltpu.HBM) for a in (q, k, v, tok)], pair, gt)
 
 
 def token_kernel(
@@ -232,6 +236,23 @@
     )
 
 
+def combine_kernel(half_ref, pair_ref, got_ref, out_ref):
+    mine = jnp.where(half_ref[0] == 0, pair_ref[0].astype(F32), pair_ref[1].astype(F32))
+    out_ref[...] = (mine + got_ref[...].astype(F32)).astype(BF16)
+
+
+def combine(half, paired, got):
+    vmem = pl.BlockSpec(memory_space=pltpu.VMEM)
+    return pl.pallas_call(
+        combine_kernel,
+        out_shape=jax.ShapeDtypeStruct((WIDTH, P_SIZE), BF16),
+        in_specs=[pl.BlockSpec(memory_space=pltpu.SMEM)] + [vmem] * 2,
+        out_specs=vmem,
+        cost_estimate=LONG,
+        compiler_params=pltpu.CompilerParams(vmem_limit_bytes=8 * 1024 * 1024),
+    )(half.reshape(1), paired, got)
+
+
 def regroup_kernel(in_ref, out_ref, held_ref):
     rows = REF_ROWS + HALF_ROWS
     for row in range(rows):
@@ -253,9 +274,7 @@
         regroup_kernel,
         out_shape=jax.ShapeDtypeStruct((NYZ * rows, 2 * WIDTH), BF16),
         scratch_shapes=[pltpu.VMEM((GROUPS, NYZ * rows, LANES), F32)],
-        cost_estimate=pl.CostEstimate(
-            flops=REGROUP_COST, bytes_accessed=REGROUP_COST, transcendentals=0
-        ),
+        cost_estimate=LONG,
         compiler_params=pltpu.CompilerParams(vmem_limit_bytes=8 * 1024 * 1024),
     )(parts)
 
@@ -294,14 +313,14 @@
     start_col = (2 * half + core) * WIDTH
     source_cols = lax.dynamic_slice_in_dim(reference_image, start_col, WIDTH, 1)
     ref_cols = (source_cols.astype(F32) + dot(reference_image, ref_weight, 1, 0)).astype(BF16)
-    ref_block = jnp.pad(ref_cols, ((0, 16 - REF_ROWS), (0, P_SIZE - WIDTH)))
-    gathered = lax.all_gather(
-        jnp.concatenate([tokens.T, ref_block], axis=0), TENSOR, axis=0, tiled=False
-    )
-    pair = ref_pair(gathered, wk, wv)
-    pair = lax.all_to_all(pair, ("y", "z"), 0, 0, tiled=True).reshape(1, NYZ * 16, LANES)
-    pair = lax.all_to_all(jnp.broadcast_to(pair, (NX, NYZ * 16, LANES)), "x", 0, 0, tiled=True)
-    tok, queries, keys, values = project(gathered, wq, wk, wv)
+    ref_cols = jnp.pad(ref_cols, ((0, 16 - REF_ROWS), (0, 0)))
+    ref_hidden = lax.all_gather(ref_cols, TENSOR, axis=0, tiled=False)
+    ref_hidden, own = lax.optimization_barrier((ref_hidden, tokens.T))
+    other = lax.ppermute(own, "h", swap)
+    pair = ref_pair(ref_hidden, wk, wv)
+    pair = lax.all_to_all(pair, FRAMES, 0, 0, tiled=True)
+    parts = lax.all_gather(jnp.stack([own, other]), "c", axis=0, tiled=False)
+    tok, queries, keys, values = project(half, parts, wq, wk, wv)
     attended, query_grads, key_grads, value_grads, pack = attention(
         queries, keys, values, pair.reshape(NX * NYZ * 16, LANES), cotangent.T, tok
     )
@@ -309,12 +328,10 @@
     kept, sent = token_parts(core, query_grads, key_grads, value_grads, wq, wk, wv)
     got = lax.ppermute(sent, "c", swap)
     paired = (kept.astype(F32) + got.astype(F32)).astype(BF16)
-    kept = lax.dynamic_index_in_dim(paired, half, 0, False)
     sent = lax.dynamic_index_in_dim(paired, 1 - half, 0, False)
     got = lax.ppermute(sent, "h", swap)
-    token_grads = (kept.astype(F32) + got.astype(F32)).astype(BF16).T
+    token_grads = combine(half, paired, got).T
     pack = regroup(pack)
-    pack, _ = lax.optimization_barrier((pack, got))
     pack = pack.reshape(NYZ, REF_ROWS + HALF_ROWS, 2 * WIDTH)
     pack = lax.all_to_all(pack, ("y", "z"), 0, 0, tiled=True)
     query_weight_grad, ref_key_grads, ref_value_grads = finish(pack)

time: 126 us -> 113 us (0.90)
  the two profiles are of different devices: /device:TPU:2 before, /device:TPU:1 now
where the time goes in v7:
time: 113 us; the launch traced here: 112 us
  starting transfers between devices  38 us (34%)
  waiting for transfers between devices  25.5 us (23%)
  Pallas kernels  20.8 us (18%)
  blocking collectives  19 us (17%)
  local copies, waits for them, and re-layouts  5.79 us (5%)
  other arithmetic  1.21 us (1%)
    all_gather x1, blocking collectives, per_device(): ref_hidden = lax.all_gather(ref_cols, TENSOR, axis=0, tiled=False)  15.8 us
    all_to_all x1, starting transfers between devices, per_device(): pair = lax.all_to_all(pair, FRAMES, 0, 0, tiled=True)  14.2 us
    all_to_all x1, waiting for transfers between devices, per_device(): pack = lax.all_to_all(pack, ('y', 'z'), 0, 0, tiled=True)  11.3 us
    all_to_all x1, waiting for transfers between devices, per_device(): pair = lax.all_to_all(pair, FRAMES, 0, 0, tiled=True)  10.9 us
    pallas_call x1, Pallas kernels, attention(): pl.pallas_call(attention_kernel, out_shape=(pltpu.HBM((WIDTH, P_SIZE), BF...  10.2 us
    all_to_all x1, starting transfers between devices, per_device(): pack = lax.all_to_all(pack, ('y', 'z'), 0, 0, tiled=True)  8.33 us
    unnamed x20, local copies, waits for them, and re-layouts  5.73 us
    ppermute x1, starting transfers between devices, per_device(): other = lax.ppermute(own, 'h', swap)  5.26 us
  transfers between devices with their start and end apart: 6, of which 4 were waited for; matrix products, arithmetic and copies ran while one was open for 1% of the time, Pallas kernels for 9%

profile of v7, /device:TPU:1, one launch (start us, length us, event | category | flops | bytes accessed | tf_op | source)
XLA Modules:
  0.0 112.2 jit_solution(17662049535972920213)
XLA Ops:
  0.6 0.0 copy-start
  0.7 1.1 %copy-done = bf16[1280,320]{0,1:T(8,128)(2,1)S(1)} copy-done((bf16[1280,320]{0,1:T(8,128)(2,1)S(1)}, bf16[1280,320]{0,1:T(8,128)(2,1)}, u32[]{:S(2)}) %copy-start) | copy-done | bytes 819224
  1.8 1.1 fusion
  2.9 15.8 %all-gather = bf16[64,320]{1,0:T(8,128)(2,1)S(1)} all-gather(bf16[16,320]{1,0:T(8,128)(2,1)S(1)} %pad.4), channel_id=2, replica_groups=mesh['x'=4,'y'=8,'z'=4,'h'=2,'c'=2] {'h','c'}, dimensions={0}, use_global_device_ids=true | all-gather | bytes 51200 | tf_op jit(solution)/shard_map/all_gather | solution.py:317
  18.7 5.3 %collective-permute-start = (bf16[320,384]{1,0:T(8,128)(2,1)}, bf16[320,384]{1,0:T(8,128)(2,1)S(1)}, u32[]{:S(2)}, u32[]{:S(2)}) collective-permute-start(bf16[320,384]{1,0:T(8,128)(2,1)} %bitcast.31), channel_id=1, source_target_pairs={{0,2},{2,0},{1,3},{3,1},{4,6},{6,4},{5,7},{7,5},{8,10},{10,8},{9,1... | collective-permute-start | bytes 737288 | tf_op jit(solution)/shard_map/ppermute | solution.py:319
  24.0 0.0 copy-start.2
  24.0 1.1 %copy-done.2 = bf16[1280,320]{0,1:T(8,128)(2,1)S(1)} copy-done((bf16[1280,320]{0,1:T(8,128)(2,1)S(1)}, bf16[1280,320]{0,1:T(8,128)(2,1)}, u32[]{:S(2)}) %copy-start.2) | copy-done | bytes 819224
  25.1 0.0 copy-start.5
  25.1 1.1 %copy-done.5 = bf16[1280,320]{0,1:T(8,128)(2,1)S(1)} copy-done((bf16[1280,320]{0,1:T(8,128)(2,1)S(1)}, bf16[1280,320]{0,1:T(8,128)(2,1)}, u32[]{:S(2)}) %copy-start.5) | copy-done | bytes 819224
  26.3 0.0 copy-start.9
  26.3 1.5 %shard_map.111 = bf16[128,16,128]{2,1,0:T(8,128)(2,1)} custom-call(bf16[4,16,320]{2,1,0:T(8,128)(2,1)S(1)} %bitcast.30, bf16[320,1280]{1,0:T(8,128)(2,1)S(1)} %bitcast.23, bf16[320,1280]{1,0:T(8,128)(2,1)S(1)} %bitcast.26), custom_call_target="tpu_custom_call" | custom-call | flops 10000000000 | bytes 10000000000 | tf_op jit(solution)/shard_map/pallas_call | solution.py:83
  27.8 14.2 %all-to-all-start = ((bf16[128,16,128]{2,1,0:T(8,128)(2,1)}), bf16[128,16,128]{2,1,0:T(8,128)(2,1)S(1)}, u32[]{:S(2)}, u32[]{:S(2)}) async-start(bf16[128,16,128]{2,1,0:T(8,128)(2,1)} %shard_map.111), calls=%async_computation | async-start | bytes 1048576 | tf_op jit(solution)/shard_map/all_to_all | solution.py:321
  42.0 0.0 copy-start.1
  42.0 0.0 copy-start.3
  42.0 0.0 copy-start.6
  42.1 0.0 collective-permute-done
  42.1 0.0 copy-done.9
  42.1 0.1 pad_maximum_fusion
  42.1 3.2 %all-gather.1 = bf16[4,320,384]{2,1,0:T(8,128)(2,1)S(1)} all-gather(bf16[2,320,384]{2,1,0:T(8,128)(2,1)S(1)} %pad_maximum_fusion), channel_id=3, replica_groups=mesh['x'=4,'y'=8,'z'=4,'h'=2,'c'=2] {'c'}, dimensions={0}, use_global_device_ids=true | all-gather | bytes 1474560 | tf_op jit(solution)/shard_map/all_gather | solution.py:322
  45.3 0.0 copy-done.1
  45.3 0.0 copy-done.3
  45.3 0.0 copy-done.6
  45.3 0.0 copy-start.8
  45.4 2.7 %shard_map.110 = (bf16[1280,384]{1,0:T(8,128)(2,1)}, bf16[384,320]{1,0:T(8,128)(2,1)}, bf16[384,320]{1,0:T(8,128)(2,1)}, bf16[384,320]{1,0:T(8,128)(2,1)}) custom-call(s32[1]{0:T(128)} %bitcast.half_ref, bf16[2,2,320,384]{3,2,1,0:T(8,128)(2,1)S(1)} %bitcast.20, bf16[320,1280]{1,0:T(8,128)(2,1)S(1)} %bitcast.21, bf16[320,1280]{1,0:T(8,128)(2,1)S(1)} %bitcast.24, ...), custom_call_target="tpu_custom_call" | custom-call | flops 10000000000 | bytes 10000000000 | tf_op jit(solution)/shard_map/pallas_call | solution.py:56
  48.0 10.9 %all-to-all-done = bf16[128,16,128]{2,1,0:T(8,128)(2,1)S(1)} async-done(((bf16[128,16,128]{2,1,0:T(8,128)(2,1)}), bf16[128,16,128]{2,1,0:T(8,128)(2,1)S(1)}, u32[]{:S(2)}, u32[]{:S(2)}) %all-to-all-start) | async-done | bytes 524320 | tf_op jit(solution)/shard_map/all_to_all | solution.py:321
  58.9 0.0 copy-done.8
  58.9 10.2 %shard_map.112 = (bf16[320,384]{1,0:T(8,128)(2,1)}, bf16[384,320]{1,0:T(8,128)(2,1)}, bf16[384,320]{1,0:T(8,128)(2,1)}, bf16[384,320]{1,0:T(8,128)(2,1)}, bf16[4,256,640]{2,1,0:T(8,128)(2,1)}) custom-call(bf16[384,320]{1,0:T(8,128)(2,1)} %get-tuple-element.22.q_in, bf16[384,320]{1,0:T(8,128)(2,1)} %get-tuple-element.23.k_in, ...), custom_call_target="tpu_custom_call" | custom-call | tf_op jit(solution)/shard_map/pallas_call | solution.py:164
  69.1 3.6 %all-to-all-start.1 = ((bf16[4,256,640]{2,1,0:T(8,128)(2,1)}), bf16[4,256,640]{2,1,0:T(8,128)(2,1)S(1)}, u32[]{:S(2)}, u32[]{:S(2)}) async-start(bf16[4,256,640]{2,1,0:T(8,128)(2,1)} %get-tuple-element.33), calls=%async_computation.1 | async-start | bytes 2621440 | tf_op jit(solution)/shard_map/all_to_all | solution.py:327
  72.7 0.0 copy-start.4
  72.7 1.1 %copy-done.4 = bf16[1280,320]{0,1:T(8,128)(2,1)S(1)} copy-done((bf16[1280,320]{0,1:T(8,128)(2,1)S(1)}, bf16[1280,320]{0,1:T(8,128)(2,1)}, u32[]{:S(2)}) %copy-start.4) | copy-done | bytes 819224
  73.8 0.0 copy-start.7
  73.8 1.1 %copy-done.7 = bf16[1280,320]{0,1:T(8,128)(2,1)S(1)} copy-done((bf16[1280,320]{0,1:T(8,128)(2,1)S(1)}, bf16[1280,320]{0,1:T(8,128)(2,1)}, u32[]{:S(2)}) %copy-start.7) | copy-done | bytes 819224
  75.0 3.9 %shard_map.113 = (bf16[2,320,384]{2,1,0:T(8,128)(2,1)}, bf16[2,320,384]{2,1,0:T(8,128)(2,1)}) custom-call(s32[1]{0:T(128)} %bitcast.12.core_ref, bf16[384,320]{1,0:T(8,128)(2,1)} %get-tuple-element.28.dq_in, bf16[384,320]{1,0:T(8,128)(2,1)} %get-tuple-element.29.dk_in, bf16[384,320]{1,0:T(8,128)(2,1)} %get-tuple-element.30.dv_in, ...), custom_call_target="tpu_custom_call" | custom-call | flops 1 | bytes 1 | tf_op jit(solution)/shard_map/pallas_call | solution.py:222
  78.9 4.7 %collective-permute-start.1 = (bf16[2,320,384]{2,1,0:T(8,128)(2,1)}, bf16[2,320,384]{2,1,0:T(8,128)(2,1)S(1)}, u32[]{:S(2)}, u32[]{:S(2)}) collective-permute-start(bf16[2,320,384]{2,1,0:T(8,128)(2,1)} %get-tuple-element.32), channel_id=1, source_target_pairs={{0,1},{1,0},{2,3},{3,2},{4,5},{5,4},{6,7},{7,6},{8,9},{9,8},{10,11... | collective-permute-start | bytes 1474568 | tf_op jit(solution)/shard_map/ppermute | solution.py:329
  83.5 1.7 %collective-permute-done.1 = bf16[2,320,384]{2,1,0:T(8,128)(2,1)S(1)} collective-permute-done((bf16[2,320,384]{2,1,0:T(8,128)(2,1)}, bf16[2,320,384]{2,1,0:T(8,128)(2,1)S(1)}, u32[]{:S(2)}, u32[]{:S(2)}) %collective-permute-start.1) | collective-permute-done | bytes 491552 | tf_op jit(solution)/shard_map/ppermute | solution.py:329
  85.2 1.1 %add_convert_fusion.pair_ref = bf16[2,320,384]{2,1,0:T(8,128)(2,1)S(1)} fusion(bf16[2,320,384]{2,1,0:T(8,128)(2,1)S(1)} %collective-permute-done.1, bf16[2,320,384]{2,1,0:T(8,128)(2,1)} %get-tuple-element.31), kind=kLoop, calls=%fused_computation.2 | loop fusion | flops 983040 | bytes 1474560 | tf_op jit(solution)/shard_map/convert_element_type | solution.py:330
  86.4 1.9 %collective-permute-start.2 = (bf16[320,384]{1,0:T(8,128)(2,1)S(1)}, bf16[320,384]{1,0:T(8,128)(2,1)S(1)}, u32[]{:S(2)}, u32[]{:S(2)}) collective-permute-start(bf16[320,384]{1,0:T(8,128)(2,1)S(1)} %dynamic-slice_bitcast_fusion), channel_id=1, source_target_pairs={{0,2},{2,0},{1,3},{3,1},{4,6},{6,4},{5,7},{7,5},{8,10},{10,8},{9,1... | collective-permute-start | bytes 737288 | tf_op jit(solution)/shard_map/ppermute | solution.py:332
  88.3 0.0 all-to-all-done.1.in_ref
  88.4 1.0 shard_map.115
  89.4 8.3 %all-to-all-start.2 = ((bf16[32,8,640]{2,1,0:T(8,128)(2,1)}), bf16[32,8,640]{2,1,0:T(8,128)(2,1)S(1)}, u32[]{:S(2)}, u32[]{:S(2)}) async-start(bf16[32,8,640]{2,1,0:T(8,128)(2,1)} %bitcast.15), calls=%async_computation.2 | async-start | bytes 655360 | tf_op jit(solution)/shard_map/all_to_all | solution.py:336
  97.7 1.7 %collective-permute-done.2.got_ref = bf16[320,384]{1,0:T(8,128)(2,1)S(1)} collective-permute-done((bf16[320,384]{1,0:T(8,128)(2,1)S(1)}, bf16[320,384]{1,0:T(8,128)(2,1)S(1)}, u32[]{:S(2)}, u32[]{:S(2)}) %collective-permute-start.2) | collective-permute-done | bytes 245792 | tf_op jit(solution)/shard_map/ppermute | solution.py:332
  99.4 0.8 shard_map.114
  100.2 11.3 %all-to-all-done.2.in_ref = bf16[32,8,640]{2,1,0:T(8,128)(2,1)S(1)} async-done(((bf16[32,8,640]{2,1,0:T(8,128)(2,1)}), bf16[32,8,640]{2,1,0:T(8,128)(2,1)S(1)}, u32[]{:S(2)}, u32[]{:S(2)}) %all-to-all-start.2) | async-done | bytes 327712 | tf_op jit(solution)/shard_map/all_to_all | solution.py:336
  111.5 0.7 shard_map.116
  (2 shorter events, 0.1 us)
Async XLA Ops:
  0.6 1.2 %copy-start = (bf16[1280,320]{0,1:T(8,128)(2,1)S(1)}, bf16[1280,320]{0,1:T(8,128)(2,1)}, u32[]{:S(2)}) copy-start(bf16[1280,320]{0,1:T(8,128)(2,1)} %param.12) | copy-start | bytes 2457604
  18.7 23.3 %collective-permute-start = (bf16[320,384]{1,0:T(8,128)(2,1)}, bf16[320,384]{1,0:T(8,128)(2,1)S(1)}, u32[]{:S(2)}, u32[]{:S(2)}) collective-permute-start(bf16[320,384]{1,0:T(8,128)(2,1)} %bitcast.31), channel_id=1, source_target_pairs={{0,2},{2,0},{1,3},{3,1},{4,6},{6,4},{5,7},{7,5},{8,10},{10,8},{9,1... | collective-permute-start | bytes 737288 | tf_op jit(solution)/shard_map/ppermute | solution.py:319
  24.0 1.1 %copy-start.2 = (bf16[1280,320]{0,1:T(8,128)(2,1)S(1)}, bf16[1280,320]{0,1:T(8,128)(2,1)}, u32[]{:S(2)}) copy-start(bf16[1280,320]{0,1:T(8,128)(2,1)} %param.10) | copy-start | bytes 2457604
  25.1 1.1 %copy-start.5 = (bf16[1280,320]{0,1:T(8,128)(2,1)S(1)}, bf16[1280,320]{0,1:T(8,128)(2,1)}, u32[]{:S(2)}) copy-start(bf16[1280,320]{0,1:T(8,128)(2,1)} %param.11) | copy-start | bytes 2457604
  26.3 15.8 %copy-start.9 = (bf16[384,320]{0,1:T(8,128)(2,1)S(1)}, bf16[384,320]{0,1:T(8,128)(2,1)}, u32[]{:S(2)}) copy-start(bf16[384,320]{0,1:T(8,128)(2,1)} %param.7) | copy-start | bytes 737284
  27.8 31.1 %all-to-all-start = ((bf16[128,16,128]{2,1,0:T(8,128)(2,1)}), bf16[128,16,128]{2,1,0:T(8,128)(2,1)S(1)}, u32[]{:S(2)}, u32[]{:S(2)}) async-start(bf16[128,16,128]{2,1,0:T(8,128)(2,1)} %shard_map.111), calls=%async_computation | async-start | bytes 1048576 | tf_op jit(solution)/shard_map/all_to_all | solution.py:321
  42.0 3.3 %copy-start.1 = (bf16[1280,320]{0,1:T(8,128)(2,1)S(1)}, bf16[1280,320]{0,1:T(8,128)(2,1)}, u32[]{:S(2)}) copy-start(bf16[1280,320]{0,1:T(8,128)(2,1)} %param.9) | copy-start | bytes 2457604
  42.0 3.3 %copy-start.3 = (bf16[1280,320]{0,1:T(8,128)(2,1)S(1)}, bf16[1280,320]{0,1:T(8,128)(2,1)}, u32[]{:S(2)}) copy-start(bf16[1280,320]{0,1:T(8,128)(2,1)} %param.10) | copy-start | bytes 2457604
  42.0 3.3 %copy-start.6 = (bf16[1280,320]{0,1:T(8,128)(2,1)S(1)}, bf16[1280,320]{0,1:T(8,128)(2,1)}, u32[]{:S(2)}) copy-start(bf16[1280,320]{0,1:T(8,128)(2,1)} %param.11) | copy-start | bytes 2457604
  45.3 13.5 %copy-start.8 = (bf16[384,320]{0,1:T(8,128)(2,1)S(1)}, bf16[384,320]{0,1:T(8,128)(2,1)}, u32[]{:S(2)}) copy-start(bf16[384,320]{0,1:T(8,128)(2,1)} %param.13) | copy-start | bytes 737284
  69.1 19.2 %all-to-all-start.1 = ((bf16[4,256,640]{2,1,0:T(8,128)(2,1)}), bf16[4,256,640]{2,1,0:T(8,128)(2,1)S(1)}, u32[]{:S(2)}, u32[]{:S(2)}) async-start(bf16[4,256,640]{2,1,0:T(8,128)(2,1)} %get-tuple-element.33), calls=%async_computation.1 | async-start | bytes 2621440 | tf_op jit(solution)/shard_map/all_to_all | solution.py:327
  72.7 1.1 %copy-start.4 = (bf16[1280,320]{0,1:T(8,128)(2,1)S(1)}, bf16[1280,320]{0,1:T(8,128)(2,1)}, u32[]{:S(2)}) copy-start(bf16[1280,320]{0,1:T(8,128)(2,1)} %param.10) | copy-start | bytes 2457604
  73.8 1.1 %copy-start.7 = (bf16[1280,320]{0,1:T(8,128)(2,1)S(1)}, bf16[1280,320]{0,1:T(8,128)(2,1)}, u32[]{:S(2)}) copy-start(bf16[1280,320]{0,1:T(8,128)(2,1)} %param.11) | copy-start | bytes 2457604
  78.9 6.4 %collective-permute-start.1 = (bf16[2,320,384]{2,1,0:T(8,128)(2,1)}, bf16[2,320,384]{2,1,0:T(8,128)(2,1)S(1)}, u32[]{:S(2)}, u32[]{:S(2)}) collective-permute-start(bf16[2,320,384]{2,1,0:T(8,128)(2,1)} %get-tuple-element.32), channel_id=1, source_target_pairs={{0,1},{1,0},{2,3},{3,2},{4,5},{5,4},{6,7},{7,6},{8,9},{9,8},{10,11... | collective-permute-start | bytes 1474568 | tf_op jit(solution)/shard_map/ppermute | solution.py:329
  86.4 13.0 %collective-permute-start.2 = (bf16[320,384]{1,0:T(8,128)(2,1)S(1)}, bf16[320,384]{1,0:T(8,128)(2,1)S(1)}, u32[]{:S(2)}, u32[]{:S(2)}) collective-permute-start(bf16[320,384]{1,0:T(8,128)(2,1)S(1)} %dynamic-slice_bitcast_fusion), channel_id=1, source_target_pairs={{0,2},{2,0},{1,3},{3,1},{4,6},{6,4},{5,7},{7,5},{8,10},{10,8},{9,1... | collective-permute-start | bytes 737288 | tf_op jit(solution)/shard_map/ppermute | solution.py:332
  89.4 22.1 %all-to-all-start.2 = ((bf16[32,8,640]{2,1,0:T(8,128)(2,1)}), bf16[32,8,640]{2,1,0:T(8,128)(2,1)S(1)}, u32[]{:S(2)}, u32[]{:S(2)}) async-start(bf16[32,8,640]{2,1,0:T(8,128)(2,1)} %bitcast.15), calls=%async_computation.2 | async-start | bytes 655360 | tf_op jit(solution)/shard_map/all_to_all | solution.py:336

commit v8 on v7

--- a/solution.py
+++ b/solution.py
@@ -67,11 +67,51 @@
     )(half.reshape(1), parts, wq, wk, wv)
 
 
-def ref_kernel(g_ref, wk_ref, wv_ref, out_ref, rows_ref):
+def cols_kernel(at_ref, r_ref, w_in, out_ref, w_ref, sem):
+    load = pltpu.make_async_copy(w_in, w_ref, sem.at[0])
+    load.start()
+    image = r_ref[...]
+    mine = image[:, :WIDTH]
+    for t in range(1, 4):
+        mine = jnp.where(at_ref[0] == t, image[:, t * WIDTH : (t + 1) * WIDTH], mine)
+    load.wait()
+    cols = mine.astype(F32) + dot(image, w_ref[...], 1, 1)
+    out_ref[...] = jnp.zeros_like(out_ref)
+    out_ref[:REF_ROWS, :] = cols.astype(BF16)
+
+
+def ref_cols(at, image, wr):
+    vmem = pl.BlockSpec(memory_space=pltpu.VMEM)
+    return pl.pallas_call(
+        cols_kernel,
+        out_shape=jax.ShapeDtypeStruct((16, WIDTH), BF16),
+        in_specs=[
+            pl.BlockSpec(memory_space=pltpu.SMEM), vmem, pl.BlockSpec(memory_space=pltpu.HBM)
+        ],
+        out_specs=vmem,
+        scratch_shapes=[
+            pltpu.VMEM((WIDTH, 4 * WIDTH), BF16),
+            pltpu.SemaphoreType.DMA((1,)),
+        ],
+        compiler_params=pltpu.CompilerParams(vmem_limit_bytes=8 * 1024 * 1024),
+    )(at.reshape(1), image, pltpu.with_memory_space_constraint(wr, pltpu.HBM))
+
+
+def ref_kernel(g_ref, wk_in, wv_in, out_ref, rows_ref, wk_ref, wv_ref, sem):
+    loads = [
+        pltpu.make_async_copy(a, b, sem.at[i])
+        for i, (a, b) in enumerate(((wk_in, wk_ref), (wv_in, wv_ref)))
+    ]
+    for load in loads:
+        load.start()
     hidden = [g_ref[t].astype(F32) for t in range(4)]
     hidden = jnp.concatenate(hidden, axis=1).astype(BF16)
-    pair = jnp.concatenate([dot(hidden, wk_ref[...], 1, 1), dot(hidden, wv_ref[...], 1, 1)], axis=1)
     rows_ref[...] = jnp.zeros_like(rows_ref)
+    pair = []
+    for load, w_ref in zip(loads, (wk_ref, wv_ref)):
+        load.wait()
+        pair.append(dot(hidden, w_ref[...], 1, 1))
+    pair = jnp.concatenate(pair, axis=1)
     for row in range(REF_ROWS):
         for group in range(GROUPS):
             at = row * GROUPS + group
@@ -80,13 +120,18 @@
 
 
 def ref_pair(gathered, wk, wv):
+    hbm, vmem = [pl.BlockSpec(memory_space=space) for space in (pltpu.HBM, pltpu.VMEM)]
     return pl.pallas_call(
         ref_kernel,
         out_shape=jax.ShapeDtypeStruct((NX * NYZ, 16, LANES), BF16),
-        scratch_shapes=[pltpu.VMEM((16, LANES), F32)],
+        in_specs=[vmem, hbm, hbm],
+        out_specs=vmem,
+        scratch_shapes=[pltpu.VMEM((16, LANES), F32)]
+        + [pltpu.VMEM((WIDTH, 4 * WIDTH), BF16)] * 2
+        + [pltpu.SemaphoreType.DMA((2,))],
         cost_estimate=LONG,
         compiler_params=pltpu.CompilerParams(vmem_limit_bytes=12 * 1024 * 1024),
-    )(gathered, wk, wv)
+    )(gathered, *[pltpu.with_memory_space_constraint(a, pltpu.HBM) for a in (wk, wv)])
 
 
 def attention_kernel(
@@ -108,21 +153,26 @@
     g_all = gt_ref[...].astype(F32).T.astype(BF16)
     for load in loads[:3]:
         load.wait()
-    for head in range(HEADS):
+    def scores(head):
         lo, hi = head * E, head * E + E
-        q, g = q_ref[:, lo:hi], g_all[:, lo:hi]
+        q = q_ref[:, lo:hi]
         k = jnp.concatenate([k_ref[:, lo:hi], r_ref[:, lo:hi]], 0)
         v = jnp.concatenate([v_ref[:, lo:hi], r_ref[:, WIDTH + lo : WIDTH + hi]], 0)
-        s = dot(k, q, 1, 1)
-        s = jnp.exp2((s - jnp.max(s, axis=0, keepdims=True)) * (SCALE * math.log2(math.e)))
-        p = s * (1.0 / jnp.sum(s, axis=0, keepdims=True))
-        p_low = p.astype(BF16)
+        return k, v, q, dot(k, q, 1, 1), dot(v, gt_ref[lo:hi, :], 1, 0)
+
+    def soften(k, v, q, s, dp):
+        e = jnp.exp2((s - jnp.max(s, axis=0, keepdims=True)) * (SCALE * math.log2(math.e)))
+        inv = 1.0 / jnp.sum(e, axis=0, keepdims=True)
+        mean = jnp.sum(e * dp, axis=0, keepdims=True) * inv
+        p = e * inv
+        return k, v, q, p.astype(BF16), (p * (dp - mean)).astype(BF16)
+
+    def write(head, k, v, q, p_low, ds):
+        lo, hi = head * E, head * E + E
         ot_ref[lo:hi, :] = dot(v, p_low, 0, 0).astype(BF16)
-        dp = dot(v, gt_ref[lo:hi, :], 1, 0)
-        ds = (p * (dp - jnp.sum(p * dp, axis=0, keepdims=True))).astype(BF16)
         dqt_ref[lo:hi, :] = dot(k, ds, 0, 0) * SCALE
         dk = dot(ds, q, 1, 0) * SCALE
-        dv = dot(p_low, g, 1, 0)
+        dv = dot(p_low, g_all[:, lo:hi], 1, 0)
         dk_ref[:, lo:hi] = dk[:P_SIZE].astype(BF16)
         dv_ref[:, lo:hi] = dv[:P_SIZE].astype(BF16)
         for col, part in ((lo, dk), (WIDTH + lo, dv)):
@@ -132,6 +182,13 @@
                     pack_ref[x, NYZ * row : NYZ * (row + 1), col : col + E] = part[
                         at : at + NYZ
                     ].astype(BF16)
+
+    ahead = scores(0)
+    for head in range(HEADS):
+        now = ahead
+        if head + 1 < HEADS:
+            ahead = scores(head + 1)
+        write(head, *soften(*now))
     dq = dqt_ref[...].T.astype(BF16)
     dq_ref[...] = dq
     loads[3].wait()
@@ -188,19 +245,21 @@
 
 
 def token_kernel(
-    core_ref, dq_in, dk_in, dv_in, wq_ref, wk_ref, wv_ref, kept_out, sent_out,
-    dq_ref, dk_ref, dv_ref, kept_ref, sent_ref, in_sem, out_sem,
+    core_ref, dq_in, dk_in, dv_in, wq_in, wk_in, wv_in, kept_out, sent_out,
+    dq_ref, dk_ref, dv_ref, wq_ref, wk_ref, wv_ref, kept_ref, sent_ref, in_sem, out_sem,
 ):
-    pairs = ((dq_in, dq_ref), (dk_in, dk_ref), (dv_in, dv_ref))
+    pairs = (
+        (wq_in, wq_ref), (dq_in, dq_ref), (wk_in, wk_ref),
+        (dk_in, dk_ref), (wv_in, wv_ref), (dv_in, dv_ref),
+    )
     loads = [pltpu.make_async_copy(a, b, in_sem.at[i]) for i, (a, b) in enumerate(pairs)]
     for load in loads:
         load.start()
     core = core_ref[0]
     total = None
-    for load, (d_ref, w_ref) in zip(
-        loads, ((dq_ref, wq_ref), (dk_ref, wk_ref), (dv_ref, wv_ref))
-    ):
-        load.wait()
+    for i, (d_ref, w_ref) in enumerate(((dq_ref, wq_ref), (dk_ref, wk_ref), (dv_ref, wv_ref))):
+        loads[2 * i].wait()
+        loads[2 * i + 1].wait()
         part = dot(d_ref[...], w_ref[...], 1, 0)
         total = part if total is None else total + part
     total = total.T.astype(BF16)
@@ -218,21 +277,21 @@
 
 
 def token_parts(core, dq, dk, dv, wq, wk, wv):
-    hbm, vmem = [pl.BlockSpec(memory_space=space) for space in (pltpu.HBM, pltpu.VMEM)]
+    hbm = pl.BlockSpec(memory_space=pltpu.HBM)
     return pl.pallas_call(
         token_kernel,
         out_shape=(pltpu.HBM((2, WIDTH, P_SIZE), BF16),) * 2,
-        in_specs=[pl.BlockSpec(memory_space=pltpu.SMEM)] + [hbm] * 3 + [vmem] * 3,
+        in_specs=[pl.BlockSpec(memory_space=pltpu.SMEM)] + [hbm] * 6,
         out_specs=[hbm] * 2,
         scratch_shapes=[pltpu.VMEM((P_SIZE, WIDTH), BF16)] * 3
+        + [pltpu.VMEM((WIDTH, 4 * WIDTH), BF16)] * 3
         + [pltpu.VMEM((2, WIDTH, P_SIZE), BF16)] * 2
-        + [pltpu.SemaphoreType.DMA((3,)), pltpu.SemaphoreType.DMA((4,))],
+        + [pltpu.SemaphoreType.DMA((6,)), pltpu.SemaphoreType.DMA((4,))],
         cost_estimate=pl.CostEstimate(flops=1, bytes_accessed=1, transcendentals=0),
         compiler_params=pltpu.CompilerParams(vmem_limit_bytes=VMEM_BYTES),
     )(
         core.reshape(1),
-        *[pltpu.with_memory_space_constraint(a, pltpu.HBM) for a in (dq, dk, dv)],
-        wq, wk, wv,
+        *[pltpu.with_memory_space_constraint(a, pltpu.HBM) for a in (dq, dk, dv, wq, wk, wv)],
     )
 
 
@@ -310,11 +369,8 @@
     core, half = lax.axis_index("c"), lax.axis_index("h")
     swap = [(0, 1), (1, 0)]
     wq, wk, wv = query_weight.T, key_weight.T, value_weight.T
-    start_col = (2 * half + core) * WIDTH
-    source_cols = lax.dynamic_slice_in_dim(reference_image, start_col, WIDTH, 1)
-    ref_cols = (source_cols.astype(F32) + dot(reference_image, ref_weight, 1, 0)).astype(BF16)
-    ref_cols = jnp.pad(ref_cols, ((0, 16 - REF_ROWS), (0, 0)))
-    ref_hidden = lax.all_gather(ref_cols, TENSOR, axis=0, tiled=False)
+    cols = ref_cols(2 * half + core, reference_image, ref_weight.T)
+    ref_hidden = lax.all_gather(cols, TENSOR, axis=0, tiled=False)
     ref_hidden, own = lax.optimization_barrier((ref_hidden, tokens.T))
     other = lax.ppermute(own, "h", swap)
     pair = ref_pair(ref_hidden, wk, wv)

time: 113 us -> 110 us (0.973)
  local copies, waits for them, and re-layouts: 5.79 us -> 0.76 us
  Pallas kernels: 20.8 us -> 22.9 us
    unnamed x20 -> x12, local copies, waits for them, and re-layouts: 5.73 us -> 0.72 us
    ppermute x1, waiting for transfers between devices: 1.67 us -> 0.09 us  [per_device(): got = lax.ppermute(sent, 'h', swap)]
    pallas_call x1, Pallas kernels: 1.5 us -> 3.03 us  [ref_pair(): pl.pallas_call(ref_kernel, out_shape=jax.ShapeDtypeStruct((NX * NYZ, 16,...]
    pallas_call x0 -> x1, Pallas kernels: none -> 1.49 us  [ref_cols(): pl.pallas_call(cols_kernel, out_shape=jax.ShapeDtypeStruct((16, WIDTH), B...]
    pallas_call x1, Pallas kernels: 10.2 us -> 8.76 us  [attention(): pl.pallas_call(attention_kernel, out_shape=(pltpu.HBM((WIDTH, P_SIZE), BF...]
  transfers between devices with their start and end apart: 6 -> 6, of which waited for: 4 -> 5; matrix products, arithmetic and copies ran while one was open for 1% -> 1% of each run, Pallas kernels for 9% -> 11%
where the time goes in v8:
time: 110 us; the launch traced here: 109 us
  starting transfers between devices  38.7 us (35%)
  waiting for transfers between devices  25.7 us (23%)
  Pallas kernels  22.9 us (21%)
  blocking collectives  18.8 us (17%)
  other arithmetic  1.21 us (1%)
    all_gather x1, blocking collectives, per_device(): ref_hidden = lax.all_gather(cols, TENSOR, axis=0, tiled=False)  15.8 us
    all_to_all x1, starting transfers between devices, per_device(): pair = lax.all_to_all(pair, FRAMES, 0, 0, tiled=True)  14.2 us
    all_to_all x1, waiting for transfers between devices, per_device(): pack = lax.all_to_all(pack, ('y', 'z'), 0, 0, tiled=True)  11.9 us
    all_to_all x1, waiting for transfers between devices, per_device(): pair = lax.all_to_all(pair, FRAMES, 0, 0, tiled=True)  11 us
    all_to_all x1, starting transfers between devices, per_device(): pack = lax.all_to_all(pack, ('y', 'z'), 0, 0, tiled=True)  8.88 us
    pallas_call x1, Pallas kernels, attention(): pl.pallas_call(attention_kernel, out_shape=(pltpu.HBM((WIDTH, P_SIZE), BF...  8.76 us
    ppermute x1, starting transfers between devices, per_device(): other = lax.ppermute(own, 'h', swap)  5.26 us
    ppermute x1, starting transfers between devices, per_device(): got = lax.ppermute(sent, 'c', swap)  4.67 us
  transfers between devices with their start and end apart: 6, of which 5 were waited for; matrix products, arithmetic and copies ran while one was open for 1% of the time, Pallas kernels for 11%

profile of v8, /device:TPU:1, one launch (start us, length us, event | category | flops | bytes accessed | tf_op | source)
XLA Modules:
  0.0 109.0 jit_solution(2003797716259727805)
XLA Ops:
  0.6 0.0 copy-start.4
  0.7 0.7 copy-done.4
  1.3 1.5 %shard_map.110 = bf16[16,320]{1,0:T(8,128)(2,1)S(1)} custom-call(s32[1]{0:T(128)} %bitcast.1.at_ref, bf16[3,1280]{1,0:T(4,128)(2,1)S(1)} %copy-done.4, bf16[320,1280]{1,0:T(8,128)(2,1)} %bitcast.31), custom_call_target="tpu_custom_call" | custom-call | tf_op jit(solution)/shard_map/pallas_call | solution.py:85
  2.8 15.8 %all-gather = bf16[64,320]{1,0:T(8,128)(2,1)S(1)} all-gather(bf16[16,320]{1,0:T(8,128)(2,1)S(1)} %shard_map.110), channel_id=2, replica_groups=mesh['x'=4,'y'=8,'z'=4,'h'=2,'c'=2] {'h','c'}, dimensions={0}, use_global_device_ids=true | all-gather | bytes 51200 | tf_op jit(solution)/shard_map/all_gather | solution.py:373
  18.7 5.3 %collective-permute-start = (bf16[320,384]{1,0:T(8,128)(2,1)}, bf16[320,384]{1,0:T(8,128)(2,1)S(1)}, u32[]{:S(2)}, u32[]{:S(2)}) collective-permute-start(bf16[320,384]{1,0:T(8,128)(2,1)} %bitcast.32), channel_id=1, source_target_pairs={{0,2},{2,0},{1,3},{3,1},{4,6},{6,4},{5,7},{7,5},{8,10},{10,8},{9,1... | collective-permute-start | bytes 737288 | tf_op jit(solution)/shard_map/ppermute | solution.py:375
  24.0 0.0 copy-start.5
  24.0 3.0 %shard_map.112 = bf16[128,16,128]{2,1,0:T(8,128)(2,1)} custom-call(bf16[4,16,320]{2,1,0:T(8,128)(2,1)S(1)} %bitcast.30, bf16[320,1280]{1,0:T(8,128)(2,1)} %bitcast.23, bf16[320,1280]{1,0:T(8,128)(2,1)} %bitcast.26), custom_call_target="tpu_custom_call" | custom-call | flops 10000000000 | bytes 10000000000 | tf_op jit(solution)/shard_map/pallas_call | solution.py:124
  27.0 14.2 %all-to-all-start = ((bf16[128,16,128]{2,1,0:T(8,128)(2,1)}), bf16[128,16,128]{2,1,0:T(8,128)(2,1)S(1)}, u32[]{:S(2)}, u32[]{:S(2)}) async-start(bf16[128,16,128]{2,1,0:T(8,128)(2,1)} %shard_map.112), calls=%async_computation | async-start | bytes 1048576 | tf_op jit(solution)/shard_map/all_to_all | solution.py:377
  41.3 0.0 copy-start
  41.3 0.0 copy-start.1
  41.3 0.0 copy-start.2
  41.3 0.0 collective-permute-done
  41.3 0.0 copy-done.5
  41.3 0.1 pad_maximum_fusion
  41.4 3.0 %all-gather.1 = bf16[4,320,384]{2,1,0:T(8,128)(2,1)S(1)} all-gather(bf16[2,320,384]{2,1,0:T(8,128)(2,1)S(1)} %pad_maximum_fusion), channel_id=3, replica_groups=mesh['x'=4,'y'=8,'z'=4,'h'=2,'c'=2] {'c'}, dimensions={0}, use_global_device_ids=true | all-gather | bytes 1474560 | tf_op jit(solution)/shard_map/all_gather | solution.py:378
  44.4 0.0 copy-done
  44.4 0.0 copy-done.1
  44.4 0.0 copy-done.2
  44.4 0.0 copy-start.3
  44.4 2.7 %shard_map.111 = (bf16[1280,384]{1,0:T(8,128)(2,1)}, bf16[384,320]{1,0:T(8,128)(2,1)}, bf16[384,320]{1,0:T(8,128)(2,1)}, bf16[384,320]{1,0:T(8,128)(2,1)}) custom-call(s32[1]{0:T(128)} %bitcast.half_ref, bf16[2,2,320,384]{3,2,1,0:T(8,128)(2,1)S(1)} %bitcast.20, bf16[320,1280]{1,0:T(8,128)(2,1)S(1)} %bitcast.22, bf16[320,1280]{1,0:T(8,128)(2,1)S(1)} %bitcast.25, ...), custom_call_target="tpu_custom_call" | custom-call | flops 10000000000 | bytes 10000000000 | tf_op jit(solution)/shard_map/pallas_call | solution.py:56
  47.1 11.0 %all-to-all-done = bf16[128,16,128]{2,1,0:T(8,128)(2,1)S(1)} async-done(((bf16[128,16,128]{2,1,0:T(8,128)(2,1)}), bf16[128,16,128]{2,1,0:T(8,128)(2,1)S(1)}, u32[]{:S(2)}, u32[]{:S(2)}) %all-to-all-start) | async-done | bytes 524320 | tf_op jit(solution)/shard_map/all_to_all | solution.py:377
  58.1 0.0 copy-done.3
  58.1 8.8 %shard_map.113 = (bf16[320,384]{1,0:T(8,128)(2,1)}, bf16[384,320]{1,0:T(8,128)(2,1)}, bf16[384,320]{1,0:T(8,128)(2,1)}, bf16[384,320]{1,0:T(8,128)(2,1)}, bf16[4,256,640]{2,1,0:T(8,128)(2,1)}) custom-call(bf16[384,320]{1,0:T(8,128)(2,1)} %get-tuple-element.22.q_in, bf16[384,320]{1,0:T(8,128)(2,1)} %get-tuple-element.23.k_in, ...), custom_call_target="tpu_custom_call" | custom-call | tf_op jit(solution)/shard_map/pallas_call | solution.py:221
  66.9 3.7 %all-to-all-start.1 = ((bf16[4,256,640]{2,1,0:T(8,128)(2,1)}), bf16[4,256,640]{2,1,0:T(8,128)(2,1)S(1)}, u32[]{:S(2)}, u32[]{:S(2)}) async-start(bf16[4,256,640]{2,1,0:T(8,128)(2,1)} %get-tuple-element.33), calls=%async_computation.1 | async-start | bytes 2621440 | tf_op jit(solution)/shard_map/all_to_all | solution.py:383
  70.6 4.4 %shard_map.114 = (bf16[2,320,384]{2,1,0:T(8,128)(2,1)}, bf16[2,320,384]{2,1,0:T(8,128)(2,1)}) custom-call(s32[1]{0:T(128)} %bitcast.14.core_ref, bf16[384,320]{1,0:T(8,128)(2,1)} %get-tuple-element.28.dq_in, bf16[384,320]{1,0:T(8,128)(2,1)} %get-tuple-element.29.dk_in, bf16[384,320]{1,0:T(8,128)(2,1)} %get-tuple-element.30.dv_in, ...), custom_call_target="tpu_custom_call" | custom-call | flops 1 | bytes 1 | tf_op jit(solution)/shard_map/pallas_call | solution.py:281
  75.1 4.7 %collective-permute-start.1 = (bf16[2,320,384]{2,1,0:T(8,128)(2,1)}, bf16[2,320,384]{2,1,0:T(8,128)(2,1)S(1)}, u32[]{:S(2)}, u32[]{:S(2)}) collective-permute-start(bf16[2,320,384]{2,1,0:T(8,128)(2,1)} %get-tuple-element.32), channel_id=1, source_target_pairs={{0,1},{1,0},{2,3},{3,2},{4,5},{5,4},{6,7},{7,6},{8,9},{9,8},{10,11... | collective-permute-start | bytes 1474568 | tf_op jit(solution)/shard_map/ppermute | solution.py:385
  79.7 1.7 %collective-permute-done.1 = bf16[2,320,384]{2,1,0:T(8,128)(2,1)S(1)} collective-permute-done((bf16[2,320,384]{2,1,0:T(8,128)(2,1)}, bf16[2,320,384]{2,1,0:T(8,128)(2,1)S(1)}, u32[]{:S(2)}, u32[]{:S(2)}) %collective-permute-start.1) | collective-permute-done | bytes 491552 | tf_op jit(solution)/shard_map/ppermute | solution.py:385
  81.4 1.1 %add_convert_fusion.pair_ref = bf16[2,320,384]{2,1,0:T(8,128)(2,1)S(1)} fusion(bf16[2,320,384]{2,1,0:T(8,128)(2,1)S(1)} %collective-permute-done.1, bf16[2,320,384]{2,1,0:T(8,128)(2,1)} %get-tuple-element.31), kind=kLoop, calls=%fused_computation | loop fusion | flops 983040 | bytes 1474560 | tf_op jit(solution)/shard_map/convert_element_type | solution.py:386
  82.6 1.9 %collective-permute-start.2 = (bf16[320,384]{1,0:T(8,128)(2,1)S(1)}, bf16[320,384]{1,0:T(8,128)(2,1)S(1)}, u32[]{:S(2)}, u32[]{:S(2)}) collective-permute-start(bf16[320,384]{1,0:T(8,128)(2,1)S(1)} %dynamic-slice_bitcast_fusion), channel_id=1, source_target_pairs={{0,2},{2,0},{1,3},{3,1},{4,6},{6,4},{5,7},{7,5},{8,10},{10,8},{9,1... | collective-permute-start | bytes 737288 | tf_op jit(solution)/shard_map/ppermute | solution.py:388
  84.5 1.0 all-to-all-done.1.in_ref
  85.6 1.0 shard_map.116
  86.6 8.9 %all-to-all-start.2 = ((bf16[32,8,640]{2,1,0:T(8,128)(2,1)}), bf16[32,8,640]{2,1,0:T(8,128)(2,1)S(1)}, u32[]{:S(2)}, u32[]{:S(2)}) async-start(bf16[32,8,640]{2,1,0:T(8,128)(2,1)} %bitcast.17), calls=%async_computation.2 | async-start | bytes 655360 | tf_op jit(solution)/shard_map/all_to_all | solution.py:392
  95.5 0.1 collective-permute-done.2.got_ref
  95.6 0.8 shard_map.115
  96.4 11.9 %all-to-all-done.2.in_ref = bf16[32,8,640]{2,1,0:T(8,128)(2,1)S(1)} async-done(((bf16[32,8,640]{2,1,0:T(8,128)(2,1)}), bf16[32,8,640]{2,1,0:T(8,128)(2,1)S(1)}, u32[]{:S(2)}, u32[]{:S(2)}) %all-to-all-start.2) | async-done | bytes 327712 | tf_op jit(solution)/shard_map/all_to_all | solution.py:392
  108.3 0.7 shard_map.117
  (1 shorter events, 0.0 us)
Async XLA Ops:
  0.6 0.7 copy-start.4
  18.7 22.6 %collective-permute-start = (bf16[320,384]{1,0:T(8,128)(2,1)}, bf16[320,384]{1,0:T(8,128)(2,1)S(1)}, u32[]{:S(2)}, u32[]{:S(2)}) collective-permute-start(bf16[320,384]{1,0:T(8,128)(2,1)} %bitcast.32), channel_id=1, source_target_pairs={{0,2},{2,0},{1,3},{3,1},{4,6},{6,4},{5,7},{7,5},{8,10},{10,8},{9,1... | collective-permute-start | bytes 737288 | tf_op jit(solution)/shard_map/ppermute | solution.py:375
  24.0 17.3 %copy-start.5 = (bf16[384,320]{0,1:T(8,128)(2,1)S(1)}, bf16[384,320]{0,1:T(8,128)(2,1)}, u32[]{:S(2)}) copy-start(bf16[384,320]{0,1:T(8,128)(2,1)} %param.7) | copy-start | bytes 737284
  27.0 31.1 %all-to-all-start = ((bf16[128,16,128]{2,1,0:T(8,128)(2,1)}), bf16[128,16,128]{2,1,0:T(8,128)(2,1)S(1)}, u32[]{:S(2)}, u32[]{:S(2)}) async-start(bf16[128,16,128]{2,1,0:T(8,128)(2,1)} %shard_map.112), calls=%async_computation | async-start | bytes 1048576 | tf_op jit(solution)/shard_map/all_to_all | solution.py:377
  41.3 3.1 %copy-start = (bf16[1280,320]{0,1:T(8,128)(2,1)S(1)}, bf16[1280,320]{0,1:T(8,128)(2,1)}, u32[]{:S(2)}) copy-start(bf16[1280,320]{0,1:T(8,128)(2,1)} %param.9) | copy-start | bytes 2457604
  41.3 3.1 %copy-start.1 = (bf16[1280,320]{0,1:T(8,128)(2,1)S(1)}, bf16[1280,320]{0,1:T(8,128)(2,1)}, u32[]{:S(2)}) copy-start(bf16[1280,320]{0,1:T(8,128)(2,1)} %param.10) | copy-start | bytes 2457604
  41.3 3.1 %copy-start.2 = (bf16[1280,320]{0,1:T(8,128)(2,1)S(1)}, bf16[1280,320]{0,1:T(8,128)(2,1)}, u32[]{:S(2)}) copy-start(bf16[1280,320]{0,1:T(8,128)(2,1)} %param.11) | copy-start | bytes 2457604
  44.4 13.7 %copy-start.3 = (bf16[384,320]{0,1:T(8,128)(2,1)S(1)}, bf16[384,320]{0,1:T(8,128)(2,1)}, u32[]{:S(2)}) copy-start(bf16[384,320]{0,1:T(8,128)(2,1)} %param.13) | copy-start | bytes 737284
  66.9 18.7 %all-to-all-start.1 = ((bf16[4,256,640]{2,1,0:T(8,128)(2,1)}), bf16[4,256,640]{2,1,0:T(8,128)(2,1)S(1)}, u32[]{:S(2)}, u32[]{:S(2)}) async-start(bf16[4,256,640]{2,1,0:T(8,128)(2,1)} %get-tuple-element.33), calls=%async_computation.1 | async-start | bytes 2621440 | tf_op jit(solution)/shard_map/all_to_all | solution.py:383
  75.1 6.4 %collective-permute-start.1 = (bf16[2,320,384]{2,1,0:T(8,128)(2,1)}, bf16[2,320,384]{2,1,0:T(8,128)(2,1)S(1)}, u32[]{:S(2)}, u32[]{:S(2)}) collective-permute-start(bf16[2,320,384]{2,1,0:T(8,128)(2,1)} %get-tuple-element.32), channel_id=1, source_target_pairs={{0,1},{1,0},{2,3},{3,2},{4,5},{5,4},{6,7},{7,6},{8,9},{9,8},{10,11... | collective-permute-start | bytes 1474568 | tf_op jit(solution)/shard_map/ppermute | solution.py:385
  82.6 13.0 %collective-permute-start.2 = (bf16[320,384]{1,0:T(8,128)(2,1)S(1)}, bf16[320,384]{1,0:T(8,128)(2,1)S(1)}, u32[]{:S(2)}, u32[]{:S(2)}) collective-permute-start(bf16[320,384]{1,0:T(8,128)(2,1)S(1)} %dynamic-slice_bitcast_fusion), channel_id=1, source_target_pairs={{0,2},{2,0},{1,3},{3,1},{4,6},{6,4},{5,7},{7,5},{8,10},{10,8},{9,1... | collective-permute-start | bytes 737288 | tf_op jit(solution)/shard_map/ppermute | solution.py:388
  86.6 21.7 %all-to-all-start.2 = ((bf16[32,8,640]{2,1,0:T(8,128)(2,1)}), bf16[32,8,640]{2,1,0:T(8,128)(2,1)S(1)}, u32[]{:S(2)}, u32[]{:S(2)}) async-start(bf16[32,8,640]{2,1,0:T(8,128)(2,1)} %bitcast.17), calls=%async_computation.2 | async-start | bytes 655360 | tf_op jit(solution)/shard_map/all_to_all | solution.py:392

commit v9 on v8

--- a/solution.py
+++ b/solution.py
@@ -12,9 +12,12 @@
 P_SIZE = 384
 HEADS = 5
 WIDTH = HEADS * E
-FRAMES = ("x", "y", "z")
+FRAMES = ("x", "yh", "yl", "z")
+FIRST = ("x", "yl")
+SECOND = ("yh", "z")
 TENSOR = ("h", "c")
-NX, NYZ = 4, 32
+N_FIRST, N_SECOND = 8, 16
+N_FRAMES = N_FIRST * N_SECOND
 REF_ROWS = 3
 ROWS_OUT = 10
 HALF_ROWS = ROWS_OUT // 2
@@ -25,6 +28,10 @@
 SCALE = 1.0 / math.sqrt(E)
 F32 = jnp.float32
 BF16 = jnp.bfloat16
+
+
+def pick(rows, low):
+    return jnp.concatenate([rows[8 * i + 4 * low : 8 * i + 4 * low + 4] for i in range(4)], axis=0)
 
 
 def dot(a, b, a_dim, b_dim):
@@ -123,7 +130,7 @@
     hbm, vmem = [pl.BlockSpec(memory_space=space) for space in (pltpu.HBM, pltpu.VMEM)]
     return pl.pallas_call(
         ref_kernel,
-        out_shape=jax.ShapeDtypeStruct((NX * NYZ, 16, LANES), BF16),
+        out_shape=jax.ShapeDtypeStruct((N_FRAMES, 16, LANES), BF16),
         in_specs=[vmem, hbm, hbm],
         out_specs=vmem,
         scratch_shapes=[pltpu.VMEM((16, LANES), F32)]
@@ -139,7 +146,6 @@
     q_ref, k_ref, v_ref, tok_ref, wide_ref, r_ref, dqt_ref, dw_ref,
     ot_ref, dq_ref, dk_ref, dv_ref, pack_ref, in_sem, out_sem,
 ):
-    n_frames = NX * NYZ
     pairs = ((k_in, k_ref), (q_in, q_ref), (v_in, v_ref), (tok_in, tok_ref))
     loads = [pltpu.make_async_copy(a, b, in_sem.at[i]) for i, (a, b) in enumerate(pairs)]
     for load in loads:
@@ -147,8 +153,8 @@
     wide_ref[...] = pair_ref[...].astype(F32)
     for row in range(REF_ROWS):
         for group in range(GROUPS):
-            r_ref[n_frames * row : n_frames * (row + 1), LANES * group : LANES * (group + 1)] = (
-                wide_ref[pl.ds(row * GROUPS + group, n_frames, stride=16), :].astype(BF16)
+            r_ref[N_FRAMES * row : N_FRAMES * (row + 1), LANES * group : LANES * (group + 1)] = (
+                wide_ref[pl.ds(row * GROUPS + group, N_FRAMES, stride=16), :].astype(BF16)
             )
     g_all = gt_ref[...].astype(F32).T.astype(BF16)
     for load in loads[:3]:
@@ -176,11 +182,12 @@
         dk_ref[:, lo:hi] = dk[:P_SIZE].astype(BF16)
         dv_ref[:, lo:hi] = dv[:P_SIZE].astype(BF16)
         for col, part in ((lo, dk), (WIDTH + lo, dv)):
-            for x in range(NX):
+            for chunk in range(N_FIRST):
                 for row in range(REF_ROWS):
-                    at = P_SIZE + n_frames * row + NYZ * x
-                    pack_ref[x, NYZ * row : NYZ * (row + 1), col : col + E] = part[
-                        at : at + NYZ
+                    at = P_SIZE + N_FRAMES * row + N_SECOND * chunk
+                    to = N_SECOND * row
+                    pack_ref[chunk, to : to + N_SECOND, col : col + E] = part[
+                        at : at + N_SECOND
                     ].astype(BF16)
 
     ahead = scores(0)
@@ -193,24 +200,30 @@
     dq_ref[...] = dq
     loads[3].wait()
     pairs = ((ot_ref, ot_out), (dq_ref, dq_out), (dk_ref, dk_out), (dv_ref, dv_out))
-    stores = [pltpu.make_async_copy(a, b, out_sem.at[NX + i]) for i, (a, b) in enumerate(pairs)]
+    stores = [pltpu.make_async_copy(a, b, out_sem.at[N_FIRST + i]) for i, (a, b) in enumerate(pairs)]
     for store in stores:
         store.start()
-    for x in range(NX):
+    for x in range(4):
         dw = dot(tok_ref[x * WIDTH : (x + 1) * WIDTH, :], dq, 1, 0)
         dw_ref[0], dw_ref[1] = dw[:, :LANES], dw[:, LANES : 2 * LANES]
         dw_ref[2, :, :E] = dw[:, 2 * LANES :]
         for row in range(HALF_ROWS):
-            at = NYZ * (REF_ROWS + row)
             left, right = [
-                [dw_ref[group, pl.ds(first, NYZ, stride=ROWS_OUT), :] for group in range(3)]
+                [dw_ref[group, pl.ds(first, 32, stride=ROWS_OUT), :] for group in range(3)]
                 for first in (row, row + HALF_ROWS)
             ]
             last = jnp.concatenate([left[2][:, :E], right[2][:, :E]], axis=1)
+            at = N_SECOND * (REF_ROWS + row)
             for group, part in enumerate((left[0], left[1], right[0], right[1], last)):
-                pack_ref[x, at : at + NYZ, LANES * group : LANES * (group + 1)] = part.astype(BF16)
-        stores.append(pltpu.make_async_copy(pack_ref.at[x], pack_out.at[x], out_sem.at[x]))
-        stores[-1].start()
+                for low in range(2):
+                    pack_ref[
+                        2 * x + low, at : at + N_SECOND, LANES * group : LANES * (group + 1)
+                    ] = pick(part, low).astype(BF16)
+        for chunk in (2 * x, 2 * x + 1):
+            stores.append(
+                pltpu.make_async_copy(pack_ref.at[chunk], pack_out.at[chunk], out_sem.at[chunk])
+            )
+            stores[-1].start()
     for store in stores:
         store.wait()
 
@@ -222,13 +235,13 @@
         attention_kernel,
         out_shape=(pltpu.HBM((WIDTH, P_SIZE), BF16),)
         + (pltpu.HBM((P_SIZE, WIDTH), BF16),) * 3
-        + (pltpu.HBM((NX, NYZ * rows, 2 * WIDTH), BF16),),
+        + (pltpu.HBM((N_FIRST, N_SECOND * rows, 2 * WIDTH), BF16),),
         in_specs=[hbm] * 4 + [vmem] * 2,
         out_specs=[hbm] * 5,
         scratch_shapes=[pltpu.VMEM((P_SIZE, WIDTH), BF16)] * 3
         + [
             pltpu.VMEM((4 * WIDTH, P_SIZE), BF16),
-            pltpu.VMEM((NX * NYZ * 16, LANES), F32),
+            pltpu.VMEM((N_FRAMES * 16, LANES), F32),
             pltpu.VMEM((P_SIZE, 2 * WIDTH), BF16),
             pltpu.VMEM((WIDTH, P_SIZE), F32),
             pltpu.VMEM((3, WIDTH, LANES), F32),
@@ -236,9 +249,9 @@
             pltpu.VMEM((P_SIZE, WIDTH), BF16),
             pltpu.VMEM((P_SIZE, WIDTH), BF16),
             pltpu.VMEM((P_SIZE, WIDTH), BF16),
-            pltpu.VMEM((NX, NYZ * rows, 2 * WIDTH), BF16),
+            pltpu.VMEM((N_FIRST, N_SECOND * rows, 2 * WIDTH), BF16),
             pltpu.SemaphoreType.DMA((4,)),
-            pltpu.SemaphoreType.DMA((NX + 4,)),
+            pltpu.SemaphoreType.DMA((N_FIRST + 4,)),
         ],
         compiler_params=pltpu.CompilerParams(vmem_limit_bytes=VMEM_BYTES),
     )(*[pltpu.with_memory_space_constraint(a, pltpu.HBM) for a in (q, k, v, tok)], pair, gt)
@@ -315,12 +328,12 @@
 def regroup_kernel(in_ref, out_ref, held_ref):
     rows = REF_ROWS + HALF_ROWS
     for row in range(rows):
-        at = NYZ * row
-        part = in_ref[0, at : at + NYZ, :].astype(F32)
-        for x in range(1, NX):
-            part = part + in_ref[x, at : at + NYZ, :].astype(F32)
+        at = N_SECOND * row
+        part = in_ref[0, at : at + N_SECOND, :].astype(F32)
+        for x in range(1, N_FIRST):
+            part = part + in_ref[x, at : at + N_SECOND, :].astype(F32)
         for group in range(GROUPS):
-            held_ref[group, pl.ds(row, NYZ, stride=rows), :] = part[
+            held_ref[group, pl.ds(row, N_SECOND, stride=rows), :] = part[
                 :, LANES * group : LANES * (group + 1)
             ]
     for group in range(GROUPS):
@@ -331,8 +344,8 @@
     rows = REF_ROWS + HALF_ROWS
     return pl.pallas_call(
         regroup_kernel,
-        out_shape=jax.ShapeDtypeStruct((NYZ * rows, 2 * WIDTH), BF16),
-        scratch_shapes=[pltpu.VMEM((GROUPS, NYZ * rows, LANES), F32)],
+        out_shape=jax.ShapeDtypeStruct((N_SECOND * rows, 2 * WIDTH), BF16),
+        scratch_shapes=[pltpu.VMEM((GROUPS, N_SECOND * rows, LANES), F32)],
         cost_estimate=LONG,
         compiler_params=pltpu.CompilerParams(vmem_limit_bytes=8 * 1024 * 1024),
     )(parts)
@@ -340,7 +353,7 @@
 
 def finish_kernel(in_ref, grad_ref, key_ref, value_ref):
     total = in_ref[0].astype(F32)
-    for j in range(1, NYZ):
+    for j in range(1, N_SECOND):
         total = total + in_ref[j].astype(F32)
     key_ref[...] = total[:REF_ROWS, :WIDTH].astype(BF16)
     value_ref[...] = total[:REF_ROWS, WIDTH:].astype(BF16)
@@ -374,13 +387,13 @@
     ref_hidden, own = lax.optimization_barrier((ref_hidden, tokens.T))
     other = lax.ppermute(own, "h", swap)
     pair = ref_pair(ref_hidden, wk, wv)
-    pair = lax.all_to_all(pair, FRAMES, 0, 0, tiled=True)
+    pair = lax.all_to_all(pair, FIRST + SECOND, 0, 0, tiled=True)
     parts = lax.all_gather(jnp.stack([own, other]), "c", axis=0, tiled=False)
     tok, queries, keys, values = project(half, parts, wq, wk, wv)
     attended, query_grads, key_grads, value_grads, pack = attention(
-        queries, keys, values, pair.reshape(NX * NYZ * 16, LANES), cotangent.T, tok
+        queries, keys, values, pair.reshape(N_FRAMES * 16, LANES), cotangent.T, tok
     )
-    pack = lax.all_to_all(pack, "x", 0, 0, tiled=True)
+    pack = lax.all_to_all(pack, FIRST, 0, 0, tiled=True)
     kept, sent = token_parts(core, query_grads, key_grads, value_grads, wq, wk, wv)
     got = lax.ppermute(sent, "c", swap)
     paired = (kept.astype(F32) + got.astype(F32)).astype(BF16)
@@ -388,14 +401,14 @@
     got = lax.ppermute(sent, "h", swap)
     token_grads = combine(half, paired, got).T
     pack = regroup(pack)
-    pack = pack.reshape(NYZ, REF_ROWS + HALF_ROWS, 2 * WIDTH)
-    pack = lax.all_to_all(pack, ("y", "z"), 0, 0, tiled=True)
+    pack = pack.reshape(N_SECOND, REF_ROWS + HALF_ROWS, 2 * WIDTH)
+    pack = lax.all_to_all(pack, SECOND, 0, 0, tiled=True)
     query_weight_grad, ref_key_grads, ref_value_grads = finish(pack)
     return attended.T, token_grads, query_weight_grad, ref_key_grads, ref_value_grads
 
 
 def solution(mesh):
-    mesh = Mesh(mesh.devices.reshape(4, 8, 4, 2, 2), FRAMES + TENSOR)
+    mesh = Mesh(mesh.devices.reshape(4, 4, 2, 4, 2, 2), FRAMES + TENSOR)
     return jax.shard_map(
         per_device,
         mesh=mesh,

time: 110 us -> 107 us (0.973)
  waiting for transfers between devices: 25.7 us -> 23.6 us
    all_to_all x3, waiting for transfers between devices: 24 us -> 18 us  [the longest x1 11.9 us: per_device(): pair = lax.all_to_all(pair, FIRST + SECOND, 0, 0, tiled=True)]
    ppermute x1, waiting for transfers between devices: 0.09 us -> 3.91 us  [per_device(): got = lax.ppermute(sent, 'h', swap)]
where the time goes in v9:
time: 107 us; the launch traced here: 106 us
  starting transfers between devices  38.3 us (36%)
  waiting for transfers between devices  23.6 us (22%)
  Pallas kernels  22.8 us (21%)
  blocking collectives  18.8 us (18%)
  other arithmetic  1.21 us (1%)
    all_gather x1, blocking collectives, per_device(): ref_hidden = lax.all_gather(cols, TENSOR, axis=0, tiled=False)  15.8 us
    all_to_all x1, starting transfers between devices, per_device(): pair = lax.all_to_all(pair, FIRST + SECOND, 0, 0, tiled=True)  14.2 us
    all_to_all x1, waiting for transfers between devices, per_device(): pair = lax.all_to_all(pair, FIRST + SECOND, 0, 0, tiled=True)  11.9 us
    pallas_call x1, Pallas kernels, attention(): pl.pallas_call(attention_kernel, out_shape=(pltpu.HBM((WIDTH, P_SIZE), BF...  8.72 us
    all_to_all x1, starting transfers between devices, per_device(): pack = lax.all_to_all(pack, SECOND, 0, 0, tiled=True)  7.87 us
    all_to_all x1, waiting for transfers between devices, per_device(): pack = lax.all_to_all(pack, SECOND, 0, 0, tiled=True)  5.41 us
    ppermute x1, starting transfers between devices, per_device(): other = lax.ppermute(own, 'h', swap)  5.26 us
    ppermute x1, starting transfers between devices, per_device(): got = lax.ppermute(sent, 'c', swap)  5.14 us
  transfers between devices with their start and end apart: 6, of which 5 were waited for; matrix products, arithmetic and copies ran while one was open for 1% of the time, Pallas kernels for 11%

profile of v9, /device:TPU:1, one launch (start us, length us, event | category | flops | bytes accessed | tf_op | source)
XLA Modules:
  0.0 106.3 jit_solution(13359706794663212132)
XLA Ops:
  0.6 0.0 copy-start.4
  0.7 0.7 copy-done.4
  1.3 1.5 %shard_map.110 = bf16[16,320]{1,0:T(8,128)(2,1)S(1)} custom-call(s32[1]{0:T(128)} %bitcast.1.at_ref, bf16[3,1280]{1,0:T(4,128)(2,1)S(1)} %copy-done.4, bf16[320,1280]{1,0:T(8,128)(2,1)} %bitcast.31), custom_call_target="tpu_custom_call" | custom-call | tf_op jit(solution)/shard_map/pallas_call | solution.py:92
  2.8 15.8 %all-gather = bf16[64,320]{1,0:T(8,128)(2,1)S(1)} all-gather(bf16[16,320]{1,0:T(8,128)(2,1)S(1)} %shard_map.110), channel_id=2, replica_groups=mesh['x'=4,'yh'=4,'yl'=2,'z'=4,'h'=2,'c'=2] {'h','c'}, dimensions={0}, use_global_device_ids=true | all-gather | bytes 51200 | tf_op jit(solution)/shard_map/all_gather | solution.py:386
  18.7 5.3 %collective-permute-start = (bf16[320,384]{1,0:T(8,128)(2,1)}, bf16[320,384]{1,0:T(8,128)(2,1)S(1)}, u32[]{:S(2)}, u32[]{:S(2)}) collective-permute-start(bf16[320,384]{1,0:T(8,128)(2,1)} %bitcast.32), channel_id=1, source_target_pairs={{0,2},{2,0},{1,3},{3,1},{4,6},{6,4},{5,7},{7,5},{8,10},{10,8},{9,1... | collective-permute-start | bytes 737288 | tf_op jit(solution)/shard_map/ppermute | solution.py:388
  24.0 0.0 copy-start.5
  24.0 3.0 %shard_map.112 = bf16[128,16,128]{2,1,0:T(8,128)(2,1)} custom-call(bf16[4,16,320]{2,1,0:T(8,128)(2,1)S(1)} %bitcast.30, bf16[320,1280]{1,0:T(8,128)(2,1)} %bitcast.23, bf16[320,1280]{1,0:T(8,128)(2,1)} %bitcast.26), custom_call_target="tpu_custom_call" | custom-call | flops 10000000000 | bytes 10000000000 | tf_op jit(solution)/shard_map/pallas_call | solution.py:131
  27.0 14.2 %all-to-all-start = ((bf16[128,16,128]{2,1,0:T(8,128)(2,1)}), bf16[128,16,128]{2,1,0:T(8,128)(2,1)S(1)}, u32[]{:S(2)}, u32[]{:S(2)}) async-start(bf16[128,16,128]{2,1,0:T(8,128)(2,1)} %shard_map.112), calls=%async_computation | async-start | bytes 1048576 | tf_op jit(solution)/shard_map/all_to_all | solution.py:390
  41.3 0.0 copy-start
  41.3 0.0 copy-start.1
  41.3 0.0 copy-start.2
  41.3 0.0 collective-permute-done
  41.3 0.0 copy-done.5
  41.3 0.1 pad_maximum_fusion
  41.4 3.0 %all-gather.1 = bf16[4,320,384]{2,1,0:T(8,128)(2,1)S(1)} all-gather(bf16[2,320,384]{2,1,0:T(8,128)(2,1)S(1)} %pad_maximum_fusion), channel_id=3, replica_groups=mesh['x'=4,'yh'=4,'yl'=2,'z'=4,'h'=2,'c'=2] {'c'}, dimensions={0}, use_global_device_ids=true | all-gather | bytes 1474560 | tf_op jit(solution)/shard_map/all_gather | solution.py:391
  44.4 0.0 copy-done
  44.4 0.0 copy-done.1
  44.4 0.0 copy-done.2
  44.4 0.0 copy-start.3
  44.4 2.7 %shard_map.111 = (bf16[1280,384]{1,0:T(8,128)(2,1)}, bf16[384,320]{1,0:T(8,128)(2,1)}, bf16[384,320]{1,0:T(8,128)(2,1)}, bf16[384,320]{1,0:T(8,128)(2,1)}) custom-call(s32[1]{0:T(128)} %bitcast.half_ref, bf16[2,2,320,384]{3,2,1,0:T(8,128)(2,1)S(1)} %bitcast.20, bf16[320,1280]{1,0:T(8,128)(2,1)S(1)} %bitcast.22, bf16[320,1280]{1,0:T(8,128)(2,1)S(1)} %bitcast.25, ...), custom_call_target="tpu_custom_call" | custom-call | flops 10000000000 | bytes 10000000000 | tf_op jit(solution)/shard_map/pallas_call | solution.py:63
  47.1 11.9 %all-to-all-done = bf16[128,16,128]{2,1,0:T(8,128)(2,1)S(1)} async-done(((bf16[128,16,128]{2,1,0:T(8,128)(2,1)}), bf16[128,16,128]{2,1,0:T(8,128)(2,1)S(1)}, u32[]{:S(2)}, u32[]{:S(2)}) %all-to-all-start) | async-done | bytes 524320 | tf_op jit(solution)/shard_map/all_to_all | solution.py:390
  59.0 0.0 copy-done.3
  59.0 8.7 %shard_map.113 = (bf16[320,384]{1,0:T(8,128)(2,1)}, bf16[384,320]{1,0:T(8,128)(2,1)}, bf16[384,320]{1,0:T(8,128)(2,1)}, bf16[384,320]{1,0:T(8,128)(2,1)}, bf16[8,128,640]{2,1,0:T(8,128)(2,1)}) custom-call(bf16[384,320]{1,0:T(8,128)(2,1)} %get-tuple-element.22.q_in, bf16[384,320]{1,0:T(8,128)(2,1)} %get-tuple-element.23.k_in, ...), custom_call_target="tpu_custom_call" | custom-call | tf_op jit(solution)/shard_map/pallas_call | solution.py:234
  67.8 3.8 %all-to-all-start.1 = ((bf16[8,128,640]{2,1,0:T(8,128)(2,1)}), bf16[8,128,640]{2,1,0:T(8,128)(2,1)S(1)}, u32[]{:S(2)}, u32[]{:S(2)}) async-start(bf16[8,128,640]{2,1,0:T(8,128)(2,1)} %get-tuple-element.33), calls=%async_computation.1 | async-start | bytes 2621440 | tf_op jit(solution)/shard_map/all_to_all | solution.py:396
  71.5 4.4 %shard_map.114 = (bf16[2,320,384]{2,1,0:T(8,128)(2,1)}, bf16[2,320,384]{2,1,0:T(8,128)(2,1)}) custom-call(s32[1]{0:T(128)} %bitcast.14.core_ref, bf16[384,320]{1,0:T(8,128)(2,1)} %get-tuple-element.28.dq_in, bf16[384,320]{1,0:T(8,128)(2,1)} %get-tuple-element.29.dk_in, bf16[384,320]{1,0:T(8,128)(2,1)} %get-tuple-element.30.dv_in, ...), custom_call_target="tpu_custom_call" | custom-call | flops 1 | bytes 1 | tf_op jit(solution)/shard_map/pallas_call | solution.py:294
  76.0 5.1 %collective-permute-start.1 = (bf16[2,320,384]{2,1,0:T(8,128)(2,1)}, bf16[2,320,384]{2,1,0:T(8,128)(2,1)S(1)}, u32[]{:S(2)}, u32[]{:S(2)}) collective-permute-start(bf16[2,320,384]{2,1,0:T(8,128)(2,1)} %get-tuple-element.32), channel_id=1, source_target_pairs={{0,1},{1,0},{2,3},{3,2},{4,5},{5,4},{6,7},{7,6},{8,9},{9,8},{10,11... | collective-permute-start | bytes 1474568 | tf_op jit(solution)/shard_map/ppermute | solution.py:398
  81.1 1.7 %collective-permute-done.1 = bf16[2,320,384]{2,1,0:T(8,128)(2,1)S(1)} collective-permute-done((bf16[2,320,384]{2,1,0:T(8,128)(2,1)}, bf16[2,320,384]{2,1,0:T(8,128)(2,1)S(1)}, u32[]{:S(2)}, u32[]{:S(2)}) %collective-permute-start.1) | collective-permute-done | bytes 491552 | tf_op jit(solution)/shard_map/ppermute | solution.py:398
  82.8 1.1 %add_convert_fusion.pair_ref = bf16[2,320,384]{2,1,0:T(8,128)(2,1)S(1)} fusion(bf16[2,320,384]{2,1,0:T(8,128)(2,1)S(1)} %collective-permute-done.1, bf16[2,320,384]{2,1,0:T(8,128)(2,1)} %get-tuple-element.31), kind=kLoop, calls=%fused_computation | loop fusion | flops 983040 | bytes 1474560 | tf_op jit(solution)/shard_map/convert_element_type | solution.py:399
  84.0 2.0 %collective-permute-start.2 = (bf16[320,384]{1,0:T(8,128)(2,1)S(1)}, bf16[320,384]{1,0:T(8,128)(2,1)S(1)}, u32[]{:S(2)}, u32[]{:S(2)}) collective-permute-start(bf16[320,384]{1,0:T(8,128)(2,1)S(1)} %dynamic-slice_bitcast_fusion), channel_id=1, source_target_pairs={{0,2},{2,0},{1,3},{3,1},{4,6},{6,4},{5,7},{7,5},{8,10},{10,8},{9,1... | collective-permute-start | bytes 737288 | tf_op jit(solution)/shard_map/ppermute | solution.py:401
  86.0 0.7 all-to-all-done.1.in_ref
  86.7 0.9 shard_map.116
  87.6 7.9 %all-to-all-start.2 = ((bf16[16,8,640]{2,1,0:T(8,128)(2,1)}), bf16[16,8,640]{2,1,0:T(8,128)(2,1)S(1)}, u32[]{:S(2)}, u32[]{:S(2)}) async-start(bf16[16,8,640]{2,1,0:T(8,128)(2,1)} %bitcast.17), calls=%async_computation.2 | async-start | bytes 327680 | tf_op jit(solution)/shard_map/all_to_all | solution.py:405
  95.5 3.9 %collective-permute-done.2.got_ref = bf16[320,384]{1,0:T(8,128)(2,1)S(1)} collective-permute-done((bf16[320,384]{1,0:T(8,128)(2,1)S(1)}, bf16[320,384]{1,0:T(8,128)(2,1)S(1)}, u32[]{:S(2)}, u32[]{:S(2)}) %collective-permute-start.2) | collective-permute-done | bytes 245792 | tf_op jit(solution)/shard_map/ppermute | solution.py:401
  99.4 0.8 shard_map.115
  100.1 5.4 %all-to-all-done.2.in_ref = bf16[16,8,640]{2,1,0:T(8,128)(2,1)S(1)} async-done(((bf16[16,8,640]{2,1,0:T(8,128)(2,1)}), bf16[16,8,640]{2,1,0:T(8,128)(2,1)S(1)}, u32[]{:S(2)}, u32[]{:S(2)}) %all-to-all-start.2) | async-done | bytes 163872 | tf_op jit(solution)/shard_map/all_to_all | solution.py:405
  105.6 0.7 shard_map.117
  (1 shorter events, 0.0 us)
Async XLA Ops:
  0.6 0.7 copy-start.4
  18.7 22.6 %collective-permute-start = (bf16[320,384]{1,0:T(8,128)(2,1)}, bf16[320,384]{1,0:T(8,128)(2,1)S(1)}, u32[]{:S(2)}, u32[]{:S(2)}) collective-permute-start(bf16[320,384]{1,0:T(8,128)(2,1)} %bitcast.32), channel_id=1, source_target_pairs={{0,2},{2,0},{1,3},{3,1},{4,6},{6,4},{5,7},{7,5},{8,10},{10,8},{9,1... | collective-permute-start | bytes 737288 | tf_op jit(solution)/shard_map/ppermute | solution.py:388
  24.0 17.3 %copy-start.5 = (bf16[384,320]{0,1:T(8,128)(2,1)S(1)}, bf16[384,320]{0,1:T(8,128)(2,1)}, u32[]{:S(2)}) copy-start(bf16[384,320]{0,1:T(8,128)(2,1)} %param.7) | copy-start | bytes 737284
  27.0 32.0 %all-to-all-start = ((bf16[128,16,128]{2,1,0:T(8,128)(2,1)}), bf16[128,16,128]{2,1,0:T(8,128)(2,1)S(1)}, u32[]{:S(2)}, u32[]{:S(2)}) async-start(bf16[128,16,128]{2,1,0:T(8,128)(2,1)} %shard_map.112), calls=%async_computation | async-start | bytes 1048576 | tf_op jit(solution)/shard_map/all_to_all | solution.py:390
  41.3 3.1 %copy-start = (bf16[1280,320]{0,1:T(8,128)(2,1)S(1)}, bf16[1280,320]{0,1:T(8,128)(2,1)}, u32[]{:S(2)}) copy-start(bf16[1280,320]{0,1:T(8,128)(2,1)} %param.9) | copy-start | bytes 2457604
  41.3 3.1 %copy-start.1 = (bf16[1280,320]{0,1:T(8,128)(2,1)S(1)}, bf16[1280,320]{0,1:T(8,128)(2,1)}, u32[]{:S(2)}) copy-start(bf16[1280,320]{0,1:T(8,128)(2,1)} %param.10) | copy-start | bytes 2457604
  41.3 3.1 %copy-start.2 = (bf16[1280,320]{0,1:T(8,128)(2,1)S(1)}, bf16[1280,320]{0,1:T(8,128)(2,1)}, u32[]{:S(2)}) copy-start(bf16[1280,320]{0,1:T(8,128)(2,1)} %param.11) | copy-start | bytes 2457604
  44.4 14.7 %copy-start.3 = (bf16[384,320]{0,1:T(8,128)(2,1)S(1)}, bf16[384,320]{0,1:T(8,128)(2,1)}, u32[]{:S(2)}) copy-start(bf16[384,320]{0,1:T(8,128)(2,1)} %param.13) | copy-start | bytes 737284
  67.8 18.9 %all-to-all-start.1 = ((bf16[8,128,640]{2,1,0:T(8,128)(2,1)}), bf16[8,128,640]{2,1,0:T(8,128)(2,1)S(1)}, u32[]{:S(2)}, u32[]{:S(2)}) async-start(bf16[8,128,640]{2,1,0:T(8,128)(2,1)} %get-tuple-element.33), calls=%async_computation.1 | async-start | bytes 2621440 | tf_op jit(solution)/shard_map/all_to_all | solution.py:396
  76.0 6.8 %collective-permute-start.1 = (bf16[2,320,384]{2,1,0:T(8,128)(2,1)}, bf16[2,320,384]{2,1,0:T(8,128)(2,1)S(1)}, u32[]{:S(2)}, u32[]{:S(2)}) collective-permute-start(bf16[2,320,384]{2,1,0:T(8,128)(2,1)} %get-tuple-element.32), channel_id=1, source_target_pairs={{0,1},{1,0},{2,3},{3,2},{4,5},{5,4},{6,7},{7,6},{8,9},{9,8},{10,11... | collective-permute-start | bytes 1474568 | tf_op jit(solution)/shard_map/ppermute | solution.py:398
  84.0 15.3 %collective-permute-start.2 = (bf16[320,384]{1,0:T(8,128)(2,1)S(1)}, bf16[320,384]{1,0:T(8,128)(2,1)S(1)}, u32[]{:S(2)}, u32[]{:S(2)}) collective-permute-start(bf16[320,384]{1,0:T(8,128)(2,1)S(1)} %dynamic-slice_bitcast_fusion), channel_id=1, source_target_pairs={{0,2},{2,0},{1,3},{3,1},{4,6},{6,4},{5,7},{7,5},{8,10},{10,8},{9,1... | collective-permute-start | bytes 737288 | tf_op jit(solution)/shard_map/ppermute | solution.py:401
  87.6 18.0 %all-to-all-start.2 = ((bf16[16,8,640]{2,1,0:T(8,128)(2,1)}), bf16[16,8,640]{2,1,0:T(8,128)(2,1)S(1)}, u32[]{:S(2)}, u32[]{:S(2)}) async-start(bf16[16,8,640]{2,1,0:T(8,128)(2,1)} %bitcast.17), calls=%async_computation.2 | async-start | bytes 327680 | tf_op jit(solution)/shard_map/all_to_all | solution.py:405

commit v10 on v9

--- a/solution.py
+++ b/solution.py
@@ -38,6 +38,20 @@
     return lax.dot_general(a, b, (((a_dim,), (b_dim,)), ((), ())), preferred_element_type=F32)
 
 
+def stack_kernel(own_ref, other_ref, out_ref):
+    out_ref[0] = own_ref[...]
+    out_ref[1] = other_ref[...]
+
+
+def stack(own, other):
+    return pl.pallas_call(
+        stack_kernel,
+        out_shape=jax.ShapeDtypeStruct((2, WIDTH, P_SIZE), BF16),
+        cost_estimate=LONG,
+        compiler_params=pltpu.CompilerParams(vmem_limit_bytes=8 * 1024 * 1024),
+    )(own, other)
+
+
 def project_kernel(
     half_ref, t_ref, wq_ref, wk_ref, wv_ref, tok_out, q_out, k_out, v_out,
     tok_ref, q_ref, k_ref, v_ref, sem,
@@ -69,7 +83,6 @@
         scratch_shapes=[pltpu.VMEM((4 * WIDTH, P_SIZE), BF16)]
         + [pltpu.VMEM((P_SIZE, WIDTH), BF16)] * 3
         + [pltpu.SemaphoreType.DMA((4,))],
-        cost_estimate=LONG,
         compiler_params=pltpu.CompilerParams(vmem_limit_bytes=VMEM_BYTES),
     )(half.reshape(1), parts, wq, wk, wv)
 
@@ -130,7 +143,7 @@
     hbm, vmem = [pl.BlockSpec(memory_space=space) for space in (pltpu.HBM, pltpu.VMEM)]
     return pl.pallas_call(
         ref_kernel,
-        out_shape=jax.ShapeDtypeStruct((N_FRAMES, 16, LANES), BF16),
+        out_shape=jax.ShapeDtypeStruct((N_SECOND, 16, LANES), BF16),
         in_specs=[vmem, hbm, hbm],
         out_specs=vmem,
         scratch_shapes=[pltpu.VMEM((16, LANES), F32)]
@@ -387,8 +400,11 @@
     ref_hidden, own = lax.optimization_barrier((ref_hidden, tokens.T))
     other = lax.ppermute(own, "h", swap)
     pair = ref_pair(ref_hidden, wk, wv)
-    pair = lax.all_to_all(pair, FIRST + SECOND, 0, 0, tiled=True)
-    parts = lax.all_gather(jnp.stack([own, other]), "c", axis=0, tiled=False)
+    pair = lax.all_to_all(pair, SECOND, 0, 0, tiled=True).reshape(1, N_SECOND * 16, LANES)
+    pair, blocks = lax.optimization_barrier((pair, stack(own, other)))
+    pair = jnp.broadcast_to(pair, (N_FIRST, N_SECOND * 16, LANES))
+    pair = lax.all_to_all(pair, FIRST, 0, 0, tiled=True)
+    parts = lax.all_gather(blocks, "c", axis=0, tiled=False)
     tok, queries, keys, values = project(half, parts, wq, wk, wv)
     attended, query_grads, key_grads, value_grads, pack = attention(
         queries, keys, values, pair.reshape(N_FRAMES * 16, LANES), cotangent.T, tok

time: 107 us -> 106 us (level)
  starting transfers between devices: 38.3 us -> 33.5 us
  blocking collectives: 18.8 us -> 20.1 us
  waiting for transfers between devices: 23.6 us -> 24.9 us
    all_to_all x1, starting transfers between devices: 7.87 us -> 3.52 us  [per_device(): pack = lax.all_to_all(pack, SECOND, 0, 0, tiled=True)]
    all_to_all x1, waiting for transfers between devices: 0.65 us -> 3.08 us  [per_device(): pack = lax.all_to_all(pack, FIRST, 0, 0, tiled=True)]
    all_to_all x1 -> x2, waiting for transfers between devices: 11.9 us -> 10.1 us  [the longest x1 9.41 us: per_device(): lax.all_to_all(pair, SECOND, 0, 0, tiled=True)]
    ppermute x1, waiting for transfers between devices: 3.91 us -> 5.2 us  [per_device(): got = lax.ppermute(sent, 'h', swap)]
    all_gather x1, blocking collectives: 3.01 us -> 4.26 us  [per_device(): parts = lax.all_gather(blocks, 'c', axis=0, tiled=False)]
    all_to_all x1 -> x2, starting transfers between devices: 14.2 us -> 14 us  [the longest x1 9.65 us: per_device(): lax.all_to_all(pair, SECOND, 0, 0, tiled=True)]
    pallas_call x1 -> x2, Pallas kernels: 3.03 us -> 2.87 us  [the longest x1 2.82 us: ref_pair(): pl.pallas_call(ref_kernel, out_shape=jax.ShapeDtypeStruct((N_SECOND, 16,...]
  transfers between devices with their start and end apart: 6 -> 7, of which waited for: 5 -> 6; matrix products, arithmetic and copies ran while one was open for 1% -> 1% of each run, Pallas kernels for 11% -> 11%
where the time goes in v10:
time: 106 us; the launch traced here: 105 us
  starting transfers between devices  33.5 us (32%)
  waiting for transfers between devices  24.9 us (23%)
  Pallas kernels  22.6 us (21%)
  blocking collectives  20.1 us (19%)
  local copies, waits for them, and re-layouts  1.61 us (2%)
  other arithmetic  1.15 us (1%)
    all_gather x1, blocking collectives, per_device(): ref_hidden = lax.all_gather(cols, TENSOR, axis=0, tiled=False)  15.8 us
    all_to_all x1, starting transfers between devices, per_device(): lax.all_to_all(pair, SECOND, 0, 0, tiled=True)  9.65 us
    all_to_all x1, waiting for transfers between devices, per_device(): lax.all_to_all(pair, SECOND, 0, 0, tiled=True)  9.41 us
    pallas_call x1, Pallas kernels, attention(): pl.pallas_call(attention_kernel, out_shape=(pltpu.HBM((WIDTH, P_SIZE), BF...  8.7 us
    ppermute x1, starting transfers between devices, per_device(): other = lax.ppermute(own, 'h', swap)  5.26 us
    ppermute x1, waiting for transfers between devices, per_device(): got = lax.ppermute(sent, 'h', swap)  5.2 us
    all_to_all x1, waiting for transfers between devices, per_device(): pack = lax.all_to_all(pack, SECOND, 0, 0, tiled=True)  4.81 us
    all_to_all x1, starting transfers between devices, per_device(): pack = lax.all_to_all(pack, FIRST, 0, 0, tiled=True)  4.77 us
  transfers between devices with their start and end apart: 7, of which 6 were waited for; matrix products, arithmetic and copies ran while one was open for 1% of the time, Pallas kernels for 11%

profile of v10, /device:TPU:1, one launch (start us, length us, event | category | flops | bytes accessed | tf_op | source)
XLA Modules:
  0.0 104.6 jit_solution(11055452586907014037)
XLA Ops:
  0.6 0.0 copy-start.4
  0.7 0.7 copy-done.4
  1.3 1.5 %shard_map.110 = bf16[16,320]{1,0:T(8,128)(2,1)S(1)} custom-call(s32[1]{0:T(128)} %bitcast.1.at_ref, bf16[3,1280]{1,0:T(4,128)(2,1)S(1)} %copy-done.4, bf16[320,1280]{1,0:T(8,128)(2,1)} %bitcast.33), custom_call_target="tpu_custom_call" | custom-call | tf_op jit(solution)/shard_map/pallas_call | solution.py:105
  2.8 15.8 %all-gather = bf16[64,320]{1,0:T(8,128)(2,1)S(1)} all-gather(bf16[16,320]{1,0:T(8,128)(2,1)S(1)} %shard_map.110), channel_id=2, replica_groups=mesh['x'=4,'yh'=4,'yl'=2,'z'=4,'h'=2,'c'=2] {'h','c'}, dimensions={0}, use_global_device_ids=true | all-gather | bytes 51200 | tf_op jit(solution)/shard_map/all_gather | solution.py:399
  18.7 5.3 %collective-permute-start = (bf16[320,384]{1,0:T(8,128)(2,1)}, bf16[320,384]{1,0:T(8,128)(2,1)S(1)}, u32[]{:S(2)}, u32[]{:S(2)}) collective-permute-start(bf16[320,384]{1,0:T(8,128)(2,1)} %bitcast.31), channel_id=1, source_target_pairs={{0,2},{2,0},{1,3},{3,1},{4,6},{6,4},{5,7},{7,5},{8,10},{10,8},{9,1... | collective-permute-start | bytes 737288 | tf_op jit(solution)/shard_map/ppermute | solution.py:401
  24.0 0.0 copy-start.5
  24.0 2.8 %shard_map.111 = bf16[16,16,128]{2,1,0:T(8,128)(2,1)} custom-call(bf16[4,16,320]{2,1,0:T(8,128)(2,1)S(1)} %bitcast.30, bf16[320,1280]{1,0:T(8,128)(2,1)} %bitcast.22, bf16[320,1280]{1,0:T(8,128)(2,1)} %bitcast.25), custom_call_target="tpu_custom_call" | custom-call | flops 10000000000 | bytes 10000000000 | tf_op jit(solution)/shard_map/pallas_call | solution.py:144
  26.8 9.7 %all-to-all-start = ((bf16[16,16,128]{2,1,0:T(8,128)(2,1)}), bf16[16,16,128]{2,1,0:T(8,128)(2,1)S(1)}, u32[]{:S(2)}, u32[]{:S(2)}) async-start(bf16[16,16,128]{2,1,0:T(8,128)(2,1)} %shard_map.111), calls=%async_computation | async-start | bytes 131072 | tf_op jit(solution)/shard_map/all_to_all | solution.py:403
  36.5 0.0 collective-permute-done.other_ref
  36.5 0.0 copy-done.5
  36.5 9.4 %all-to-all-done = bf16[16,16,128]{2,1,0:T(8,128)(2,1)S(1)} async-done(((bf16[16,16,128]{2,1,0:T(8,128)(2,1)}), bf16[16,16,128]{2,1,0:T(8,128)(2,1)S(1)}, u32[]{:S(2)}, u32[]{:S(2)}) %all-to-all-start) | async-done | bytes 65568 | tf_op jit(solution)/shard_map/all_to_all | solution.py:403
  45.9 0.9 broadcast_in_dim.8
  46.8 0.0 copy-start
  46.8 0.0 copy-start.1
  46.8 0.0 copy-start.2
  46.8 4.3 %all-to-all-start.1 = ((bf16[8,256,128]{2,1,0:T(8,128)(2,1)}), bf16[8,256,128]{2,1,0:T(8,128)(2,1)S(1)}, u32[]{:S(2)}, u32[]{:S(2)}) async-start(bf16[8,256,128]{2,1,0:T(8,128)(2,1)} %broadcast_in_dim.8), calls=%async_computation.1 | async-start | bytes 1048576 | tf_op jit(solution)/shard_map/all_to_all | solution.py:406
  51.1 4.3 %all-gather.1 = bf16[4,320,384]{2,1,0:T(8,128)(2,1)S(1)} all-gather(bf16[2,320,384]{2,1,0:T(8,128)(2,1)S(1)} %shard_map.112), channel_id=3, replica_groups=mesh['x'=4,'yh'=4,'yl'=2,'z'=4,'h'=2,'c'=2] {'c'}, dimensions={0}, use_global_device_ids=true | all-gather | bytes 1474560 | tf_op jit(solution)/shard_map/all_gather | solution.py:407
  55.4 0.0 copy-done
  55.4 0.0 copy-done.1
  55.4 0.0 copy-done.2
  55.4 0.0 copy-start.3
  55.4 2.7 %shard_map.113 = (bf16[1280,384]{1,0:T(8,128)(2,1)}, bf16[384,320]{1,0:T(8,128)(2,1)}, bf16[384,320]{1,0:T(8,128)(2,1)}, bf16[384,320]{1,0:T(8,128)(2,1)}) custom-call(s32[1]{0:T(128)} %bitcast.half_ref, bf16[2,2,320,384]{3,2,1,0:T(8,128)(2,1)S(1)} %bitcast.19, bf16[320,1280]{1,0:T(8,128)(2,1)S(1)} %bitcast.21, bf16[320,1280]{1,0:T(8,128)(2,1)S(1)} %bitcast.24, ...), custom_call_target="tpu_custom_call" | custom-call | tf_op jit(solution)/shard_map/pallas_call | solution.py:77
  58.1 0.7 all-to-all-done.1
  58.8 0.0 copy-done.3
  58.8 8.7 %shard_map.114 = (bf16[320,384]{1,0:T(8,128)(2,1)}, bf16[384,320]{1,0:T(8,128)(2,1)}, bf16[384,320]{1,0:T(8,128)(2,1)}, bf16[384,320]{1,0:T(8,128)(2,1)}, bf16[8,128,640]{2,1,0:T(8,128)(2,1)}) custom-call(bf16[384,320]{1,0:T(8,128)(2,1)} %get-tuple-element.26.q_in, bf16[384,320]{1,0:T(8,128)(2,1)} %get-tuple-element.27.k_in, ...), custom_call_target="tpu_custom_call" | custom-call | tf_op jit(solution)/shard_map/pallas_call | solution.py:247
  67.5 4.8 %all-to-all-start.2 = ((bf16[8,128,640]{2,1,0:T(8,128)(2,1)}), bf16[8,128,640]{2,1,0:T(8,128)(2,1)S(1)}, u32[]{:S(2)}, u32[]{:S(2)}) async-start(bf16[8,128,640]{2,1,0:T(8,128)(2,1)} %get-tuple-element.37), calls=%async_computation.2 | async-start | bytes 2621440 | tf_op jit(solution)/shard_map/all_to_all | solution.py:412
  72.3 4.4 %shard_map.115 = (bf16[2,320,384]{2,1,0:T(8,128)(2,1)}, bf16[2,320,384]{2,1,0:T(8,128)(2,1)}) custom-call(s32[1]{0:T(128)} %bitcast.14.core_ref, bf16[384,320]{1,0:T(8,128)(2,1)} %get-tuple-element.32.dq_in, bf16[384,320]{1,0:T(8,128)(2,1)} %get-tuple-element.33.dk_in, bf16[384,320]{1,0:T(8,128)(2,1)} %get-tuple-element.34.dv_in, ...), custom_call_target="tpu_custom_call" | custom-call | flops 1 | bytes 1 | tf_op jit(solution)/shard_map/pallas_call | solution.py:307
  76.7 4.1 %collective-permute-start.1 = (bf16[2,320,384]{2,1,0:T(8,128)(2,1)}, bf16[2,320,384]{2,1,0:T(8,128)(2,1)S(1)}, u32[]{:S(2)}, u32[]{:S(2)}) collective-permute-start(bf16[2,320,384]{2,1,0:T(8,128)(2,1)} %get-tuple-element.36), channel_id=1, source_target_pairs={{0,1},{1,0},{2,3},{3,2},{4,5},{5,4},{6,7},{7,6},{8,9},{9,8},{10,11... | collective-permute-start | bytes 1474568 | tf_op jit(solution)/shard_map/ppermute | solution.py:414
  80.8 1.7 %collective-permute-done.1 = bf16[2,320,384]{2,1,0:T(8,128)(2,1)S(1)} collective-permute-done((bf16[2,320,384]{2,1,0:T(8,128)(2,1)}, bf16[2,320,384]{2,1,0:T(8,128)(2,1)S(1)}, u32[]{:S(2)}, u32[]{:S(2)}) %collective-permute-start.1) | collective-permute-done | bytes 491552 | tf_op jit(solution)/shard_map/ppermute | solution.py:414
  82.5 1.1 %add_convert_fusion.pair_ref = bf16[2,320,384]{2,1,0:T(8,128)(2,1)S(1)} fusion(bf16[2,320,384]{2,1,0:T(8,128)(2,1)S(1)} %collective-permute-done.1, bf16[2,320,384]{2,1,0:T(8,128)(2,1)} %get-tuple-element.35), kind=kLoop, calls=%fused_computation | loop fusion | flops 983040 | bytes 1474560 | tf_op jit(solution)/shard_map/convert_element_type | solution.py:415
  83.7 1.9 %collective-permute-start.2 = (bf16[320,384]{1,0:T(8,128)(2,1)S(1)}, bf16[320,384]{1,0:T(8,128)(2,1)S(1)}, u32[]{:S(2)}, u32[]{:S(2)}) collective-permute-start(bf16[320,384]{1,0:T(8,128)(2,1)S(1)} %dynamic-slice_bitcast_fusion), channel_id=1, source_target_pairs={{0,2},{2,0},{1,3},{3,1},{4,6},{6,4},{5,7},{7,5},{8,10},{10,8},{9,1... | collective-permute-start | bytes 737288 | tf_op jit(solution)/shard_map/ppermute | solution.py:417
  85.6 3.1 %all-to-all-done.2.in_ref = bf16[8,128,640]{2,1,0:T(8,128)(2,1)S(1)} async-done(((bf16[8,128,640]{2,1,0:T(8,128)(2,1)}), bf16[8,128,640]{2,1,0:T(8,128)(2,1)S(1)}, u32[]{:S(2)}, u32[]{:S(2)}) %all-to-all-start.2) | async-done | bytes 1310752 | tf_op jit(solution)/shard_map/all_to_all | solution.py:412
  88.7 0.9 shard_map.117
  89.6 3.5 %all-to-all-start.3 = ((bf16[16,8,640]{2,1,0:T(8,128)(2,1)}), bf16[16,8,640]{2,1,0:T(8,128)(2,1)S(1)}, u32[]{:S(2)}, u32[]{:S(2)}) async-start(bf16[16,8,640]{2,1,0:T(8,128)(2,1)} %bitcast.17), calls=%async_computation.3 | async-start | bytes 327680 | tf_op jit(solution)/shard_map/all_to_all | solution.py:421
  93.1 5.2 %collective-permute-done.2.got_ref = bf16[320,384]{1,0:T(8,128)(2,1)S(1)} collective-permute-done((bf16[320,384]{1,0:T(8,128)(2,1)S(1)}, bf16[320,384]{1,0:T(8,128)(2,1)S(1)}, u32[]{:S(2)}, u32[]{:S(2)}) %collective-permute-start.2) | collective-permute-done | bytes 245792 | tf_op jit(solution)/shard_map/ppermute | solution.py:417
  98.3 0.8 shard_map.116
  99.1 4.8 %all-to-all-done.3.in_ref = bf16[16,8,640]{2,1,0:T(8,128)(2,1)S(1)} async-done(((bf16[16,8,640]{2,1,0:T(8,128)(2,1)}), bf16[16,8,640]{2,1,0:T(8,128)(2,1)S(1)}, u32[]{:S(2)}, u32[]{:S(2)}) %all-to-all-start.3) | async-done | bytes 163872 | tf_op jit(solution)/shard_map/all_to_all | solution.py:421
  103.9 0.7 shard_map.118
  (2 shorter events, 0.1 us)
Async XLA Ops:
  0.6 0.7 copy-start.4
  18.7 17.8 %collective-permute-start = (bf16[320,384]{1,0:T(8,128)(2,1)}, bf16[320,384]{1,0:T(8,128)(2,1)S(1)}, u32[]{:S(2)}, u32[]{:S(2)}) collective-permute-start(bf16[320,384]{1,0:T(8,128)(2,1)} %bitcast.31), channel_id=1, source_target_pairs={{0,2},{2,0},{1,3},{3,1},{4,6},{6,4},{5,7},{7,5},{8,10},{10,8},{9,1... | collective-permute-start | bytes 737288 | tf_op jit(solution)/shard_map/ppermute | solution.py:401
  24.0 12.5 %copy-start.5 = (bf16[384,320]{0,1:T(8,128)(2,1)S(1)}, bf16[384,320]{0,1:T(8,128)(2,1)}, u32[]{:S(2)}) copy-start(bf16[384,320]{0,1:T(8,128)(2,1)} %param.7) | copy-start | bytes 737284
  26.8 19.1 %all-to-all-start = ((bf16[16,16,128]{2,1,0:T(8,128)(2,1)}), bf16[16,16,128]{2,1,0:T(8,128)(2,1)S(1)}, u32[]{:S(2)}, u32[]{:S(2)}) async-start(bf16[16,16,128]{2,1,0:T(8,128)(2,1)} %shard_map.111), calls=%async_computation | async-start | bytes 131072 | tf_op jit(solution)/shard_map/all_to_all | solution.py:403
  46.8 8.6 %copy-start = (bf16[1280,320]{0,1:T(8,128)(2,1)S(1)}, bf16[1280,320]{0,1:T(8,128)(2,1)}, u32[]{:S(2)}) copy-start(bf16[1280,320]{0,1:T(8,128)(2,1)} %param.9) | copy-start | bytes 2457604
  46.8 8.6 %copy-start.1 = (bf16[1280,320]{0,1:T(8,128)(2,1)S(1)}, bf16[1280,320]{0,1:T(8,128)(2,1)}, u32[]{:S(2)}) copy-start(bf16[1280,320]{0,1:T(8,128)(2,1)} %param.10) | copy-start | bytes 2457604
  46.8 8.6 %copy-start.2 = (bf16[1280,320]{0,1:T(8,128)(2,1)S(1)}, bf16[1280,320]{0,1:T(8,128)(2,1)}, u32[]{:S(2)}) copy-start(bf16[1280,320]{0,1:T(8,128)(2,1)} %param.11) | copy-start | bytes 2457604
  46.8 12.0 %all-to-all-start.1 = ((bf16[8,256,128]{2,1,0:T(8,128)(2,1)}), bf16[8,256,128]{2,1,0:T(8,128)(2,1)S(1)}, u32[]{:S(2)}, u32[]{:S(2)}) async-start(bf16[8,256,128]{2,1,0:T(8,128)(2,1)} %broadcast_in_dim.8), calls=%async_computation.1 | async-start | bytes 1048576 | tf_op jit(solution)/shard_map/all_to_all | solution.py:406
  55.4 3.4 %copy-start.3 = (bf16[384,320]{0,1:T(8,128)(2,1)S(1)}, bf16[384,320]{0,1:T(8,128)(2,1)}, u32[]{:S(2)}) copy-start(bf16[384,320]{0,1:T(8,128)(2,1)} %param.13) | copy-start | bytes 737284
  67.5 21.2 %all-to-all-start.2 = ((bf16[8,128,640]{2,1,0:T(8,128)(2,1)}), bf16[8,128,640]{2,1,0:T(8,128)(2,1)S(1)}, u32[]{:S(2)}, u32[]{:S(2)}) async-start(bf16[8,128,640]{2,1,0:T(8,128)(2,1)} %get-tuple-element.37), calls=%async_computation.2 | async-start | bytes 2621440 | tf_op jit(solution)/shard_map/all_to_all | solution.py:412
  76.7 5.8 %collective-permute-start.1 = (bf16[2,320,384]{2,1,0:T(8,128)(2,1)}, bf16[2,320,384]{2,1,0:T(8,128)(2,1)S(1)}, u32[]{:S(2)}, u32[]{:S(2)}) collective-permute-start(bf16[2,320,384]{2,1,0:T(8,128)(2,1)} %get-tuple-element.36), channel_id=1, source_target_pairs={{0,1},{1,0},{2,3},{3,2},{4,5},{5,4},{6,7},{7,6},{8,9},{9,8},{10,11... | collective-permute-start | bytes 1474568 | tf_op jit(solution)/shard_map/ppermute | solution.py:414
  83.7 14.6 %collective-permute-start.2 = (bf16[320,384]{1,0:T(8,128)(2,1)S(1)}, bf16[320,384]{1,0:T(8,128)(2,1)S(1)}, u32[]{:S(2)}, u32[]{:S(2)}) collective-permute-start(bf16[320,384]{1,0:T(8,128)(2,1)S(1)} %dynamic-slice_bitcast_fusion), channel_id=1, source_target_pairs={{0,2},{2,0},{1,3},{3,1},{4,6},{6,4},{5,7},{7,5},{8,10},{10,8},{9,1... | collective-permute-start | bytes 737288 | tf_op jit(solution)/shard_map/ppermute | solution.py:417
  89.6 14.3 %all-to-all-start.3 = ((bf16[16,8,640]{2,1,0:T(8,128)(2,1)}), bf16[16,8,640]{2,1,0:T(8,128)(2,1)S(1)}, u32[]{:S(2)}, u32[]{:S(2)}) async-start(bf16[16,8,640]{2,1,0:T(8,128)(2,1)} %bitcast.17), calls=%async_computation.3 | async-start | bytes 327680 | tf_op jit(solution)/shard_map/all_to_all | solution.py:421

commit v11 on v10

--- a/solution.py
+++ b/solution.py
@@ -38,6 +38,25 @@
     return lax.dot_general(a, b, (((a_dim,), (b_dim,)), ((), ())), preferred_element_type=F32)
 
 
+def spread_kernel(in_ref, out_ref, sem):
+    copies = [pltpu.make_async_copy(in_ref, out_ref.at[i], sem.at[i]) for i in range(N_FIRST)]
+    for copy in copies:
+        copy.start()
+    for copy in copies:
+        copy.wait()
+
+
+def spread(pair):
+    return pl.pallas_call(
+        spread_kernel,
+        out_shape=pltpu.HBM((N_FIRST,) + pair.shape, BF16),
+        out_specs=pl.BlockSpec(memory_space=pltpu.HBM),
+        scratch_shapes=[pltpu.SemaphoreType.DMA((N_FIRST,))],
+        cost_estimate=LONG,
+        compiler_params=pltpu.CompilerParams(vmem_limit_bytes=8 * 1024 * 1024),
+    )(pair)
+
+
 def stack_kernel(own_ref, other_ref, out_ref):
     out_ref[0] = own_ref[...]
     out_ref[1] = other_ref[...]
@@ -149,7 +168,6 @@
         scratch_shapes=[pltpu.VMEM((16, LANES), F32)]
         + [pltpu.VMEM((WIDTH, 4 * WIDTH), BF16)] * 2
         + [pltpu.SemaphoreType.DMA((2,))],
-        cost_estimate=LONG,
         compiler_params=pltpu.CompilerParams(vmem_limit_bytes=12 * 1024 * 1024),
     )(gathered, *[pltpu.with_memory_space_constraint(a, pltpu.HBM) for a in (wk, wv)])
 
@@ -400,10 +418,9 @@
     ref_hidden, own = lax.optimization_barrier((ref_hidden, tokens.T))
     other = lax.ppermute(own, "h", swap)
     pair = ref_pair(ref_hidden, wk, wv)
-    pair = lax.all_to_all(pair, SECOND, 0, 0, tiled=True).reshape(1, N_SECOND * 16, LANES)
-    pair, blocks = lax.optimization_barrier((pair, stack(own, other)))
-    pair = jnp.broadcast_to(pair, (N_FIRST, N_SECOND * 16, LANES))
-    pair = lax.all_to_all(pair, FIRST, 0, 0, tiled=True)
+    pair = lax.all_to_all(pair, SECOND, 0, 0, tiled=True).reshape(N_SECOND * 16, LANES)
+    blocks = stack(own, other)
+    pair = lax.all_to_all(spread(pair), FIRST, 0, 0, tiled=True)
     parts = lax.all_gather(blocks, "c", axis=0, tiled=False)
     tok, queries, keys, values = project(half, parts, wq, wk, wv)
     attended, query_grads, key_grads, value_grads, pack = attention(

time: 106 us -> 106 us (level)
  starting transfers between devices: 33.5 us -> 44.3 us
  waiting for transfers between devices: 24.9 us -> 14.2 us
    all_to_all x2, waiting for transfers between devices: 10.1 us -> 3.2 us  [the longest x1 2 us: per_device(): lax.all_to_all(pair, SECOND, 0, 0, tiled=True).reshape(N_SECOND * 16, LANES)]
    ppermute x1, starting transfers between devices: 1.92 us -> 7.78 us  [per_device(): got = lax.ppermute(sent, 'h', swap)]
    all_to_all x1, starting transfers between devices: 3.52 us -> 9.2 us  [per_device(): pack = lax.all_to_all(pack, SECOND, 0, 0, tiled=True)]
    ppermute x1, waiting for transfers between devices: 5.2 us -> 0.01 us  [per_device(): got = lax.ppermute(sent, 'h', swap)]
    all_to_all x1, waiting for transfers between devices: 4.81 us -> 9.31 us  [per_device(): pack = lax.all_to_all(pack, SECOND, 0, 0, tiled=True)]
    all_to_all x1, waiting for transfers between devices: 3.08 us -> 0.01 us  [per_device(): pack = lax.all_to_all(pack, FIRST, 0, 0, tiled=True)]
    all_to_all x2, starting transfers between devices: 14 us -> 11.5 us  [the longest x1 7.41 us: per_device(): lax.all_to_all(pair, SECOND, 0, 0, tiled=True).reshape(N_SECOND * 16, LANES)]
    ppermute x1, starting transfers between devices: 5.26 us -> 7.52 us  [per_device(): other = lax.ppermute(own, 'h', swap)]
  transfers between devices with their start and end apart: 7 -> 7, of which waited for: 6 -> 4; matrix products, arithmetic and copies ran while one was open for 1% -> 1% of each run, Pallas kernels for 11% -> 9%
where the time goes in v11:
time: 106 us; the launch traced here: 105 us
  starting transfers between devices  44.3 us (42%)
  Pallas kernels  23.4 us (22%)
  blocking collectives  20 us (19%)
  waiting for transfers between devices  14.2 us (13%)
  other arithmetic  1.15 us (1%)
    all_gather x1, blocking collectives, per_device(): ref_hidden = lax.all_gather(cols, TENSOR, axis=0, tiled=False)  15.8 us
    all_to_all x1, waiting for transfers between devices, per_device(): pack = lax.all_to_all(pack, SECOND, 0, 0, tiled=True)  9.31 us
    all_to_all x1, starting transfers between devices, per_device(): pack = lax.all_to_all(pack, SECOND, 0, 0, tiled=True)  9.2 us
    pallas_call x1, Pallas kernels, attention(): pl.pallas_call(attention_kernel, out_shape=(pltpu.HBM((WIDTH, P_SIZE), BF...  8.71 us
    ppermute x1, starting transfers between devices, per_device(): got = lax.ppermute(sent, 'h', swap)  7.78 us
    ppermute x1, starting transfers between devices, per_device(): other = lax.ppermute(own, 'h', swap)  7.52 us
    all_to_all x1, starting transfers between devices, per_device(): lax.all_to_all(pair, SECOND, 0, 0, tiled=True).reshape(N_SECOND * 16, LANES)  7.41 us
    pallas_call x1, Pallas kernels, token_parts(): pl.pallas_call(token_kernel, out_shape=(pltpu.HBM((2, WIDTH, P_SIZE), BF1...  4.44 us
  transfers between devices with their start and end apart: 7, of which 4 were waited for; matrix products, arithmetic and copies ran while one was open for 1% of the time, Pallas kernels for 9%

profile of v11, /device:TPU:1, one launch (start us, length us, event | category | flops | bytes accessed | tf_op | source)
XLA Modules:
  0.0 104.7 jit_solution(2592086711286480142)
XLA Ops:
  0.6 0.0 copy-start.4
  0.7 0.7 copy-done.4
  1.3 0.0 copy-start.5
  1.3 1.5 %shard_map.110 = bf16[16,320]{1,0:T(8,128)(2,1)S(1)} custom-call(s32[1]{0:T(128)} %bitcast.1.at_ref, bf16[3,1280]{1,0:T(4,128)(2,1)S(1)} %copy-done.4, bf16[320,1280]{1,0:T(8,128)(2,1)} %bitcast.33), custom_call_target="tpu_custom_call" | custom-call | tf_op jit(solution)/shard_map/pallas_call | solution.py:124
  2.9 15.8 %all-gather = bf16[64,320]{1,0:T(8,128)(2,1)S(1)} all-gather(bf16[16,320]{1,0:T(8,128)(2,1)S(1)} %shard_map.110), channel_id=2, replica_groups=mesh['x'=4,'yh'=4,'yl'=2,'z'=4,'h'=2,'c'=2] {'h','c'}, dimensions={0}, use_global_device_ids=true | all-gather | bytes 51200 | tf_op jit(solution)/shard_map/all_gather | solution.py:417
  18.7 2.8 %shard_map.113 = bf16[16,16,128]{2,1,0:T(8,128)(2,1)} custom-call(bf16[4,16,320]{2,1,0:T(8,128)(2,1)S(1)} %bitcast.29, bf16[320,1280]{1,0:T(8,128)(2,1)} %bitcast.18, bf16[320,1280]{1,0:T(8,128)(2,1)} %bitcast.21), custom_call_target="tpu_custom_call" | custom-call | tf_op jit(solution)/shard_map/pallas_call | solution.py:163
  21.5 7.4 %all-to-all-start = ((bf16[16,16,128]{2,1,0:T(8,128)(2,1)}), bf16[16,16,128]{2,1,0:T(8,128)(2,1)S(1)}, u32[]{:S(2)}, u32[]{:S(2)}) async-start(bf16[16,16,128]{2,1,0:T(8,128)(2,1)} %shard_map.113), calls=%async_computation | async-start | bytes 131072 | tf_op jit(solution)/shard_map/all_to_all | solution.py:421
  28.9 0.0 copy-done.5
  28.9 7.5 %collective-permute-start = (bf16[320,384]{1,0:T(8,128)(2,1)S(1)}, bf16[320,384]{1,0:T(8,128)(2,1)S(1)}, u32[]{:S(2)}, u32[]{:S(2)}) collective-permute-start(bf16[320,384]{1,0:T(8,128)(2,1)S(1)} %bitcast.31), channel_id=1, source_target_pairs={{0,2},{2,0},{1,3},{3,1},{4,6},{6,4},{5,7},{7,5},{8,10},{10,8},{9,1... | collective-permute-start | bytes 737288 | tf_op jit(solution)/shard_map/ppermute | solution.py:419
  36.5 2.0 %all-to-all-done = bf16[16,16,128]{2,1,0:T(8,128)(2,1)S(1)} async-done(((bf16[16,16,128]{2,1,0:T(8,128)(2,1)}), bf16[16,16,128]{2,1,0:T(8,128)(2,1)S(1)}, u32[]{:S(2)}, u32[]{:S(2)}) %all-to-all-start) | async-done | bytes 65568 | tf_op jit(solution)/shard_map/all_to_all | solution.py:421
  38.5 0.9 shard_map.114
  39.3 4.1 %all-to-all-start.1 = ((bf16[8,256,128]{2,1,0:T(8,128)(2,1)}), bf16[8,256,128]{2,1,0:T(8,128)(2,1)S(1)}, u32[]{:S(2)}, u32[]{:S(2)}) async-start(bf16[8,256,128]{2,1,0:T(8,128)(2,1)} %shard_map.114), calls=%async_computation.1 | async-start | bytes 1048576 | tf_op jit(solution)/shard_map/all_to_all | solution.py:423
  43.4 0.0 collective-permute-done.other_ref
  43.5 0.0 copy-start.1
  43.5 0.0 copy-start.2
  43.5 0.0 copy-start
  43.6 4.2 %all-gather.1 = bf16[4,320,384]{2,1,0:T(8,128)(2,1)S(1)} all-gather(bf16[2,320,384]{2,1,0:T(8,128)(2,1)S(1)} %shard_map.111), channel_id=3, replica_groups=mesh['x'=4,'yh'=4,'yl'=2,'z'=4,'h'=2,'c'=2] {'c'}, dimensions={0}, use_global_device_ids=true | all-gather | bytes 1474560 | tf_op jit(solution)/shard_map/all_gather | solution.py:424
  47.7 0.0 copy-done.1
  47.7 0.0 copy-done.2
  47.7 0.0 copy-done
  47.7 0.0 copy-start.3
  47.7 2.7 %shard_map.112 = (bf16[1280,384]{1,0:T(8,128)(2,1)}, bf16[384,320]{1,0:T(8,128)(2,1)}, bf16[384,320]{1,0:T(8,128)(2,1)}, bf16[384,320]{1,0:T(8,128)(2,1)}) custom-call(s32[1]{0:T(128)} %bitcast.half_ref, bf16[2,2,320,384]{3,2,1,0:T(8,128)(2,1)S(1)} %bitcast.24, bf16[320,1280]{1,0:T(8,128)(2,1)S(1)} %bitcast.26, bf16[320,1280]{1,0:T(8,128)(2,1)S(1)} %bitcast.20, ...), custom_call_target="tpu_custom_call" | custom-call | tf_op jit(solution)/shard_map/pallas_call | solution.py:96
  50.4 1.2 %all-to-all-done.1 = bf16[8,256,128]{2,1,0:T(8,128)(2,1)S(1)} async-done(((bf16[8,256,128]{2,1,0:T(8,128)(2,1)}), bf16[8,256,128]{2,1,0:T(8,128)(2,1)S(1)}, u32[]{:S(2)}, u32[]{:S(2)}) %all-to-all-start.1) | async-done | bytes 524320 | tf_op jit(solution)/shard_map/all_to_all | solution.py:423
  51.7 0.0 copy-done.3
  51.7 8.7 %shard_map.115 = (bf16[320,384]{1,0:T(8,128)(2,1)}, bf16[384,320]{1,0:T(8,128)(2,1)}, bf16[384,320]{1,0:T(8,128)(2,1)}, bf16[384,320]{1,0:T(8,128)(2,1)}, bf16[8,128,640]{2,1,0:T(8,128)(2,1)}) custom-call(bf16[384,320]{1,0:T(8,128)(2,1)} %get-tuple-element.22.q_in, bf16[384,320]{1,0:T(8,128)(2,1)} %get-tuple-element.23.k_in, ...), custom_call_target="tpu_custom_call" | custom-call | tf_op jit(solution)/shard_map/pallas_call | solution.py:265
  60.4 4.2 %all-to-all-start.2 = ((bf16[8,128,640]{2,1,0:T(8,128)(2,1)}), bf16[8,128,640]{2,1,0:T(8,128)(2,1)S(1)}, u32[]{:S(2)}, u32[]{:S(2)}) async-start(bf16[8,128,640]{2,1,0:T(8,128)(2,1)} %get-tuple-element.33), calls=%async_computation.2 | async-start | bytes 2621440 | tf_op jit(solution)/shard_map/all_to_all | solution.py:429
  64.6 4.4 %shard_map.116 = (bf16[2,320,384]{2,1,0:T(8,128)(2,1)}, bf16[2,320,384]{2,1,0:T(8,128)(2,1)}) custom-call(s32[1]{0:T(128)} %bitcast.13.core_ref, bf16[384,320]{1,0:T(8,128)(2,1)} %get-tuple-element.28.dq_in, bf16[384,320]{1,0:T(8,128)(2,1)} %get-tuple-element.29.dk_in, bf16[384,320]{1,0:T(8,128)(2,1)} %get-tuple-element.30.dv_in, ...), custom_call_target="tpu_custom_call" | custom-call | flops 1 | bytes 1 | tf_op jit(solution)/shard_map/pallas_call | solution.py:325
  69.1 4.1 %collective-permute-start.1 = (bf16[2,320,384]{2,1,0:T(8,128)(2,1)}, bf16[2,320,384]{2,1,0:T(8,128)(2,1)S(1)}, u32[]{:S(2)}, u32[]{:S(2)}) collective-permute-start(bf16[2,320,384]{2,1,0:T(8,128)(2,1)} %get-tuple-element.32), channel_id=1, source_target_pairs={{0,1},{1,0},{2,3},{3,2},{4,5},{5,4},{6,7},{7,6},{8,9},{9,8},{10,11... | collective-permute-start | bytes 1474568 | tf_op jit(solution)/shard_map/ppermute | solution.py:431
  73.2 1.7 %collective-permute-done.1 = bf16[2,320,384]{2,1,0:T(8,128)(2,1)S(1)} collective-permute-done((bf16[2,320,384]{2,1,0:T(8,128)(2,1)}, bf16[2,320,384]{2,1,0:T(8,128)(2,1)S(1)}, u32[]{:S(2)}, u32[]{:S(2)}) %collective-permute-start.1) | collective-permute-done | bytes 491552 | tf_op jit(solution)/shard_map/ppermute | solution.py:431
  74.8 1.1 %add_convert_fusion.pair_ref = bf16[2,320,384]{2,1,0:T(8,128)(2,1)S(1)} fusion(bf16[2,320,384]{2,1,0:T(8,128)(2,1)S(1)} %collective-permute-done.1, bf16[2,320,384]{2,1,0:T(8,128)(2,1)} %get-tuple-element.31), kind=kLoop, calls=%fused_computation | loop fusion | flops 983040 | bytes 1474560 | tf_op jit(solution)/shard_map/convert_element_type | solution.py:432
  76.0 7.8 %collective-permute-start.2 = (bf16[320,384]{1,0:T(8,128)(2,1)S(1)}, bf16[320,384]{1,0:T(8,128)(2,1)S(1)}, u32[]{:S(2)}, u32[]{:S(2)}) collective-permute-start(bf16[320,384]{1,0:T(8,128)(2,1)S(1)} %dynamic-slice_bitcast_fusion), channel_id=1, source_target_pairs={{0,2},{2,0},{1,3},{3,1},{4,6},{6,4},{5,7},{7,5},{8,10},{10,8},{9,1... | collective-permute-start | bytes 737288 | tf_op jit(solution)/shard_map/ppermute | solution.py:434
  83.8 0.0 all-to-all-done.2.in_ref
  83.8 0.9 shard_map.118
  84.7 9.2 %all-to-all-start.3 = ((bf16[16,8,640]{2,1,0:T(8,128)(2,1)}), bf16[16,8,640]{2,1,0:T(8,128)(2,1)S(1)}, u32[]{:S(2)}, u32[]{:S(2)}) async-start(bf16[16,8,640]{2,1,0:T(8,128)(2,1)} %bitcast.16), calls=%async_computation.3 | async-start | bytes 327680 | tf_op jit(solution)/shard_map/all_to_all | solution.py:438
  93.9 0.0 collective-permute-done.2.got_ref
  93.9 0.8 shard_map.117
  94.7 9.3 %all-to-all-done.3.in_ref = bf16[16,8,640]{2,1,0:T(8,128)(2,1)S(1)} async-done(((bf16[16,8,640]{2,1,0:T(8,128)(2,1)}), bf16[16,8,640]{2,1,0:T(8,128)(2,1)S(1)}, u32[]{:S(2)}, u32[]{:S(2)}) %all-to-all-start.3) | async-done | bytes 163872 | tf_op jit(solution)/shard_map/all_to_all | solution.py:438
  104.0 0.7 shard_map.119
  (2 shorter events, 0.1 us)
Async XLA Ops:
  0.6 0.7 copy-start.4
  1.3 27.6 %copy-start.5 = (bf16[384,320]{0,1:T(8,128)(2,1)S(1)}, bf16[384,320]{0,1:T(8,128)(2,1)}, u32[]{:S(2)}) copy-start(bf16[384,320]{0,1:T(8,128)(2,1)} %param.7) | copy-start | bytes 737284
  21.5 17.0 %all-to-all-start = ((bf16[16,16,128]{2,1,0:T(8,128)(2,1)}), bf16[16,16,128]{2,1,0:T(8,128)(2,1)S(1)}, u32[]{:S(2)}, u32[]{:S(2)}) async-start(bf16[16,16,128]{2,1,0:T(8,128)(2,1)} %shard_map.113), calls=%async_computation | async-start | bytes 131072 | tf_op jit(solution)/shard_map/all_to_all | solution.py:421
  28.9 14.6 %collective-permute-start = (bf16[320,384]{1,0:T(8,128)(2,1)S(1)}, bf16[320,384]{1,0:T(8,128)(2,1)S(1)}, u32[]{:S(2)}, u32[]{:S(2)}) collective-permute-start(bf16[320,384]{1,0:T(8,128)(2,1)S(1)} %bitcast.31), channel_id=1, source_target_pairs={{0,2},{2,0},{1,3},{3,1},{4,6},{6,4},{5,7},{7,5},{8,10},{10,8},{9,1... | collective-permute-start | bytes 737288 | tf_op jit(solution)/shard_map/ppermute | solution.py:419
  39.3 12.3 %all-to-all-start.1 = ((bf16[8,256,128]{2,1,0:T(8,128)(2,1)}), bf16[8,256,128]{2,1,0:T(8,128)(2,1)S(1)}, u32[]{:S(2)}, u32[]{:S(2)}) async-start(bf16[8,256,128]{2,1,0:T(8,128)(2,1)} %shard_map.114), calls=%async_computation.1 | async-start | bytes 1048576 | tf_op jit(solution)/shard_map/all_to_all | solution.py:423
  43.5 4.2 %copy-start.1 = (bf16[1280,320]{0,1:T(8,128)(2,1)S(1)}, bf16[1280,320]{0,1:T(8,128)(2,1)}, u32[]{:S(2)}) copy-start(bf16[1280,320]{0,1:T(8,128)(2,1)} %param.11) | copy-start | bytes 2457604
  43.5 4.2 %copy-start.2 = (bf16[1280,320]{0,1:T(8,128)(2,1)S(1)}, bf16[1280,320]{0,1:T(8,128)(2,1)}, u32[]{:S(2)}) copy-start(bf16[1280,320]{0,1:T(8,128)(2,1)} %param.9) | copy-start | bytes 2457604
  43.5 4.2 %copy-start = (bf16[1280,320]{0,1:T(8,128)(2,1)S(1)}, bf16[1280,320]{0,1:T(8,128)(2,1)}, u32[]{:S(2)}) copy-start(bf16[1280,320]{0,1:T(8,128)(2,1)} %param.10) | copy-start | bytes 2457604
  47.7 3.9 %copy-start.3 = (bf16[384,320]{0,1:T(8,128)(2,1)S(1)}, bf16[384,320]{0,1:T(8,128)(2,1)}, u32[]{:S(2)}) copy-start(bf16[384,320]{0,1:T(8,128)(2,1)} %param.13) | copy-start | bytes 737284
  60.4 23.4 %all-to-all-start.2 = ((bf16[8,128,640]{2,1,0:T(8,128)(2,1)}), bf16[8,128,640]{2,1,0:T(8,128)(2,1)S(1)}, u32[]{:S(2)}, u32[]{:S(2)}) async-start(bf16[8,128,640]{2,1,0:T(8,128)(2,1)} %get-tuple-element.33), calls=%async_computation.2 | async-start | bytes 2621440 | tf_op jit(solution)/shard_map/all_to_all | solution.py:429
  69.1 5.8 %collective-permute-start.1 = (bf16[2,320,384]{2,1,0:T(8,128)(2,1)}, bf16[2,320,384]{2,1,0:T(8,128)(2,1)S(1)}, u32[]{:S(2)}, u32[]{:S(2)}) collective-permute-start(bf16[2,320,384]{2,1,0:T(8,128)(2,1)} %get-tuple-element.32), channel_id=1, source_target_pairs={{0,1},{1,0},{2,3},{3,2},{4,5},{5,4},{6,7},{7,6},{8,9},{9,8},{10,11... | collective-permute-start | bytes 1474568 | tf_op jit(solution)/shard_map/ppermute | solution.py:431
  76.0 17.9 %collective-permute-start.2 = (bf16[320,384]{1,0:T(8,128)(2,1)S(1)}, bf16[320,384]{1,0:T(8,128)(2,1)S(1)}, u32[]{:S(2)}, u32[]{:S(2)}) collective-permute-start(bf16[320,384]{1,0:T(8,128)(2,1)S(1)} %dynamic-slice_bitcast_fusion), channel_id=1, source_target_pairs={{0,2},{2,0},{1,3},{3,1},{4,6},{6,4},{5,7},{7,5},{8,10},{10,8},{9,1... | collective-permute-start | bytes 737288 | tf_op jit(solution)/shard_map/ppermute | solution.py:434
  84.7 19.3 %all-to-all-start.3 = ((bf16[16,8,640]{2,1,0:T(8,128)(2,1)}), bf16[16,8,640]{2,1,0:T(8,128)(2,1)S(1)}, u32[]{:S(2)}, u32[]{:S(2)}) async-start(bf16[16,8,640]{2,1,0:T(8,128)(2,1)} %bitcast.16), calls=%async_computation.3 | async-start | bytes 327680 | tf_op jit(solution)/shard_map/all_to_all | solution.py:438

commit v12 on v11

--- a/solution.py
+++ b/solution.py
@@ -173,9 +173,9 @@
 
 
 def attention_kernel(
-    q_in, k_in, v_in, tok_in, pair_ref, gt_ref, ot_out, dq_out, dk_out, dv_out, pack_out,
+    q_in, k_in, v_in, tok_in, pair_ref, gt_ref, ot_out, grads_out, pack_out,
     q_ref, k_ref, v_ref, tok_ref, wide_ref, r_ref, dqt_ref, dw_ref,
-    ot_ref, dq_ref, dk_ref, dv_ref, pack_ref, in_sem, out_sem,
+    ot_ref, grads_ref, pack_ref, in_sem, out_sem,
 ):
     pairs = ((k_in, k_ref), (q_in, q_ref), (v_in, v_ref), (tok_in, tok_ref))
     loads = [pltpu.make_async_copy(a, b, in_sem.at[i]) for i, (a, b) in enumerate(pairs)]
@@ -210,8 +210,8 @@
         dqt_ref[lo:hi, :] = dot(k, ds, 0, 0) * SCALE
         dk = dot(ds, q, 1, 0) * SCALE
         dv = dot(p_low, g_all[:, lo:hi], 1, 0)
-        dk_ref[:, lo:hi] = dk[:P_SIZE].astype(BF16)
-        dv_ref[:, lo:hi] = dv[:P_SIZE].astype(BF16)
+        grads_ref[:, WIDTH + lo : WIDTH + hi] = dk[:P_SIZE].astype(BF16)
+        grads_ref[:, 2 * WIDTH + lo : 2 * WIDTH + hi] = dv[:P_SIZE].astype(BF16)
         for col, part in ((lo, dk), (WIDTH + lo, dv)):
             for chunk in range(N_FIRST):
                 for row in range(REF_ROWS):
@@ -228,9 +228,9 @@
             ahead = scores(head + 1)
         write(head, *soften(*now))
     dq = dqt_ref[...].T.astype(BF16)
-    dq_ref[...] = dq
+    grads_ref[:, :WIDTH] = dq
     loads[3].wait()
-    pairs = ((ot_ref, ot_out), (dq_ref, dq_out), (dk_ref, dk_out), (dv_ref, dv_out))
+    pairs = ((ot_ref, ot_out), (grads_ref, grads_out))
     stores = [pltpu.make_async_copy(a, b, out_sem.at[N_FIRST + i]) for i, (a, b) in enumerate(pairs)]
     for store in stores:
         store.start()
@@ -265,10 +265,10 @@
     return pl.pallas_call(
         attention_kernel,
         out_shape=(pltpu.HBM((WIDTH, P_SIZE), BF16),)
-        + (pltpu.HBM((P_SIZE, WIDTH), BF16),) * 3
+        + (pltpu.HBM((P_SIZE, 3 * WIDTH), BF16),)
         + (pltpu.HBM((N_FIRST, N_SECOND * rows, 2 * WIDTH), BF16),),
         in_specs=[hbm] * 4 + [vmem] * 2,
-        out_specs=[hbm] * 5,
+        out_specs=[hbm] * 3,
         scratch_shapes=[pltpu.VMEM((P_SIZE, WIDTH), BF16)] * 3
         + [
             pltpu.VMEM((4 * WIDTH, P_SIZE), BF16),
@@ -277,35 +277,29 @@
             pltpu.VMEM((WIDTH, P_SIZE), F32),
             pltpu.VMEM((3, WIDTH, LANES), F32),
             pltpu.VMEM((WIDTH, P_SIZE), BF16),
-            pltpu.VMEM((P_SIZE, WIDTH), BF16),
-            pltpu.VMEM((P_SIZE, WIDTH), BF16),
-            pltpu.VMEM((P_SIZE, WIDTH), BF16),
+            pltpu.VMEM((P_SIZE, 3 * WIDTH), BF16),
             pltpu.VMEM((N_FIRST, N_SECOND * rows, 2 * WIDTH), BF16),
             pltpu.SemaphoreType.DMA((4,)),
-            pltpu.SemaphoreType.DMA((N_FIRST + 4,)),
+            pltpu.SemaphoreType.DMA((N_FIRST + 2,)),
         ],
         compiler_params=pltpu.CompilerParams(vmem_limit_bytes=VMEM_BYTES),
     )(*[pltpu.with_memory_space_constraint(a, pltpu.HBM) for a in (q, k, v, tok)], pair, gt)
 
 
 def token_kernel(
-    core_ref, dq_in, dk_in, dv_in, wq_in, wk_in, wv_in, kept_out, sent_out,
-    dq_ref, dk_ref, dv_ref, wq_ref, wk_ref, wv_ref, kept_ref, sent_ref, in_sem, out_sem,
+    core_ref, grads_in, wq_in, wk_in, wv_in, kept_out, sent_out,
+    grads_ref, w_ref, kept_ref, sent_ref, in_sem, out_sem,
 ):
-    pairs = (
-        (wq_in, wq_ref), (dq_in, dq_ref), (wk_in, wk_ref),
-        (dk_in, dk_ref), (wv_in, wv_ref), (dv_in, dv_ref),
-    )
+    pairs = [(grads_in, grads_ref)]
+    for i, w_in in enumerate((wq_in, wk_in, wv_in)):
+        pairs.append((w_in, w_ref.at[pl.ds(i * WIDTH, WIDTH)]))
     loads = [pltpu.make_async_copy(a, b, in_sem.at[i]) for i, (a, b) in enumerate(pairs)]
     for load in loads:
         load.start()
     core = core_ref[0]
-    total = None
-    for i, (d_ref, w_ref) in enumerate(((dq_ref, wq_ref), (dk_ref, wk_ref), (dv_ref, wv_ref))):
-        loads[2 * i].wait()
-        loads[2 * i + 1].wait()
-        part = dot(d_ref[...], w_ref[...], 1, 0)
-        total = part if total is None else total + part
+    for load in loads:
+        load.wait()
+    total = dot(grads_ref[...], w_ref[...], 1, 0)
     total = total.T.astype(BF16)
     stores = []
     for half in range(2):
@@ -320,22 +314,24 @@
         store.wait()
 
 
-def token_parts(core, dq, dk, dv, wq, wk, wv):
+def token_parts(core, grads, wq, wk, wv):
     hbm = pl.BlockSpec(memory_space=pltpu.HBM)
     return pl.pallas_call(
         token_kernel,
         out_shape=(pltpu.HBM((2, WIDTH, P_SIZE), BF16),) * 2,
-        in_specs=[pl.BlockSpec(memory_space=pltpu.SMEM)] + [hbm] * 6,
+        in_specs=[pl.BlockSpec(memory_space=pltpu.SMEM)] + [hbm] * 4,
         out_specs=[hbm] * 2,
-        scratch_shapes=[pltpu.VMEM((P_SIZE, WIDTH), BF16)] * 3
-        + [pltpu.VMEM((WIDTH, 4 * WIDTH), BF16)] * 3
+        scratch_shapes=[
+            pltpu.VMEM((P_SIZE, 3 * WIDTH), BF16),
+            pltpu.VMEM((3 * WIDTH, 4 * WIDTH), BF16),
+        ]
         + [pltpu.VMEM((2, WIDTH, P_SIZE), BF16)] * 2
-        + [pltpu.SemaphoreType.DMA((6,)), pltpu.SemaphoreType.DMA((4,))],
+        + [pltpu.SemaphoreType.DMA((4,)), pltpu.SemaphoreType.DMA((4,))],
         cost_estimate=pl.CostEstimate(flops=1, bytes_accessed=1, transcendentals=0),
         compiler_params=pltpu.CompilerParams(vmem_limit_bytes=VMEM_BYTES),
     )(
         core.reshape(1),
-        *[pltpu.with_memory_space_constraint(a, pltpu.HBM) for a in (dq, dk, dv, wq, wk, wv)],
+        *[pltpu.with_memory_space_constraint(a, pltpu.HBM) for a in (grads, wq, wk, wv)],
     )
 
 
@@ -423,11 +419,11 @@
     pair = lax.all_to_all(spread(pair), FIRST, 0, 0, tiled=True)
     parts = lax.all_gather(blocks, "c", axis=0, tiled=False)
     tok, queries, keys, values = project(half, parts, wq, wk, wv)
-    attended, query_grads, key_grads, value_grads, pack = attention(
+    attended, grads, pack = attention(
         queries, keys, values, pair.reshape(N_FRAMES * 16, LANES), cotangent.T, tok
     )
     pack = lax.all_to_all(pack, FIRST, 0, 0, tiled=True)
-    kept, sent = token_parts(core, query_grads, key_grads, value_grads, wq, wk, wv)
+    kept, sent = token_parts(core, grads, wq, wk, wv)
     got = lax.ppermute(sent, "c", swap)
     paired = (kept.astype(F32) + got.astype(F32)).astype(BF16)
     sent = lax.dynamic_index_in_dim(paired, 1 - half, 0, False)

time: 106 us -> 106 us (level)
  no operation moved by 1% of the time
where the time goes in v12:
time: 106 us; the launch traced here: 105 us
  starting transfers between devices  44.8 us (42%)
  Pallas kernels  23.1 us (22%)
  blocking collectives  20 us (19%)
  waiting for transfers between devices  14.2 us (13%)
  other arithmetic  1.15 us (1%)
    all_gather x1, blocking collectives, per_device(): ref_hidden = lax.all_gather(cols, TENSOR, axis=0, tiled=False)  15.8 us
    all_to_all x1, starting transfers between devices, per_device(): pack = lax.all_to_all(pack, SECOND, 0, 0, tiled=True)  9.63 us
    all_to_all x1, waiting for transfers between devices, per_device(): pack = lax.all_to_all(pack, SECOND, 0, 0, tiled=True)  9.31 us
    pallas_call x1, Pallas kernels, attention(): pl.pallas_call(attention_kernel, out_shape=(pltpu.HBM((WIDTH, P_SIZE), BF...  8.84 us
    ppermute x1, starting transfers between devices, per_device(): got = lax.ppermute(sent, 'h', swap)  7.78 us
    ppermute x1, starting transfers between devices, per_device(): other = lax.ppermute(own, 'h', swap)  7.52 us
    all_to_all x1, starting transfers between devices, per_device(): lax.all_to_all(pair, SECOND, 0, 0, tiled=True).reshape(N_SECOND * 16, LANES)  7.41 us
    all_to_all x1, starting transfers between devices, per_device(): pack = lax.all_to_all(pack, FIRST, 0, 0, tiled=True)  4.23 us
  transfers between devices with their start and end apart: 7, of which 4 were waited for; matrix products, arithmetic and copies ran while one was open for 1% of the time, Pallas kernels for 9%

profile of v12, /device:TPU:1, one launch (start us, length us, event | category | flops | bytes accessed | tf_op | source)
XLA Modules:
  0.0 104.9 jit_solution(15795277838908917152)
XLA Ops:
  0.6 0.0 copy-start.4
  0.7 0.7 copy-done.4
  1.3 0.0 copy-start.5
  1.3 1.5 %shard_map.110 = bf16[16,320]{1,0:T(8,128)(2,1)S(1)} custom-call(s32[1]{0:T(128)} %bitcast.1.at_ref, bf16[3,1280]{1,0:T(4,128)(2,1)S(1)} %copy-done.4, bf16[320,1280]{1,0:T(8,128)(2,1)} %bitcast.33), custom_call_target="tpu_custom_call" | custom-call | tf_op jit(solution)/shard_map/pallas_call | solution.py:124
  2.9 15.8 %all-gather = bf16[64,320]{1,0:T(8,128)(2,1)S(1)} all-gather(bf16[16,320]{1,0:T(8,128)(2,1)S(1)} %shard_map.110), channel_id=2, replica_groups=mesh['x'=4,'yh'=4,'yl'=2,'z'=4,'h'=2,'c'=2] {'h','c'}, dimensions={0}, use_global_device_ids=true | all-gather | bytes 51200 | tf_op jit(solution)/shard_map/all_gather | solution.py:413
  18.7 2.8 %shard_map.113 = bf16[16,16,128]{2,1,0:T(8,128)(2,1)} custom-call(bf16[4,16,320]{2,1,0:T(8,128)(2,1)S(1)} %bitcast.29, bf16[320,1280]{1,0:T(8,128)(2,1)} %bitcast.18, bf16[320,1280]{1,0:T(8,128)(2,1)} %bitcast.21), custom_call_target="tpu_custom_call" | custom-call | tf_op jit(solution)/shard_map/pallas_call | solution.py:163
  21.5 7.4 %all-to-all-start = ((bf16[16,16,128]{2,1,0:T(8,128)(2,1)}), bf16[16,16,128]{2,1,0:T(8,128)(2,1)S(1)}, u32[]{:S(2)}, u32[]{:S(2)}) async-start(bf16[16,16,128]{2,1,0:T(8,128)(2,1)} %shard_map.113), calls=%async_computation | async-start | bytes 131072 | tf_op jit(solution)/shard_map/all_to_all | solution.py:417
  28.9 0.0 copy-done.5
  28.9 7.5 %collective-permute-start = (bf16[320,384]{1,0:T(8,128)(2,1)S(1)}, bf16[320,384]{1,0:T(8,128)(2,1)S(1)}, u32[]{:S(2)}, u32[]{:S(2)}) collective-permute-start(bf16[320,384]{1,0:T(8,128)(2,1)S(1)} %bitcast.31), channel_id=1, source_target_pairs={{0,2},{2,0},{1,3},{3,1},{4,6},{6,4},{5,7},{7,5},{8,10},{10,8},{9,1... | collective-permute-start | bytes 737288 | tf_op jit(solution)/shard_map/ppermute | solution.py:415
  36.5 2.0 %all-to-all-done = bf16[16,16,128]{2,1,0:T(8,128)(2,1)S(1)} async-done(((bf16[16,16,128]{2,1,0:T(8,128)(2,1)}), bf16[16,16,128]{2,1,0:T(8,128)(2,1)S(1)}, u32[]{:S(2)}, u32[]{:S(2)}) %all-to-all-start) | async-done | bytes 65568 | tf_op jit(solution)/shard_map/all_to_all | solution.py:417
  38.5 0.9 shard_map.114
  39.3 4.1 %all-to-all-start.1 = ((bf16[8,256,128]{2,1,0:T(8,128)(2,1)}), bf16[8,256,128]{2,1,0:T(8,128)(2,1)S(1)}, u32[]{:S(2)}, u32[]{:S(2)}) async-start(bf16[8,256,128]{2,1,0:T(8,128)(2,1)} %shard_map.114), calls=%async_computation.1 | async-start | bytes 1048576 | tf_op jit(solution)/shard_map/all_to_all | solution.py:419
  43.4 0.0 collective-permute-done.other_ref
  43.5 0.0 copy-start.1
  43.5 0.0 copy-start.2
  43.5 0.0 copy-start
  43.6 4.2 %all-gather.1 = bf16[4,320,384]{2,1,0:T(8,128)(2,1)S(1)} all-gather(bf16[2,320,384]{2,1,0:T(8,128)(2,1)S(1)} %shard_map.111), channel_id=3, replica_groups=mesh['x'=4,'yh'=4,'yl'=2,'z'=4,'h'=2,'c'=2] {'c'}, dimensions={0}, use_global_device_ids=true | all-gather | bytes 1474560 | tf_op jit(solution)/shard_map/all_gather | solution.py:420
  47.7 0.0 copy-done.1
  47.7 0.0 copy-done.2
  47.7 0.0 copy-done
  47.7 0.0 copy-start.3
  47.7 2.7 %shard_map.112 = (bf16[1280,384]{1,0:T(8,128)(2,1)}, bf16[384,320]{1,0:T(8,128)(2,1)}, bf16[384,320]{1,0:T(8,128)(2,1)}, bf16[384,320]{1,0:T(8,128)(2,1)}) custom-call(s32[1]{0:T(128)} %bitcast.half_ref, bf16[2,2,320,384]{3,2,1,0:T(8,128)(2,1)S(1)} %bitcast.24, bf16[320,1280]{1,0:T(8,128)(2,1)S(1)} %bitcast.26, bf16[320,1280]{1,0:T(8,128)(2,1)S(1)} %bitcast.20, ...), custom_call_target="tpu_custom_call" | custom-call | tf_op jit(solution)/shard_map/pallas_call | solution.py:96
  50.4 1.2 %all-to-all-done.1 = bf16[8,256,128]{2,1,0:T(8,128)(2,1)S(1)} async-done(((bf16[8,256,128]{2,1,0:T(8,128)(2,1)}), bf16[8,256,128]{2,1,0:T(8,128)(2,1)S(1)}, u32[]{:S(2)}, u32[]{:S(2)}) %all-to-all-start.1) | async-done | bytes 524320 | tf_op jit(solution)/shard_map/all_to_all | solution.py:419
  51.7 0.0 copy-done.3
  51.7 8.8 %shard_map.115 = (bf16[320,384]{1,0:T(8,128)(2,1)}, bf16[384,960]{1,0:T(8,128)(2,1)}, bf16[8,128,640]{2,1,0:T(8,128)(2,1)}) custom-call(bf16[384,320]{1,0:T(8,128)(2,1)} %get-tuple-element.20.q_in, bf16[384,320]{1,0:T(8,128)(2,1)} %get-tuple-element.21.k_in, bf16[384,320]{1,0:T(8,128)(2,1)} %get-tuple-element.22.v_in, ...), custom_call_target="tpu_custom_call" | custom-call | tf_op jit(solution)/shard_map/pallas_call | solution.py:265
  60.5 4.2 %all-to-all-start.2 = ((bf16[8,128,640]{2,1,0:T(8,128)(2,1)}), bf16[8,128,640]{2,1,0:T(8,128)(2,1)S(1)}, u32[]{:S(2)}, u32[]{:S(2)}) async-start(bf16[8,128,640]{2,1,0:T(8,128)(2,1)} %get-tuple-element.29), calls=%async_computation.2 | async-start | bytes 2621440 | tf_op jit(solution)/shard_map/all_to_all | solution.py:425
  64.7 4.0 %shard_map.116 = (bf16[2,320,384]{2,1,0:T(8,128)(2,1)}, bf16[2,320,384]{2,1,0:T(8,128)(2,1)}) custom-call(s32[1]{0:T(128)} %bitcast.13.core_ref, bf16[384,960]{1,0:T(8,128)(2,1)} %get-tuple-element.26.grads_in, bf16[320,1280]{1,0:T(8,128)(2,1)} %bitcast.25, bf16[320,1280]{1,0:T(8,128)(2,1)} %bitcast.19, bf16[320,1280]{1,0:T(8,128)(2,1)} %bitcast.22), custom_call_target="tpu_custom_call" | custom-call | flops 1 | bytes 1 | tf_op jit(solution)/shard_map/pallas_call | solution.py:319
  68.8 4.1 %collective-permute-start.1 = (bf16[2,320,384]{2,1,0:T(8,128)(2,1)}, bf16[2,320,384]{2,1,0:T(8,128)(2,1)S(1)}, u32[]{:S(2)}, u32[]{:S(2)}) collective-permute-start(bf16[2,320,384]{2,1,0:T(8,128)(2,1)} %get-tuple-element.28), channel_id=1, source_target_pairs={{0,1},{1,0},{2,3},{3,2},{4,5},{5,4},{6,7},{7,6},{8,9},{9,8},{10,11... | collective-permute-start | bytes 1474568 | tf_op jit(solution)/shard_map/ppermute | solution.py:427
  72.9 1.7 %collective-permute-done.1 = bf16[2,320,384]{2,1,0:T(8,128)(2,1)S(1)} collective-permute-done((bf16[2,320,384]{2,1,0:T(8,128)(2,1)}, bf16[2,320,384]{2,1,0:T(8,128)(2,1)S(1)}, u32[]{:S(2)}, u32[]{:S(2)}) %collective-permute-start.1) | collective-permute-done | bytes 491552 | tf_op jit(solution)/shard_map/ppermute | solution.py:427
  74.5 1.1 %add_convert_fusion.pair_ref = bf16[2,320,384]{2,1,0:T(8,128)(2,1)S(1)} fusion(bf16[2,320,384]{2,1,0:T(8,128)(2,1)S(1)} %collective-permute-done.1, bf16[2,320,384]{2,1,0:T(8,128)(2,1)} %get-tuple-element.27), kind=kLoop, calls=%fused_computation | loop fusion | flops 983040 | bytes 1474560 | tf_op jit(solution)/shard_map/convert_element_type | solution.py:428
  75.7 7.8 %collective-permute-start.2 = (bf16[320,384]{1,0:T(8,128)(2,1)S(1)}, bf16[320,384]{1,0:T(8,128)(2,1)S(1)}, u32[]{:S(2)}, u32[]{:S(2)}) collective-permute-start(bf16[320,384]{1,0:T(8,128)(2,1)S(1)} %dynamic-slice_bitcast_fusion), channel_id=1, source_target_pairs={{0,2},{2,0},{1,3},{3,1},{4,6},{6,4},{5,7},{7,5},{8,10},{10,8},{9,1... | collective-permute-start | bytes 737288 | tf_op jit(solution)/shard_map/ppermute | solution.py:430
  83.5 0.0 all-to-all-done.2.in_ref
  83.5 0.9 shard_map.118
  84.4 9.6 %all-to-all-start.3 = ((bf16[16,8,640]{2,1,0:T(8,128)(2,1)}), bf16[16,8,640]{2,1,0:T(8,128)(2,1)S(1)}, u32[]{:S(2)}, u32[]{:S(2)}) async-start(bf16[16,8,640]{2,1,0:T(8,128)(2,1)} %bitcast.16), calls=%async_computation.3 | async-start | bytes 327680 | tf_op jit(solution)/shard_map/all_to_all | solution.py:434
  94.0 0.0 collective-permute-done.2.got_ref
  94.1 0.8 shard_map.117
  94.8 9.3 %all-to-all-done.3.in_ref = bf16[16,8,640]{2,1,0:T(8,128)(2,1)S(1)} async-done(((bf16[16,8,640]{2,1,0:T(8,128)(2,1)}), bf16[16,8,640]{2,1,0:T(8,128)(2,1)S(1)}, u32[]{:S(2)}, u32[]{:S(2)}) %all-to-all-start.3) | async-done | bytes 163872 | tf_op jit(solution)/shard_map/all_to_all | solution.py:434
  104.2 0.7 shard_map.119
  (2 shorter events, 0.1 us)
Async XLA Ops:
  0.6 0.7 copy-start.4
  1.3 27.6 %copy-start.5 = (bf16[384,320]{0,1:T(8,128)(2,1)S(1)}, bf16[384,320]{0,1:T(8,128)(2,1)}, u32[]{:S(2)}) copy-start(bf16[384,320]{0,1:T(8,128)(2,1)} %param.7) | copy-start | bytes 737284
  21.5 17.0 %all-to-all-start = ((bf16[16,16,128]{2,1,0:T(8,128)(2,1)}), bf16[16,16,128]{2,1,0:T(8,128)(2,1)S(1)}, u32[]{:S(2)}, u32[]{:S(2)}) async-start(bf16[16,16,128]{2,1,0:T(8,128)(2,1)} %shard_map.113), calls=%async_computation | async-start | bytes 131072 | tf_op jit(solution)/shard_map/all_to_all | solution.py:417
  28.9 14.6 %collective-permute-start = (bf16[320,384]{1,0:T(8,128)(2,1)S(1)}, bf16[320,384]{1,0:T(8,128)(2,1)S(1)}, u32[]{:S(2)}, u32[]{:S(2)}) collective-permute-start(bf16[320,384]{1,0:T(8,128)(2,1)S(1)} %bitcast.31), channel_id=1, source_target_pairs={{0,2},{2,0},{1,3},{3,1},{4,6},{6,4},{5,7},{7,5},{8,10},{10,8},{9,1... | collective-permute-start | bytes 737288 | tf_op jit(solution)/shard_map/ppermute | solution.py:415
  39.3 12.3 %all-to-all-start.1 = ((bf16[8,256,128]{2,1,0:T(8,128)(2,1)}), bf16[8,256,128]{2,1,0:T(8,128)(2,1)S(1)}, u32[]{:S(2)}, u32[]{:S(2)}) async-start(bf16[8,256,128]{2,1,0:T(8,128)(2,1)} %shard_map.114), calls=%async_computation.1 | async-start | bytes 1048576 | tf_op jit(solution)/shard_map/all_to_all | solution.py:419
  43.5 4.2 %copy-start.1 = (bf16[1280,320]{0,1:T(8,128)(2,1)S(1)}, bf16[1280,320]{0,1:T(8,128)(2,1)}, u32[]{:S(2)}) copy-start(bf16[1280,320]{0,1:T(8,128)(2,1)} %param.11) | copy-start | bytes 2457604
  43.5 4.2 %copy-start.2 = (bf16[1280,320]{0,1:T(8,128)(2,1)S(1)}, bf16[1280,320]{0,1:T(8,128)(2,1)}, u32[]{:S(2)}) copy-start(bf16[1280,320]{0,1:T(8,128)(2,1)} %param.9) | copy-start | bytes 2457604
  43.5 4.2 %copy-start = (bf16[1280,320]{0,1:T(8,128)(2,1)S(1)}, bf16[1280,320]{0,1:T(8,128)(2,1)}, u32[]{:S(2)}) copy-start(bf16[1280,320]{0,1:T(8,128)(2,1)} %param.10) | copy-start | bytes 2457604
  47.7 3.9 %copy-start.3 = (bf16[384,320]{0,1:T(8,128)(2,1)S(1)}, bf16[384,320]{0,1:T(8,128)(2,1)}, u32[]{:S(2)}) copy-start(bf16[384,320]{0,1:T(8,128)(2,1)} %param.13) | copy-start | bytes 737284
  60.5 23.0 %all-to-all-start.2 = ((bf16[8,128,640]{2,1,0:T(8,128)(2,1)}), bf16[8,128,640]{2,1,0:T(8,128)(2,1)S(1)}, u32[]{:S(2)}, u32[]{:S(2)}) async-start(bf16[8,128,640]{2,1,0:T(8,128)(2,1)} %get-tuple-element.29), calls=%async_computation.2 | async-start | bytes 2621440 | tf_op jit(solution)/shard_map/all_to_all | solution.py:425
  68.8 5.8 %collective-permute-start.1 = (bf16[2,320,384]{2,1,0:T(8,128)(2,1)}, bf16[2,320,384]{2,1,0:T(8,128)(2,1)S(1)}, u32[]{:S(2)}, u32[]{:S(2)}) collective-permute-start(bf16[2,320,384]{2,1,0:T(8,128)(2,1)} %get-tuple-element.28), channel_id=1, source_target_pairs={{0,1},{1,0},{2,3},{3,2},{4,5},{5,4},{6,7},{7,6},{8,9},{9,8},{10,11... | collective-permute-start | bytes 1474568 | tf_op jit(solution)/shard_map/ppermute | solution.py:427
  75.7 18.3 %collective-permute-start.2 = (bf16[320,384]{1,0:T(8,128)(2,1)S(1)}, bf16[320,384]{1,0:T(8,128)(2,1)S(1)}, u32[]{:S(2)}, u32[]{:S(2)}) collective-permute-start(bf16[320,384]{1,0:T(8,128)(2,1)S(1)} %dynamic-slice_bitcast_fusion), channel_id=1, source_target_pairs={{0,2},{2,0},{1,3},{3,1},{4,6},{6,4},{5,7},{7,5},{8,10},{10,8},{9,1... | collective-permute-start | bytes 737288 | tf_op jit(solution)/shard_map/ppermute | solution.py:430
  84.4 19.7 %all-to-all-start.3 = ((bf16[16,8,640]{2,1,0:T(8,128)(2,1)}), bf16[16,8,640]{2,1,0:T(8,128)(2,1)S(1)}, u32[]{:S(2)}, u32[]{:S(2)}) async-start(bf16[16,8,640]{2,1,0:T(8,128)(2,1)} %bitcast.16), calls=%async_computation.3 | async-start | bytes 327680 | tf_op jit(solution)/shard_map/all_to_all | solution.py:434

commit v13 on v12

--- a/solution.py
+++ b/solution.py
@@ -136,14 +136,19 @@
     )(at.reshape(1), image, pltpu.with_memory_space_constraint(wr, pltpu.HBM))
 
 
-def ref_kernel(g_ref, wk_in, wv_in, out_ref, rows_ref, wk_ref, wv_ref, sem):
+def ref_kernel(half_ref, g_ref, wk_in, wv_in, out_ref, rows_ref, wk_ref, wv_ref, sem):
     loads = [
         pltpu.make_async_copy(a, b, sem.at[i])
         for i, (a, b) in enumerate(((wk_in, wk_ref), (wv_in, wv_ref)))
     ]
     for load in loads:
         load.start()
-    hidden = [g_ref[t].astype(F32) for t in range(4)]
+    first = half_ref[0] == 0
+    hidden = []
+    for low in range(2):
+        for c in range(2):
+            own, other = g_ref[c, low].astype(F32), g_ref[c, 1 - low].astype(F32)
+            hidden.append(jnp.where(first, own, other))
     hidden = jnp.concatenate(hidden, axis=1).astype(BF16)
     rows_ref[...] = jnp.zeros_like(rows_ref)
     pair = []
@@ -158,18 +163,18 @@
     out_ref[...] = jnp.broadcast_to(rows_ref[...].astype(BF16)[None], out_ref.shape)
 
 
-def ref_pair(gathered, wk, wv):
+def ref_pair(half, gathered, wk, wv):
     hbm, vmem = [pl.BlockSpec(memory_space=space) for space in (pltpu.HBM, pltpu.VMEM)]
     return pl.pallas_call(
         ref_kernel,
         out_shape=jax.ShapeDtypeStruct((N_SECOND, 16, LANES), BF16),
-        in_specs=[vmem, hbm, hbm],
+        in_specs=[pl.BlockSpec(memory_space=pltpu.SMEM), vmem, hbm, hbm],
         out_specs=vmem,
         scratch_shapes=[pltpu.VMEM((16, LANES), F32)]
         + [pltpu.VMEM((WIDTH, 4 * WIDTH), BF16)] * 2
         + [pltpu.SemaphoreType.DMA((2,))],
         compiler_params=pltpu.CompilerParams(vmem_limit_bytes=12 * 1024 * 1024),
-    )(gathered, *[pltpu.with_memory_space_constraint(a, pltpu.HBM) for a in (wk, wv)])
+    )(half.reshape(1), gathered, *[pltpu.with_memory_space_constraint(a, pltpu.HBM) for a in (wk, wv)])
 
 
 def attention_kernel(
@@ -410,10 +415,11 @@
     swap = [(0, 1), (1, 0)]
     wq, wk, wv = query_weight.T, key_weight.T, value_weight.T
     cols = ref_cols(2 * half + core, reference_image, ref_weight.T)
-    ref_hidden = lax.all_gather(cols, TENSOR, axis=0, tiled=False)
+    cols = jnp.stack([cols, lax.ppermute(cols, "h", swap)])
+    ref_hidden = lax.all_gather(cols, "c", axis=0, tiled=False)
     ref_hidden, own = lax.optimization_barrier((ref_hidden, tokens.T))
     other = lax.ppermute(own, "h", swap)
-    pair = ref_pair(ref_hidden, wk, wv)
+    pair = ref_pair(half, ref_hidden, wk, wv)
     pair = lax.all_to_all(pair, SECOND, 0, 0, tiled=True).reshape(N_SECOND * 16, LANES)
     blocks = stack(own, other)
     pair = lax.all_to_all(spread(pair), FIRST, 0, 0, tiled=True)

time: 106 us -> 108 us (1.019)
  starting transfers between devices: 44.8 us -> 56.8 us
  blocking collectives: 20 us -> 9.73 us
    ppermute x0 -> x1, starting transfers between devices: none -> 11.5 us  [per_device(): cols = jnp.stack([cols, lax.ppermute(cols, 'h', swap)])]
    all_gather x1, blocking collectives: 15.8 us -> 5.32 us  [per_device(): ref_hidden = lax.all_gather(cols, 'c', axis=0, tiled=False)]
    ppermute x0 -> x1, waiting for transfers between devices: none -> 1.08 us  [per_device(): cols = jnp.stack([cols, lax.ppermute(cols, 'h', swap)])]
  transfers between devices with their start and end apart: 7 -> 8, of which waited for: 4 -> 5; matrix products, arithmetic and copies ran while one was open for 1% -> 1% of each run, Pallas kernels for 9% -> 9%
where the time goes in v13:
time: 108 us; the launch traced here: 107 us
  starting transfers between devices  56.8 us (53%)
  Pallas kernels  23.1 us (21%)
  waiting for transfers between devices  14.4 us (13%)
  blocking collectives  9.73 us (9%)
  other arithmetic  1.16 us (1%)
    ppermute x1, starting transfers between devices, per_device(): cols = jnp.stack([cols, lax.ppermute(cols, 'h', swap)])  11.5 us
    all_to_all x1, starting transfers between devices, per_device(): pack = lax.all_to_all(pack, SECOND, 0, 0, tiled=True)  9.67 us
    all_to_all x1, waiting for transfers between devices, per_device(): pack = lax.all_to_all(pack, SECOND, 0, 0, tiled=True)  9.31 us
    pallas_call x1, Pallas kernels, attention(): pl.pallas_call(attention_kernel, out_shape=(pltpu.HBM((WIDTH, P_SIZE), BF...  8.82 us
    ppermute x1, starting transfers between devices, per_device(): got = lax.ppermute(sent, 'h', swap)  7.75 us
    ppermute x1, starting transfers between devices, per_device(): other = lax.ppermute(own, 'h', swap)  7.55 us
    all_to_all x1, starting transfers between devices, per_device(): lax.all_to_all(pair, SECOND, 0, 0, tiled=True).reshape(N_SECOND * 16, LANES)  7.38 us
    all_gather x1, blocking collectives, per_device(): ref_hidden = lax.all_gather(cols, 'c', axis=0, tiled=False)  5.32 us
  transfers between devices with their start and end apart: 8, of which 5 were waited for; matrix products, arithmetic and copies ran while one was open for 1% of the time, Pallas kernels for 9%

profile of v13, /device:TPU:1, one launch (start us, length us, event | category | flops | bytes accessed | tf_op | source)
XLA Modules:
  0.0 106.9 jit_solution(9378613940289963698)
XLA Ops:
  0.6 0.0 copy-start.4
  0.7 0.7 copy-done.4
  1.3 0.0 copy-start.5
  1.3 1.5 %shard_map.110 = bf16[16,320]{1,0:T(8,128)(2,1)S(1)} custom-call(s32[1]{0:T(128)} %bitcast.1.at_ref, bf16[3,1280]{1,0:T(4,128)(2,1)S(1)} %copy-done.4, bf16[320,1280]{1,0:T(8,128)(2,1)} %bitcast.36), custom_call_target="tpu_custom_call" | custom-call | tf_op jit(solution)/shard_map/pallas_call | solution.py:124
  2.9 11.5 %collective-permute-start = (bf16[16,320]{1,0:T(8,128)(2,1)S(1)}, bf16[16,320]{1,0:T(8,128)(2,1)S(1)}, u32[]{:S(2)}, u32[]{:S(2)}) collective-permute-start(bf16[16,320]{1,0:T(8,128)(2,1)S(1)} %shard_map.110), channel_id=1, source_target_pairs={{0,2},{2,0},{1,3},{3,1},{4,6},{6,4},{5,7},{7,5},{8,10},{10,8},{9,1... | collective-permute-start | bytes 30728 | tf_op jit(solution)/shard_map/ppermute | solution.py:418
  14.4 1.1 %collective-permute-done = bf16[16,320]{1,0:T(8,128)(2,1)S(1)} collective-permute-done((bf16[16,320]{1,0:T(8,128)(2,1)S(1)}, bf16[16,320]{1,0:T(8,128)(2,1)S(1)}, u32[]{:S(2)}, u32[]{:S(2)}) %collective-permute-start) | collective-permute-done | bytes 10272 | tf_op jit(solution)/shard_map/ppermute | solution.py:418
  15.5 5.3 %all-gather = bf16[4,16,320]{2,1,0:T(8,128)(2,1)S(1)} all-gather(bf16[2,16,320]{2,1,0:T(8,128)(2,1)S(1)} %pad_maximum_fusion), channel_id=2, replica_groups=mesh['x'=4,'yh'=4,'yl'=2,'z'=4,'h'=2,'c'=2] {'c'}, dimensions={0}, use_global_device_ids=true | all-gather | bytes 61440 | tf_op jit(solution)/shard_map/all_gather | solution.py:419
  20.8 2.8 %shard_map.113 = bf16[16,16,128]{2,1,0:T(8,128)(2,1)} custom-call(s32[1]{0:T(128)} %bitcast.half_ref, bf16[2,2,16,320]{3,2,1,0:T(8,128)(2,1)S(1)} %bitcast.31, bf16[320,1280]{1,0:T(8,128)(2,1)} %bitcast.20, bf16[320,1280]{1,0:T(8,128)(2,1)} %bitcast.23), custom_call_target="tpu_custom_call" | custom-call | tf_op jit(solution)/shard_map/pallas_call | solution.py:168
  23.6 7.4 %all-to-all-start = ((bf16[16,16,128]{2,1,0:T(8,128)(2,1)}), bf16[16,16,128]{2,1,0:T(8,128)(2,1)S(1)}, u32[]{:S(2)}, u32[]{:S(2)}) async-start(bf16[16,16,128]{2,1,0:T(8,128)(2,1)} %shard_map.113), calls=%async_computation | async-start | bytes 131072 | tf_op jit(solution)/shard_map/all_to_all | solution.py:423
  30.9 0.0 copy-done.5
  31.0 7.5 %collective-permute-start.1 = (bf16[320,384]{1,0:T(8,128)(2,1)S(1)}, bf16[320,384]{1,0:T(8,128)(2,1)S(1)}, u32[]{:S(2)}, u32[]{:S(2)}) collective-permute-start(bf16[320,384]{1,0:T(8,128)(2,1)S(1)} %bitcast.34), channel_id=1, source_target_pairs={{0,2},{2,0},{1,3},{3,1},{4,6},{6,4},{5,7},{7,5},{8,10},{10,8},{9,1... | collective-permute-start | bytes 737288 | tf_op jit(solution)/shard_map/ppermute | solution.py:421
  38.5 1.9 %all-to-all-done = bf16[16,16,128]{2,1,0:T(8,128)(2,1)S(1)} async-done(((bf16[16,16,128]{2,1,0:T(8,128)(2,1)}), bf16[16,16,128]{2,1,0:T(8,128)(2,1)S(1)}, u32[]{:S(2)}, u32[]{:S(2)}) %all-to-all-start) | async-done | bytes 65568 | tf_op jit(solution)/shard_map/all_to_all | solution.py:423
  40.4 0.9 shard_map.114
  41.3 4.2 %all-to-all-start.1 = ((bf16[8,256,128]{2,1,0:T(8,128)(2,1)}), bf16[8,256,128]{2,1,0:T(8,128)(2,1)S(1)}, u32[]{:S(2)}, u32[]{:S(2)}) async-start(bf16[8,256,128]{2,1,0:T(8,128)(2,1)} %shard_map.114), calls=%async_computation.1 | async-start | bytes 1048576 | tf_op jit(solution)/shard_map/all_to_all | solution.py:425
  45.5 0.0 collective-permute-done.1.other_ref
  45.5 0.0 copy-start.1
  45.5 0.0 copy-start.2
  45.6 0.0 copy-start
  45.6 4.4 %all-gather.1 = bf16[4,320,384]{2,1,0:T(8,128)(2,1)S(1)} all-gather(bf16[2,320,384]{2,1,0:T(8,128)(2,1)S(1)} %shard_map.111), channel_id=3, replica_groups=mesh['x'=4,'yh'=4,'yl'=2,'z'=4,'h'=2,'c'=2] {'c'}, dimensions={0}, use_global_device_ids=true | all-gather | bytes 1474560 | tf_op jit(solution)/shard_map/all_gather | solution.py:426
  50.0 0.0 copy-done.1
  50.0 0.0 copy-done.2
  50.0 0.0 copy-done
  50.0 0.0 copy-start.3
  50.0 2.7 %shard_map.112 = (bf16[1280,384]{1,0:T(8,128)(2,1)}, bf16[384,320]{1,0:T(8,128)(2,1)}, bf16[384,320]{1,0:T(8,128)(2,1)}, bf16[384,320]{1,0:T(8,128)(2,1)}) custom-call(s32[1]{0:T(128)} %bitcast.half_ref, bf16[2,2,320,384]{3,2,1,0:T(8,128)(2,1)S(1)} %bitcast.26, bf16[320,1280]{1,0:T(8,128)(2,1)S(1)} %bitcast.28, bf16[320,1280]{1,0:T(8,128)(2,1)S(1)} %bitcast.22, ...), custom_call_target="tpu_custom_call" | custom-call | tf_op jit(solution)/shard_map/pallas_call | solution.py:96
  52.7 0.5 all-to-all-done.1
  53.2 0.0 copy-done.3
  53.2 8.8 %shard_map.115 = (bf16[320,384]{1,0:T(8,128)(2,1)}, bf16[384,960]{1,0:T(8,128)(2,1)}, bf16[8,128,640]{2,1,0:T(8,128)(2,1)}) custom-call(bf16[384,320]{1,0:T(8,128)(2,1)} %get-tuple-element.20.q_in, bf16[384,320]{1,0:T(8,128)(2,1)} %get-tuple-element.21.k_in, bf16[384,320]{1,0:T(8,128)(2,1)} %get-tuple-element.22.v_in, ...), custom_call_target="tpu_custom_call" | custom-call | tf_op jit(solution)/shard_map/pallas_call | solution.py:270
  62.0 5.0 %all-to-all-start.2 = ((bf16[8,128,640]{2,1,0:T(8,128)(2,1)}), bf16[8,128,640]{2,1,0:T(8,128)(2,1)S(1)}, u32[]{:S(2)}, u32[]{:S(2)}) async-start(bf16[8,128,640]{2,1,0:T(8,128)(2,1)} %get-tuple-element.29), calls=%async_computation.2 | async-start | bytes 2621440 | tf_op jit(solution)/shard_map/all_to_all | solution.py:431
  67.0 4.0 %shard_map.116 = (bf16[2,320,384]{2,1,0:T(8,128)(2,1)}, bf16[2,320,384]{2,1,0:T(8,128)(2,1)}) custom-call(s32[1]{0:T(128)} %bitcast.15.core_ref, bf16[384,960]{1,0:T(8,128)(2,1)} %get-tuple-element.26.grads_in, bf16[320,1280]{1,0:T(8,128)(2,1)} %bitcast.27, bf16[320,1280]{1,0:T(8,128)(2,1)} %bitcast.21, bf16[320,1280]{1,0:T(8,128)(2,1)} %bitcast.24), custom_call_target="tpu_custom_call" | custom-call | flops 1 | bytes 1 | tf_op jit(solution)/shard_map/pallas_call | solution.py:324
  71.0 3.9 %collective-permute-start.2 = (bf16[2,320,384]{2,1,0:T(8,128)(2,1)}, bf16[2,320,384]{2,1,0:T(8,128)(2,1)S(1)}, u32[]{:S(2)}, u32[]{:S(2)}) collective-permute-start(bf16[2,320,384]{2,1,0:T(8,128)(2,1)} %get-tuple-element.28), channel_id=1, source_target_pairs={{0,1},{1,0},{2,3},{3,2},{4,5},{5,4},{6,7},{7,6},{8,9},{9,8},{10,11... | collective-permute-start | bytes 1474568 | tf_op jit(solution)/shard_map/ppermute | solution.py:433
  74.9 1.7 %collective-permute-done.2 = bf16[2,320,384]{2,1,0:T(8,128)(2,1)S(1)} collective-permute-done((bf16[2,320,384]{2,1,0:T(8,128)(2,1)}, bf16[2,320,384]{2,1,0:T(8,128)(2,1)S(1)}, u32[]{:S(2)}, u32[]{:S(2)}) %collective-permute-start.2) | collective-permute-done | bytes 491552 | tf_op jit(solution)/shard_map/ppermute | solution.py:433
  76.6 1.1 %add_convert_fusion.pair_ref = bf16[2,320,384]{2,1,0:T(8,128)(2,1)S(1)} fusion(bf16[2,320,384]{2,1,0:T(8,128)(2,1)S(1)} %collective-permute-done.2, bf16[2,320,384]{2,1,0:T(8,128)(2,1)} %get-tuple-element.27), kind=kLoop, calls=%fused_computation | loop fusion | flops 983040 | bytes 1474560 | tf_op jit(solution)/shard_map/convert_element_type | solution.py:434
  77.8 7.8 %collective-permute-start.3 = (bf16[320,384]{1,0:T(8,128)(2,1)S(1)}, bf16[320,384]{1,0:T(8,128)(2,1)S(1)}, u32[]{:S(2)}, u32[]{:S(2)}) collective-permute-start(bf16[320,384]{1,0:T(8,128)(2,1)S(1)} %dynamic-slice_bitcast_fusion), channel_id=1, source_target_pairs={{0,2},{2,0},{1,3},{3,1},{4,6},{6,4},{5,7},{7,5},{8,10},{10,8},{9,1... | collective-permute-start | bytes 737288 | tf_op jit(solution)/shard_map/ppermute | solution.py:436
  85.5 0.0 all-to-all-done.2.in_ref
  85.5 0.9 shard_map.118
  86.4 9.7 %all-to-all-start.3 = ((bf16[16,8,640]{2,1,0:T(8,128)(2,1)}), bf16[16,8,640]{2,1,0:T(8,128)(2,1)S(1)}, u32[]{:S(2)}, u32[]{:S(2)}) async-start(bf16[16,8,640]{2,1,0:T(8,128)(2,1)} %bitcast.18), calls=%async_computation.3 | async-start | bytes 327680 | tf_op jit(solution)/shard_map/all_to_all | solution.py:440
  96.1 0.0 collective-permute-done.3.got_ref
  96.1 0.8 shard_map.117
  96.9 9.3 %all-to-all-done.3.in_ref = bf16[16,8,640]{2,1,0:T(8,128)(2,1)S(1)} async-done(((bf16[16,8,640]{2,1,0:T(8,128)(2,1)}), bf16[16,8,640]{2,1,0:T(8,128)(2,1)S(1)}, u32[]{:S(2)}, u32[]{:S(2)}) %all-to-all-start.3) | async-done | bytes 163872 | tf_op jit(solution)/shard_map/all_to_all | solution.py:440
  106.2 0.7 shard_map.119
  (3 shorter events, 0.1 us)
Async XLA Ops:
  0.6 0.7 copy-start.4
  1.3 29.6 %copy-start.5 = (bf16[384,320]{0,1:T(8,128)(2,1)S(1)}, bf16[384,320]{0,1:T(8,128)(2,1)}, u32[]{:S(2)}) copy-start(bf16[384,320]{0,1:T(8,128)(2,1)} %param.7) | copy-start | bytes 737284
  2.9 12.6 %collective-permute-start = (bf16[16,320]{1,0:T(8,128)(2,1)S(1)}, bf16[16,320]{1,0:T(8,128)(2,1)S(1)}, u32[]{:S(2)}, u32[]{:S(2)}) collective-permute-start(bf16[16,320]{1,0:T(8,128)(2,1)S(1)} %shard_map.110), channel_id=1, source_target_pairs={{0,2},{2,0},{1,3},{3,1},{4,6},{6,4},{5,7},{7,5},{8,10},{10,8},{9,1... | collective-permute-start | bytes 30728 | tf_op jit(solution)/shard_map/ppermute | solution.py:418
  23.6 16.9 %all-to-all-start = ((bf16[16,16,128]{2,1,0:T(8,128)(2,1)}), bf16[16,16,128]{2,1,0:T(8,128)(2,1)S(1)}, u32[]{:S(2)}, u32[]{:S(2)}) async-start(bf16[16,16,128]{2,1,0:T(8,128)(2,1)} %shard_map.113), calls=%async_computation | async-start | bytes 131072 | tf_op jit(solution)/shard_map/all_to_all | solution.py:423
  31.0 14.5 %collective-permute-start.1 = (bf16[320,384]{1,0:T(8,128)(2,1)S(1)}, bf16[320,384]{1,0:T(8,128)(2,1)S(1)}, u32[]{:S(2)}, u32[]{:S(2)}) collective-permute-start(bf16[320,384]{1,0:T(8,128)(2,1)S(1)} %bitcast.34), channel_id=1, source_target_pairs={{0,2},{2,0},{1,3},{3,1},{4,6},{6,4},{5,7},{7,5},{8,10},{10,8},{9,1... | collective-permute-start | bytes 737288 | tf_op jit(solution)/shard_map/ppermute | solution.py:421
  41.3 11.8 %all-to-all-start.1 = ((bf16[8,256,128]{2,1,0:T(8,128)(2,1)}), bf16[8,256,128]{2,1,0:T(8,128)(2,1)S(1)}, u32[]{:S(2)}, u32[]{:S(2)}) async-start(bf16[8,256,128]{2,1,0:T(8,128)(2,1)} %shard_map.114), calls=%async_computation.1 | async-start | bytes 1048576 | tf_op jit(solution)/shard_map/all_to_all | solution.py:425
  45.5 4.5 %copy-start.1 = (bf16[1280,320]{0,1:T(8,128)(2,1)S(1)}, bf16[1280,320]{0,1:T(8,128)(2,1)}, u32[]{:S(2)}) copy-start(bf16[1280,320]{0,1:T(8,128)(2,1)} %param.11) | copy-start | bytes 2457604
  45.5 4.5 %copy-start.2 = (bf16[1280,320]{0,1:T(8,128)(2,1)S(1)}, bf16[1280,320]{0,1:T(8,128)(2,1)}, u32[]{:S(2)}) copy-start(bf16[1280,320]{0,1:T(8,128)(2,1)} %param.9) | copy-start | bytes 2457604
  45.6 4.4 %copy-start = (bf16[1280,320]{0,1:T(8,128)(2,1)S(1)}, bf16[1280,320]{0,1:T(8,128)(2,1)}, u32[]{:S(2)}) copy-start(bf16[1280,320]{0,1:T(8,128)(2,1)} %param.10) | copy-start | bytes 2457604
  50.0 3.2 %copy-start.3 = (bf16[384,320]{0,1:T(8,128)(2,1)S(1)}, bf16[384,320]{0,1:T(8,128)(2,1)}, u32[]{:S(2)}) copy-start(bf16[384,320]{0,1:T(8,128)(2,1)} %param.13) | copy-start | bytes 737284
  62.0 23.5 %all-to-all-start.2 = ((bf16[8,128,640]{2,1,0:T(8,128)(2,1)}), bf16[8,128,640]{2,1,0:T(8,128)(2,1)S(1)}, u32[]{:S(2)}, u32[]{:S(2)}) async-start(bf16[8,128,640]{2,1,0:T(8,128)(2,1)} %get-tuple-element.29), calls=%async_computation.2 | async-start | bytes 2621440 | tf_op jit(solution)/shard_map/all_to_all | solution.py:431
  71.0 5.5 %collective-permute-start.2 = (bf16[2,320,384]{2,1,0:T(8,128)(2,1)}, bf16[2,320,384]{2,1,0:T(8,128)(2,1)S(1)}, u32[]{:S(2)}, u32[]{:S(2)}) collective-permute-start(bf16[2,320,384]{2,1,0:T(8,128)(2,1)} %get-tuple-element.28), channel_id=1, source_target_pairs={{0,1},{1,0},{2,3},{3,2},{4,5},{5,4},{6,7},{7,6},{8,9},{9,8},{10,11... | collective-permute-start | bytes 1474568 | tf_op jit(solution)/shard_map/ppermute | solution.py:433
  77.8 18.3 %collective-permute-start.3 = (bf16[320,384]{1,0:T(8,128)(2,1)S(1)}, bf16[320,384]{1,0:T(8,128)(2,1)S(1)}, u32[]{:S(2)}, u32[]{:S(2)}) collective-permute-start(bf16[320,384]{1,0:T(8,128)(2,1)S(1)} %dynamic-slice_bitcast_fusion), channel_id=1, source_target_pairs={{0,2},{2,0},{1,3},{3,1},{4,6},{6,4},{5,7},{7,5},{8,10},{10,8},{9,1... | collective-permute-start | bytes 737288 | tf_op jit(solution)/shard_map/ppermute | solution.py:436
  86.4 19.8 %all-to-all-start.3 = ((bf16[16,8,640]{2,1,0:T(8,128)(2,1)}), bf16[16,8,640]{2,1,0:T(8,128)(2,1)S(1)}, u32[]{:S(2)}, u32[]{:S(2)}) async-start(bf16[16,8,640]{2,1,0:T(8,128)(2,1)} %bitcast.18), calls=%async_computation.3 | async-start | bytes 327680 | tf_op jit(solution)/shard_map/all_to_all | solution.py:440
